TPU v7x, 32 devices: a whole 2x2x4 slice. The times are simulated.
32 devices in a mesh: member: 4 (over y, core), fsdp: 8 (over z, x).
Axes of the slice: x: 2, y: 2, z: 4, core: 2. Of those that a mesh axis runs over, the one named last changes fastest.
Arguments:
- tokens: bfloat16 [1536, 4096], P('fsdp'), may hold values from -6 to 6
- routes: int32 [1536, 2], P('fsdp'), may hold values from 0 to 3, all different within a row; in each aligned block of 192 rows (0 to 191, 192 to 383, ...) at most 144 rows name the same one
- combine: float32 [1536, 2], P('fsdp'), may hold values from 0.25 to 1
- gate_weight: bfloat16 [4, 11008, 4096], P('member', None, 'fsdp'), may hold values from -0.09375 to 0.09375
- up_weight: bfloat16 [4, 11008, 4096], P('member', None, 'fsdp'), may hold values from -0.09375 to 0.09375
- down_weight: bfloat16 [4, 11008, 4096], P('member', None, 'fsdp'), may hold values from -0.0546875 to 0.0546875
Outputs:
- mixed: bfloat16 [1536, 4096], P('fsdp', 'member')
Inputs may be any that keep to these rules, and one draw needn't show every extreme that they name: `routes`: each row names two different experts. In each aligned block of 192 rows no expert is named by more than 144 rows, a bound that some block reaches.
All inputs are finite; a program needn't handle non-finite values.
Results may differ from a plain program's by a relative error of at most 0.0049.
Values may be sent and summed in bfloat16 or wider, within the bound.
No kernel may reach another device: no remote copies, remote signals or barrier semaphores. Data moves between devices by JAX's collectives and lax.ppermute only.
A program may use at most 128 MiB of HBM per device.

v0:
```python
import jax
import jax.numpy as jnp
from jax import lax
from jax.sharding import PartitionSpec as P


def blocked(weight, groups):
    return weight.reshape(groups, weight.shape[1] // groups, weight.shape[2])


def body(tokens, routes, combine, gate_weight, up_weight, down_weight):
    expert = lax.axis_index("member")
    groups = lax.axis_size("fsdp")
    tok_rows = tokens.shape[0]
    capacity = 3 * tok_rows // lax.axis_size("member")
    picked = routes == expert
    chosen = jnp.any(picked, axis=1)
    token_weight = jnp.sum(jnp.where(picked, combine, jnp.zeros_like(combine)), axis=1)
    position = jnp.cumsum(chosen.astype(jnp.int32)) - 1
    slot_ids = jnp.arange(capacity, dtype=jnp.int32)
    placed = (position[:, None] == slot_ids[None, :]) & chosen[:, None]
    packed = lax.dot_general(
        placed.astype(jnp.bfloat16),
        tokens,
        (((0,), (0,)), ((), ())),
        preferred_element_type=jnp.float32,
    ).astype(jnp.bfloat16)
    gate_local, up_local, down_moved = (
        lax.all_to_all(
            blocked(gate_weight, groups), "fsdp", split_axis=0, concat_axis=0, tiled=True
        ),
        lax.all_to_all(blocked(up_weight, groups), "fsdp", split_axis=0, concat_axis=0, tiled=True),
        lax.all_to_all(
            blocked(down_weight, groups), "fsdp", split_axis=0, concat_axis=0, tiled=True
        ),
    )
    feat_part = gate_local.shape[2]
    piece = lax.all_gather(packed, "fsdp", axis=0, tiled=True)
    split_rows = piece.reshape(piece.shape[0], groups, feat_part)
    gate_act = lax.dot_general(
        split_rows, gate_local, (((1, 2), (0, 2)), ((), ())), preferred_element_type=jnp.float32
    )
    up_act = lax.dot_general(
        split_rows, up_local, (((1, 2), (0, 2)), ((), ())), preferred_element_type=jnp.float32
    )
    hidden = (jax.nn.silu(gate_act) * up_act).astype(jnp.bfloat16)
    result = lax.dot_general(
        hidden, down_moved, (((1,), (1,)), ((), ())), preferred_element_type=jnp.float32
    )
    expert_out = lax.psum_scatter(
        result.reshape(capacity * lax.axis_size("fsdp"), groups * feat_part),
        "fsdp",
        scatter_dimension=0,
        tiled=True,
    )
    spread = jnp.where(placed, token_weight[:, None], jnp.zeros_like(token_weight[:, None]))
    weighted = jnp.dot(
        spread, expert_out, precision=lax.Precision.HIGHEST, preferred_element_type=jnp.float32
    )
    mixed = lax.psum_scatter(weighted, "member", scatter_dimension=1, tiled=True)
    return mixed.astype(jnp.bfloat16)


def solution(mesh):
    placed = (
        P("fsdp", None),
        P("fsdp", None),
        P("fsdp", None),
        P("member", None, "fsdp"),
        P("member", None, "fsdp"),
        P("member", None, "fsdp"),
    )
    return jax.shard_map(
        body, mesh=mesh, in_specs=placed, out_specs=P("fsdp", "member"), check_vma=False
    )
```

profile of v0, /device:TPU:4, one launch (start us, length us, event | category | flops | bytes accessed | tf_op | source)
XLA Modules:
  0.0 1273.7 jit_solution(3098609290927753363)
XLA Ops:
  6.5 0.0 copy-start
  6.5 251.6 %all_to_all.15 = bf16[8,1376,512]{2,1,0:T(8,128)(2,1)} all-to-all(bf16[8,1376,512]{2,1,0:T(8,128)(2,1)} %bitcast.44), channel_id=1, replica_groups=mesh['member'=4,'fsdp'=8] {'fsdp'}, dimensions={0} | all-to-all | bytes 22544384 | tf_op jit(solution)/shard_map/all_to_all | solution.py:29
  258.1 0.0 copy-start.2
  258.1 5.4 all-to-all-start.1
  263.5 0.0 all-gather.2.cloned.1.call-start
  263.5 0.0 copy-done.2
  263.6 0.3 reduce-window.9
  263.9 0.1 slice.10
  264.0 0.1 slice_reduce_fusion
  264.1 0.1 add_bitcast_fusion
  264.2 0.0 copy-done
  264.2 1.7 convolution_convert_fusion
  265.9 0.0 all-gather.2.cloned.1.call-update
  265.9 355.4 %all-to-all-done.1 = bf16[8,1376,512]{2,1,0:T(8,128)(2,1)} async-done(((bf16[8,1376,512]{2,1,0:T(8,128)(2,1)}), bf16[8,1376,512]{2,1,0:T(8,128)(2,1)}, u32[]{:S(2)}, u32[]{:S(2)}) %all-to-all-start.1) | async-done | bytes 11272224 | tf_op jit(solution)/shard_map/all_to_all | solution.py:32
  621.2 5.2 all-to-all-start.2
  626.5 0.0 reduce-scatter.7.cloned.1.call-start
  626.5 0.0 all-gather.2.cloned.1.call-done
  626.6 0.0 copy-start.4
  626.6 18.4 %fusion.4 = f32[1152,1376]{0,1:T(8,128)S(1)} fusion(bf16[8,1376,512]{2,1,0:T(8,128)(2,1)} %all_to_all.15, bf16[144,8,8,512]{3,2,1,0:T(8,128)(2,1)} %bitcast.47), kind=kOutput, calls=%fused_computation.4 | convolution fusion | flops 12985565184 | bytes 27049984 | tf_op jit(solution)/shard_map/dot_general | solution.py:40
  645.0 0.0 copy-done.4
  645.0 19.0 %fusion.18 = bf16[1152,1376,1]{0,1,2:T(8,128)(2,1)} fusion(bf16[8,1376,512]{2,1,0:T(8,128)(2,1)} %all-to-all-done.1, bf16[144,8,8,512]{3,2,1,0:T(8,128)(2,1)S(1)} %bitcast.48, f32[1152,1376]{0,1:T(8,128)S(1)} %fusion.4), kind=kOutput, calls=%fused_computation.10 | convolution fusion | flops 12995076096 | bytes 30220288 | tf_op jit(solution)/shard_map/dot_general | solution.py:43
  664.0 205.9 %all-to-all-done.2 = bf16[8,1376,512]{2,1,0:T(8,128)(2,1)} async-done(((bf16[8,1376,512]{2,1,0:T(8,128)(2,1)}), bf16[8,1376,512]{2,1,0:T(8,128)(2,1)}, u32[]{:S(2)}, u32[]{:S(2)}) %all-to-all-start.2) | async-done | bytes 11272224 | tf_op jit(solution)/shard_map/all_to_all | solution.py:33
  869.9 21.9 %fusion.35 = f32[1152,8,512]{0,2,1:T(8,128)} fusion(bf16[1152,1376,1]{0,1,2:T(8,128)(2,1)} %fusion.18, bf16[8,1376,512]{2,1,0:T(8,128)(2,1)} %all-to-all-done.2), kind=kOutput, calls=%fused_computation.31 | convolution fusion | flops 12985565184 | bytes 33316864 | tf_op jit(solution)/shard_map/dot_general | solution.py:47
  891.8 18.7 %copy.11 = f32[1152,4096]{1,0:T(8,128)} copy(f32[1152,4096]{0,1:T(8,128)} %bitcast.43) | data formatting | bytes 37748736
  910.6 0.0 copy-start.3
  910.6 0.0 reduce-scatter.7.cloned.1.call-update
  910.6 0.0 copy-start.1
  910.6 0.2 reduce-scatter.5.cloned.1.call-start
  910.8 0.4 copy-done.3
  911.3 311.8 %reduce-scatter.7.cloned.1.call-done = f32[144,4096]{1,0:T(8,128)} async-done(((f32[1152,4096]{1,0:T(8,128)}), f32[144,4096]{1,0:T(8,128)}) %reduce-scatter.7.cloned.1.call-update) | async-done | bytes 2359312
  1223.1 6.0 fusion.21
  1229.1 0.0 reduce-scatter.5.cloned.1.call-update
  1229.1 36.1 %reduce-scatter.5.cloned.1.call-done = f32[192,1024]{1,0:T(8,128)} async-done(((f32[192,4096]{1,0:T(8,128)}), f32[192,1024]{1,0:T(8,128)}) %reduce-scatter.5.cloned.1.call-update) | async-done | bytes 786448 | tf_op jit(solution)/shard_map/reduce_scatter | solution.py:60
  1265.2 1.9 convert_element_type.13
  1267.2 0.0 copy-done.1
  (5 shorter events, 0.1 us)
Async XLA Ops:
  6.5 257.6 %copy-start = (bf16[192,4096]{1,0:T(8,128)(2,1)S(1)}, bf16[192,4096]{1,0:T(8,128)(2,1)}, u32[]{:S(2)}) copy-start(bf16[192,4096]{1,0:T(8,128)(2,1)} %param.6) | copy-start | bytes 4718596
  258.1 5.4 copy-start.2
  258.1 363.1 %all-to-all-start.1 = ((bf16[8,1376,512]{2,1,0:T(8,128)(2,1)}), bf16[8,1376,512]{2,1,0:T(8,128)(2,1)}, u32[]{:S(2)}, u32[]{:S(2)}) async-start(bf16[8,1376,512]{2,1,0:T(8,128)(2,1)} %bitcast.45), calls=%async_computation.1 | async-start | bytes 22544384 | tf_op jit(solution)/shard_map/all_to_all | solution.py:32
  263.5 363.1 %all-gather.2.cloned.1.call-start = ((), (), s32[]{:S(2)}) async-start(), calls=%async_computation.5 | async-start | bytes 10616832 | tf_op jit(solution)/shard_map/all_gather | solution.py:38
  621.2 248.7 %all-to-all-start.2 = ((bf16[8,1376,512]{2,1,0:T(8,128)(2,1)}), bf16[8,1376,512]{2,1,0:T(8,128)(2,1)}, u32[]{:S(2)}, u32[]{:S(2)}) async-start(bf16[8,1376,512]{2,1,0:T(8,128)(2,1)} %bitcast.46), calls=%async_computation.2 | async-start | bytes 22544384 | tf_op jit(solution)/shard_map/all_to_all | solution.py:33
  626.5 596.6 %reduce-scatter.7.cloned.1.call-start = ((), (), s32[]{:S(2)}) async-start(), calls=%async_computation.7 | async-start | bytes 21233664
  626.6 18.4 %copy-start.4 = (bf16[1152,4096]{1,0:T(8,128)(2,1)S(1)}, bf16[1152,4096]{1,0:T(8,128)(2,1)}, u32[]{:S(2)}) copy-start(bf16[1152,4096]{1,0:T(8,128)(2,1)} %all-gather.2.cloned.1.call-done) | copy-start | bytes 28311556
  910.6 0.7 copy-start.3
  910.6 356.6 %copy-start.1 = (bf16[192,4096]{1,0:T(8,128)(2,1)S(1)}, bf16[192,4096]{1,0:T(8,128)(2,1)}, u32[]{:S(2)}) copy-start(bf16[192,4096]{1,0:T(8,128)(2,1)} %param.6) | copy-start | bytes 4718596
  910.6 354.6 %reduce-scatter.5.cloned.1.call-start = ((), (), s32[]{:S(2)}) async-start(), calls=%async_computation.6 | async-start | bytes 3932160 | tf_op jit(solution)/shard_map/reduce_scatter | solution.py:60
Sparse Core Ops, SparseCore 0:
  266.5 333.7 all-gather.1
  910.7 312.3 reduce-scatter.6
  1229.3 35.9 reduce-scatter.4
where the time goes:
time: 1280 us; the launch traced here: 1270 us
  waiting for transfers between devices  909 us (71%)
  blocking collectives  252 us (20%)
  matrix products  67.1 us (5%)
  local copies, waits for them, and re-layouts  19.3 us (2%)
  between operations  13.2 us (1%)
    all_to_all x1, waiting for transfers between devices, body(): lax.all_to_all(blocked(up_weight, groups), 'fsdp', split_axis=0, concat_a...  355 us
    unnamed x4, waiting for transfers between devices  312 us
    all_to_all x1, blocking collectives, body(): lax.all_to_all(blocked(gate_weight, groups), 'fsdp', split_axis=0, concat...  252 us
    all_to_all x1, waiting for transfers between devices, body(): lax.all_to_all(blocked(down_weight, groups), 'fsdp', split_axis=0, concat...  206 us
    reduce_scatter x1, waiting for transfers between devices, body(): lax.psum_scatter(weighted, 'member', scatter_dimension=1, tiled=True)  36.1 us
  transfers between devices with their start and end apart: 5, of which 4 were waited for; matrix products, arithmetic and copies ran while one was open for 3% of the time, Pallas kernels for 0%

commit v1 on v0

v1 whole, which is shorter than its diff:
```python
import functools

import jax
import jax.numpy as jnp
from jax import lax
from jax.experimental import pallas as pl
from jax.experimental.pallas import tpu as pltpu
from jax.sharding import PartitionSpec as P

WIDTH = 256
HOP = 2
AHEAD = 3
BATCH = 2
VMEM = 58 * 1024 * 1024


def grid_of(size):
    across = 1
    while across * across * 4 <= size:
        across *= 2
    return size // across, across


def begin(src, dst, sem):
    copy = pltpu.make_async_copy(src, dst, sem)
    copy.start()
    return copy


def taker(refs):
    refs = list(refs)

    def take(count=1):
        out = refs[:count]
        del refs[:count]
        return out

    return take


def rows_at(ref, start, width):
    return ref.at[pl.ds(pl.multiple_of(start, 16), width)]


def chain_kernel(cfg, *refs):
    deep, across, width, sums, sums_in, back, back_in = cfg
    take = taker(refs)
    (info,) = take()
    if sums:
        gate, up, toks = take(3)
        got = [take(across - 1) for _ in range(deep)]
    came = take(2) if sums_in or back_in else None
    sent = take(2)
    (hid_out,) = take() if back else (None,)
    if sums:
        toks_v, w_v, tok_sem, w_sem = take(4)
    if came:
        came_v, came_sem = take(2)
    sent_v, sent_sem = take(2)
    if back:
        hid_v, hid_sem = take(2)
    place = info[0]
    odd = lax.rem(place, 2)
    wide = 2 * width if sums else 0
    in_wide = came[0].shape[1] - (width if back_in else 0) if came else 0
    half = sent[0].shape[0]
    copies = []

    waits = [[], []]
    for s in range(2):
        if came:
            for slot in range(2):

                @pl.when(lax.rem(odd + s, 2) == 1 - slot)
                def _(src=came[slot], s=s):
                    pltpu.make_async_copy(src, came_v.at[s], came_sem.at[s]).start()

            waits[s].append(pltpu.make_async_copy(came[0], came_v.at[s], came_sem.at[s]))
    if sums:
        part_rows = gate.shape[0] // across
        tok_copies = [
            begin(
                toks.at[:, pl.ds(s * half, half)],
                toks_v.at[:, pl.ds(s * half, half)],
                tok_sem.at[s],
            )
            for s in (1, 0)
        ][::-1]
        for s in range(2):
            own = info[1] * part_rows + info[2 + s]
            for k, ref in enumerate((gate, up)):
                waits[s].append(
                    begin(
                        rows_at(ref, own, width),
                        w_v.at[s, 0, pl.ds(k * width, width)],
                        w_sem.at[s, 0, k],
                    )
                )
            for j in range(1, across):
                dst, sem = w_v.at[s, j], w_sem.at[s, j, 0]
                for i in range(deep):
                    here = i if s == 0 else deep - 1 - i

                    @pl.when(place == here)
                    def _(src=got[i][j - 1], dst=dst, sem=sem):
                        pltpu.make_async_copy(src.at[pl.ds(0, 2 * width)], dst, sem).start()

                waits[s].append(
                    pltpu.make_async_copy(got[0][j - 1].at[pl.ds(0, 2 * width)], dst, sem)
                )

    ends = []
    for s in range(2):
        for copy in waits[s]:
            copy.wait()
        if not sums:
            continue
        mine = 1 - s
        tok_copies[mine].wait()
        total = None
        for j in range(across):
            term = lax.dot_general(
                toks_v[j, pl.ds(mine * half, half), :],
                w_v[s, j],
                (((1,), (1,)), ((), ())),
                preferred_element_type=jnp.float32,
            )
            total = term if total is None else total + term
        if sums_in:
            first = place == (0 if s == 0 else deep - 1)
            before = came_v[s, :, : 2 * width].astype(jnp.float32)
            total = total + jnp.where(first, 0.0, before)
        sent_v[s, :, : 2 * width] = total.astype(jnp.bfloat16)
        if back:
            value, upper = total[:, :width], total[:, width:]
            hidden = value / (1.0 + jnp.exp(-value)) * upper
            column = lax.broadcasted_iota(jnp.int32, hidden.shape, 1)
            ends.append(jnp.where(column >= info[4], hidden, 0.0).astype(jnp.bfloat16))
    if back:
        for s in range(2):
            value = came_v[s, :, in_wide:] if back_in else None
            if sums:
                at_end = place == (0 if s == 0 else deep - 1)
                other = value if back_in else jnp.zeros_like(ends[1 - s])
                value = jnp.where(at_end, ends[1 - s], other)
            sent_v[s, :, wide:] = value
            hid_v[pl.ds(s * half, half)] = value
    for s in range(2):
        for slot in range(2):

            @pl.when(lax.rem(odd + s, 2) == slot)
            def _(dst=sent[slot], s=s):
                pltpu.make_async_copy(sent_v.at[s], dst, sent_sem.at[s]).start()

        copies.append(pltpu.make_async_copy(sent_v.at[s], sent[0], sent_sem.at[s]))
    if back:
        copies.append(begin(hid_v, hid_out, hid_sem))
    for copy in copies:
        copy.wait()


def side_kernel(cfg, *refs):
    deep, across, width, steps, n_send = cfg
    take = taker(refs)
    (info,) = take()
    gate, up, down = take(3)
    hids = take(steps)
    got = [[take(across - 1) for _ in range(deep)] for _ in range(steps)]
    acc_in = take() if steps else None
    sent = take(n_send)
    acc_out = take() if steps else None
    if n_send:
        send_v, send_sem, sendo_sem = take(3)
    if steps:
        hid_v, d_v, acc_v, hid_sem, d_sem, acc_sem, acco_sem = take(7)
    place = info[0]
    part_rows = gate.shape[0] // across
    waits, copies, sends = [], [], []
    if steps:
        acc_in, acc_out = acc_in[0], acc_out[0]
        half = acc_in.shape[0] // 2
        for n in range(steps):
            waits.append(begin(hids[n], hid_v.at[n], hid_sem.at[n]))
            for s in range(2):
                own = info[1] * part_rows + info[2 + 4 * n + s]
                waits.append(
                    begin(rows_at(down, own, width), d_v.at[n, s, 0], d_sem.at[n, s, 0])
                )
                for j in range(1, across):
                    dst, sem = d_v.at[n, s, j], d_sem.at[n, s, j]
                    for i in range(deep):
                        here = i if s == 0 else deep - 1 - i

                        @pl.when(place == here)
                        def _(src=got[n][i][j - 1], dst=dst, sem=sem):
                            pltpu.make_async_copy(
                                src.at[pl.ds(2 * width, width)], dst, sem
                            ).start()

                    waits.append(
                        pltpu.make_async_copy(
                            got[n][0][j - 1].at[pl.ds(2 * width, width)], dst, sem
                        )
                    )
        tile = half // 2
        acc_copies = [
            begin(
                acc_in.at[pl.ds(i * tile, tile)],
                acc_v.at[pl.ds(i * tile, tile)],
                acc_sem.at[i],
            )
            for i in range(4)
        ]
    base = 2 + 4 * steps
    for j in range(n_send):
        for k, ref in enumerate((gate, up, down)):
            sends.append(
                begin(
                    rows_at(ref, info[base + j], width),
                    send_v.at[j, pl.ds(k * width, width)],
                    send_sem.at[j, k],
                )
            )
    for copy in sends:
        copy.wait()
    for j in range(n_send):
        copies.append(begin(send_v.at[j], sent[j], sendo_sem.at[j]))
    if steps:
        for copy in waits:
            copy.wait()
        feat = d_v.shape[-1]
        for i in range(4):
            s = i // 2
            here = pl.ds(i * tile, tile)
            acc_copies[i].wait()
            for j in range(across):
                total = acc_v[here, pl.ds(j * feat, feat)]
                for n in range(steps):
                    hidden = hid_v[n, here, :]
                    valid = info[4 + 4 * n + s] > 0
                    hidden = jnp.where(valid, hidden, jnp.zeros_like(hidden))
                    total += lax.dot_general(
                        hidden,
                        d_v[n, s, j],
                        (((1,), (0,)), ((), ())),
                        preferred_element_type=jnp.float32,
                    )
                acc_v[here, pl.ds(j * feat, feat)] = total
            copies.append(begin(acc_v.at[here], acc_out.at[here], acco_sem.at[i]))
    for copy in copies:
        copy.wait()


def call(kernel, args, outs, scratch, aliases, flops, nbytes, name):
    return list(
        pl.pallas_call(
            kernel,
            out_shape=outs,
            in_specs=[pl.BlockSpec(memory_space=pltpu.SMEM)]
            + [pl.BlockSpec(memory_space=pl.ANY)] * (len(args) - 1),
            out_specs=[pl.BlockSpec(memory_space=pl.ANY)] * len(outs),
            scratch_shapes=scratch,
            input_output_aliases=aliases,
            compiler_params=pltpu.CompilerParams(vmem_limit_bytes=VMEM),
            cost_estimate=pl.CostEstimate(
                flops=flops, bytes_accessed=nbytes, transcendentals=0
            ),
            name=name,
        )(*args)
    )


def body(tokens, routes, combine, gate_weight, up_weight, down_weight):
    hop, width, ahead, batch = HOP, WIDTH, AHEAD, BATCH
    expert = lax.axis_index("member")
    members = lax.axis_size("member")
    groups = lax.axis_size("fsdp")
    me = lax.axis_index("fsdp")
    deep, across = grid_of(groups)
    z, x = me // across, lax.rem(me, across)
    tok_rows = tokens.shape[0]
    capacity = 3 * tok_rows // members
    gate_weight, up_weight, down_weight = gate_weight[0], up_weight[0], down_weight[0]
    hidden_all, feat = gate_weight.shape
    part_rows = hidden_all // across
    n_chunks = -(-part_rows // width)
    total_rows = capacity * groups
    half_rows = total_rows // 2
    bf, f32 = jnp.bfloat16, jnp.float32
    dma = pltpu.SemaphoreType.DMA

    def swap(array, dz, dx):
        perm = [
            (a * across + b, (a ^ dz) * across + (b ^ dx))
            for a in range(deep)
            for b in range(across)
        ]
        return lax.ppermute(array, "fsdp", perm)

    def pairing(array, slot):
        perm = []
        for m in range(members):
            for a in range(deep):
                b = a ^ 1 if slot == 0 else ((a + 1) ^ 1) - 1
                for c in range(across):
                    there = (m, b) if 0 <= b < deep else (m ^ 1, a)
                    perm.append(
                        (m * groups + a * across + c, there[0] * groups + there[1] * across + c)
                    )
        return lax.ppermute(array, ("member", "fsdp"), perm)

    def start_of(chunk):
        return jnp.minimum(jnp.clip(chunk, 0, n_chunks - 1) * width, part_rows - width)

    got = {}

    def hand_over(k, arrays):
        got[k] = [swap(a, 0, j + 1) for j, a in enumerate(arrays)]

    def send_start(k, j):
        return (x ^ j) * part_rows + min(k * width, part_rows - width)

    def hand_over_early(k, weights):
        hand_over(
            k,
            [
                jnp.concatenate(
                    [lax.dynamic_slice_in_dim(w, send_start(k, j), width, 0) for w in weights]
                )
                for j in range(1, across)
            ],
        )

    weights = (gate_weight, up_weight, down_weight)
    early = min(ahead, n_chunks)
    for k in range(min(2, early)):
        hand_over_early(k, weights)

    picked = routes == expert
    chosen = jnp.any(picked, axis=1)
    token_weight = jnp.sum(jnp.where(picked, combine, jnp.zeros_like(combine)), axis=1)
    position = jnp.cumsum(chosen.astype(jnp.int32)) - 1
    slot_ids = jnp.arange(capacity, dtype=jnp.int32)
    placed = (position[:, None] == slot_ids[None, :]) & chosen[:, None]
    packed = lax.dot_general(
        placed.astype(bf), tokens, (((0,), (0,)), ((), ())), preferred_element_type=f32
    ).astype(bf)
    token_ids = jnp.arange(tok_rows, dtype=jnp.int32)
    came_from = jnp.sum(jnp.where(placed, token_ids[:, None] + 1, 0), axis=0)
    weight = jnp.sum(jnp.where(placed, token_weight[:, None], 0.0), axis=0)
    high = lax.reduce_precision(weight, 8, 7)
    middle = lax.reduce_precision(weight - high, 8, 7)
    low = weight - high - middle
    notes = jnp.stack(
        [(came_from // 128).astype(f32), (came_from % 128).astype(f32), high, middle, low], axis=1
    ).astype(bf)
    notes = jnp.pad(notes, ((0, 0), (0, 128 - notes.shape[1])))

    def pick(array, index):
        return lax.dynamic_index_in_dim(array, index, 0, keepdims=False)

    def columns(array, index, size):
        return lax.dynamic_slice_in_dim(array, index * size, size, 1)

    pieces = []
    for k in range(deep):
        piece = jnp.concatenate([columns(packed, z ^ k, across * feat), notes], axis=1)
        pieces.append(swap(piece, k, 0) if k else piece)
    pieces = jnp.stack(pieces)
    mine = jnp.concatenate([pick(pieces, z ^ a) for a in range(deep)])
    mine, got[0] = lax.optimization_barrier((mine, got[0]))
    by_group = [swap(mine, 0, i) if i else mine for i in range(across)]
    by_group, weights = lax.optimization_barrier((by_group, weights))
    for k in range(2, early):
        hand_over_early(k, weights)
    toks = jnp.stack(
        [jnp.concatenate([columns(g, x ^ j, feat) for g in by_group]) for j in range(across)]
    )
    notes = jnp.concatenate([g[:, across * feat :] for g in by_group])[:, :5].astype(f32)
    notes = notes.T.reshape(5, across * deep, capacity)
    came_from = (notes[0] * 128.0 + notes[1]).astype(jnp.int32) - 1
    weight = notes[2] + notes[3] + notes[4]

    reach = hop * (deep - 1)
    n_steps = n_chunks + 2 * reach
    acc = jnp.zeros((total_rows, across * feat), f32)
    msgs, waiting, order = {}, [], None
    early_at = reach + n_chunks - 1 + hop * (deep // 2 - 1)
    early_half = jnp.where(z < deep // 2, 0, 1)

    def own_parts(which):
        rows = lax.dynamic_slice_in_dim(acc, which * half_rows, half_rows, 0)
        return [
            swap(rows[:, j * feat : (j + 1) * feat].astype(bf), 0, j) for j in range(1, across)
        ]

    last_skip = n_chunks * width - part_rows

    def candidates(base):
        return [a for i in range(deep) for a in got[min(max(base - hop * i, 0), n_chunks - 1)]]

    for t in range(n_steps):
        sums = t < n_chunks + reach
        back = t >= reach
        before = t - hop
        sums_in = sums and before >= 0
        back_in = back and before >= reach
        cfg = (deep, across, width, sums, sums_in, back, back_in)
        skip = last_skip if t - reach == n_chunks - 1 else 0
        up_c, dn_c = t - hop * z, t - hop * (deep - 1 - z)
        info = jnp.stack([z, x, start_of(up_c), start_of(dn_c), jnp.int32(skip)]).astype(
            jnp.int32
        )
        if order is not None:
            info, order = lax.optimization_barrier((info, order))
            if "acc" in order:
                acc = order["acc"]
            if "sent" in order:
                hand_over(t - 1 + early, order["sent"])
            order = None
        if t == early_at + 3:
            info, early_parts = lax.optimization_barrier((info, early_parts))
        args, outs, scratch = [info], [], []
        if sums:
            args += [gate_weight, up_weight, toks] + candidates(t)
            scratch += [
                pltpu.VMEM((across, total_rows, feat), bf),
                pltpu.VMEM((2, across, 2 * width, feat), bf),
                dma((2,)),
                dma((2, across, 2)),
            ]
        if sums_in or back_in:
            args += list(msgs[before])
            scratch += [pltpu.VMEM((2,) + msgs[before][0].shape, bf), dma((2,))]
        out_width = 2 * width * sums + width * back
        outs += [jax.ShapeDtypeStruct((half_rows, out_width), bf)] * 2
        scratch += [pltpu.VMEM((2, half_rows, out_width), bf), dma((2,))]
        if back:
            outs += [jax.ShapeDtypeStruct((total_rows, width), bf)]
            scratch += [pltpu.VMEM((total_rows, width), bf), dma]
        res = call(
            functools.partial(chain_kernel, cfg),
            args,
            outs,
            scratch,
            {},
            4 * total_rows * width * across * feat * sums,
            8 * 1024 * 1024,
            "chain_step",
        )
        if back:
            waiting.append((t, res[2]))

        next_k = t + early
        n_send = across - 1 if next_k < n_chunks else 0
        flush = len(waiting) == batch or t in (early_at, n_steps - 1)
        steps = len(waiting) if flush else 0
        if not steps and not n_send:
            if t + hop < n_steps:
                msgs[t] = (pairing(res[0], 0), pairing(res[1], 1))
            continue
        done, entries = [], [z, x]
        if steps:
            done, waiting = waiting, []
        for at, _ in done:
            up_c, dn_c = at - reach - hop * z, at - reach - hop * (deep - 1 - z)
            entries += [start_of(up_c), start_of(dn_c)]
            entries += [((c >= 0) & (c < n_chunks)).astype(jnp.int32) for c in (up_c, dn_c)]
        entries += [send_start(next_k, j + 1) for j in range(n_send)]
        side_info = jnp.stack([jnp.int32(e) for e in entries]).astype(jnp.int32)
        side_info, res = lax.optimization_barrier((side_info, res))
        if t + hop < n_steps:
            msgs[t] = (pairing(res[0], 0), pairing(res[1], 1))
        args = [side_info]
        args += [gate_weight, up_weight, down_weight] + [hid for _, hid in done]
        for at, _ in done:
            args += candidates(at - reach)
        aliases, outs, scratch = {}, [], []
        outs += [jax.ShapeDtypeStruct((3 * width, feat), bf)] * n_send
        if n_send:
            scratch += [
                pltpu.VMEM((n_send, 3 * width, feat), bf),
                dma((n_send, 3)),
                dma((n_send,)),
            ]
        if steps:
            aliases = {len(args): n_send}
            args += [acc]
            outs += [jax.ShapeDtypeStruct(acc.shape, f32)]
            scratch += [
                pltpu.VMEM((steps, total_rows, width), bf),
                pltpu.VMEM((steps, 2, across, width, feat), bf),
                pltpu.VMEM(acc.shape, f32),
                dma((steps,)),
                dma((steps, 2, across)),
                dma((4,)),
                dma((4,)),
            ]
        res = call(
            functools.partial(side_kernel, (deep, across, width, steps, n_send)),
            args,
            outs,
            scratch,
            aliases,
            2 * total_rows * width * across * feat * steps,
            (12 if steps else 2) * 1024 * 1024,
            "side_step",
        )
        order = {}
        if steps:
            order["acc"] = acc = res.pop()
        if n_send:
            order["sent"] = res
        if t == early_at:
            early_parts = own_parts(early_half)

    late_parts = own_parts(1 - early_half)
    group_rows = total_rows // across
    whole = acc[:, :feat]
    for j in range(1, across):
        first, second = early_parts[j - 1], late_parts[j - 1]
        part = jnp.concatenate(
            [
                jnp.where(early_half == 0, first, second),
                jnp.where(early_half == 0, second, first),
            ]
        )
        part = jnp.concatenate(
            [part[(i ^ j) * group_rows : ((i ^ j) + 1) * group_rows] for i in range(across)]
        )
        whole = whole + part.astype(f32)
    whole = whole.reshape(across * deep, capacity, feat)
    spread = jnp.where(
        came_from[:, None, :] == token_ids[None, :, None], weight[:, None, :], 0.0
    )
    weighted = lax.dot_general(
        spread,
        whole,
        (((2,), (1,)), ((0,), (0,))),
        precision=lax.Precision.HIGHEST,
        preferred_element_type=f32,
    ).reshape(across, deep, tok_rows, feat)
    weighted = jnp.stack([pick(weighted, x ^ b) for b in range(across)], axis=1)
    share = groups // members
    left = weighted.reshape(members, share * tok_rows, feat)
    bit = 1
    while bit < members:
        pairs = left.reshape(left.shape[0] // 2, 2, share * tok_rows, feat)
        side = (expert // bit) % 2
        keep, give = (
            lax.dynamic_index_in_dim(pairs, s, 1, keepdims=False) for s in (side, 1 - side)
        )
        give = give if bit == 1 else give.astype(bf)
        came = lax.ppermute(give, "member", [(m, m ^ bit) for m in range(members)])
        left = keep + came.astype(f32)
        bit *= 2
    mixed = left.astype(bf).reshape(share, tok_rows, feat)
    slot = lax.rem(me, share)
    parts = []
    for j in range(share):
        perm = []
        for r in range(members):
            for f in range(groups):
                block = r * share + ((f % share) ^ j)
                perm.append((r * groups + f, (f // share) * groups + block))
        parts.append(lax.ppermute(pick(mixed, slot ^ j), ("member", "fsdp"), perm))
    parts = jnp.stack(parts)
    return jnp.concatenate([pick(parts, slot ^ c) for c in range(share)], axis=1)


def solution(mesh):
    placed = (
        P("fsdp", None),
        P("fsdp", None),
        P("fsdp", None),
        P("member", None, "fsdp"),
        P("member", None, "fsdp"),
        P("member", None, "fsdp"),
    )
    return jax.shard_map(
        body, mesh=mesh, in_specs=placed, out_specs=P("fsdp", "member"), check_vma=False
    )
```

time: 1280 us -> 738 us (0.58)
  waiting for transfers between devices: 909 us -> 209 us
  Pallas kernels: 0 us -> 327 us
  blocking collectives: 252 us -> 0 us
  starting transfers between devices: 10.9 us -> 97.4 us
  matrix products: 67.1 us -> 4.42 us
  local copies, waits for them, and re-layouts: 19.3 us -> 70.5 us
  other arithmetic: 2.41 us -> 16.8 us
    all_to_all x2 -> x0, waiting for transfers between devices: 561 us -> none  [the longest x1 355 us: body(): lax.all_to_all(blocked(up_weight, groups), 'fsdp', split_axis=0, concat_a...]
    pallas_call x0 -> x61, Pallas kernels: none -> 327 us  [call(): pl.pallas_call(kernel, out_shape=outs, in_specs=[pl.BlockSpec(memory_spac...]
    unnamed x4 -> x0, waiting for transfers between devices: 312 us -> none
    all_to_all x1 -> x0, blocking collectives: 252 us -> none  [body(): lax.all_to_all(blocked(gate_weight, groups), 'fsdp', split_axis=0, concat...]
    ppermute x0 -> x96, waiting for transfers between devices: none -> 209 us  [the longest x64 94.4 us: pairing(): return lax.ppermute(array, ('member', 'fsdp'), perm)]
    ppermute x0 -> x96, starting transfers between devices: none -> 97.4 us  [the longest x64 61.9 us: pairing(): return lax.ppermute(array, ('member', 'fsdp'), perm)]
    dot_general x5 -> x2, matrix products: 67.1 us -> 4.42 us  [the longest x1 3.95 us: body(): lax.dot_general(spread, whole, (((2,), (1,)), ((0,), (0,))), precision=la...]
    reduce_scatter x1 -> x0, waiting for transfers between devices: 36.1 us -> none  [body(): lax.psum_scatter(weighted, 'member', scatter_dimension=1, tiled=True)]
  transfers between devices with their start and end apart: 5 -> 96, of which waited for: 4 -> 35; matrix products, arithmetic and copies ran while one was open for 3% -> 7% of each run, Pallas kernels for 0% -> 44%
where the time goes in v1:
time: 738 us; the launch traced here: 727 us
  Pallas kernels  327 us (44%)
  waiting for transfers between devices  209 us (28%)
  starting transfers between devices  97.4 us (13%)
  local copies, waits for them, and re-layouts  70.5 us (10%)
  other arithmetic  16.8 us (2%)
    pallas_call x61, Pallas kernels, call(): pl.pallas_call(kernel, out_shape=outs, in_specs=[pl.BlockSpec(memory_spac...  327 us
    ppermute x64, waiting for transfers between devices, pairing(): return lax.ppermute(array, ('member', 'fsdp'), perm)  94.4 us
    ppermute x28, waiting for transfers between devices, swap(): return lax.ppermute(array, 'fsdp', perm)  85.2 us
    ppermute x64, starting transfers between devices, pairing(): return lax.ppermute(array, ('member', 'fsdp'), perm)  61.9 us
    ppermute x28, starting transfers between devices, swap(): return lax.ppermute(array, 'fsdp', perm)  27.9 us
    unnamed x108, local copies, waits for them, and re-layouts  23.4 us
    another operation x34, local copies, waits for them, and re-layouts, body(): jnp.stack([z, x, start_of(up_c), start_of(dn_c), jnp.int32(skip)])  22.2 us
    ppermute x2, waiting for transfers between devices, body(): parts.append(lax.ppermute(pick(mixed, slot ^ j), ('member', 'fsdp'), perm))  15.5 us
  transfers between devices with their start and end apart: 96, of which 35 were waited for; matrix products, arithmetic and copies ran while one was open for 7% of the time, Pallas kernels for 44%

profile of v1, /device:TPU:4, one launch (start us, length us, event | category | flops | bytes accessed | tf_op | source)
XLA Modules:
  0.0 727.5 jit_solution(429147609403182323)
XLA Ops:
  13.3 6.0 collective-permute-done
  19.3 11.7 %collective-permute-done.1 = bf16[144,1152]{1,0:T(8,128)(2,1)} collective-permute-done((bf16[144,1152]{1,0:T(8,128)(2,1)S(1)}, bf16[144,1152]{1,0:T(8,128)(2,1)}, u32[]{:S(2)}, u32[]{:S(2)}) %collective-permute-start.1) | collective-permute-done | bytes 331808 | tf_op jit(solution)/shard_map/ppermute | solution.py:298
  37.0 27.8 %collective-permute-done.4 = bf16[576,1152]{1,0:T(8,128)(2,1)} collective-permute-done((bf16[576,1152]{1,0:T(8,128)(2,1)S(1)}, bf16[576,1152]{1,0:T(8,128)(2,1)}, u32[]{:S(2)}, u32[]{:S(2)}) %collective-permute-start.4) | collective-permute-done | bytes 1327136 | tf_op jit(solution)/shard_map/ppermute | solution.py:298
  68.1 5.2 chain_step.34
  73.3 6.4 collective-permute-start.7
  90.5 5.2 chain_step.35
  104.9 5.5 chain_step.36
  121.8 5.6 chain_step.37
  129.2 8.6 %collective-permute-done.12.refs_4_.refs_5_.refs_6_.refs_7_.refs_8_.refs_9_ = bf16[768,512]{1,0:T(8,128)(2,1)S(1)} collective-permute-done((bf16[768,512]{1,0:T(8,128)(2,1)}, bf16[768,512]{1,0:T(8,128)(2,1)S(1)}, u32[]{:S(2)}, u32[]{:S(2)}) %collective-permute-start.12) | collective-permute-done | bytes 786464 | tf_op jit(solution)/shard_map/ppermute | solution.py:298
  142.8 5.5 chain_step.38
  155.5 5.6 chain_step.39
  164.3 7.1 collective-permute-done.18.refs_4_.refs_5_.refs_6_.refs_7_.refs_8_.refs_9_
  176.5 6.6 chain_step.40
  191.1 6.3 chain_step.41
  199.3 5.9 collective-permute-done.24.refs_4_.refs_5_.refs_6_.refs_7_.refs_8_.refs_9_
  208.7 7.3 %side_step.34 = (bf16[768,512]{1,0:T(8,128)(2,1)}, f32[1152,1024]{1,0:T(8,128)}) custom-call(s32[11]{0:T(128)} %stack.1209.refs_0_, bf16[11008,512]{1,0:T(8,128)(2,1)} %bitcast.225, bf16[11008,512]{1,0:T(8,128)(2,1)} %bitcast.281, bf16[11008,512]{1,0:T(8,128)(2,1)} %bitcast.329, ...), custom_call_target="tpu_custom_call", output_to_operand_aliasing={{1}: (14, {})} | custom-call | flops 1207959552 | bytes 12582912 | tf_op jit(solution)/shard_map/side_step/pallas_call | solution.py:256
  217.9 6.5 chain_step.42
  230.8 6.5 chain_step.43
  240.0 7.3 side_step.36
  248.9 6.6 chain_step.44
  261.0 5.2 collective-permute-done.34.refs_8_
  267.1 6.6 chain_step.45
  276.2 7.3 side_step.38
  285.4 6.6 chain_step.46
  297.5 6.7 collective-permute-done.40.refs_8_
  305.6 6.6 chain_step.47
  313.9 7.3 side_step.40
  324.0 6.5 chain_step.48
  336.6 5.4 collective-permute-done.46.refs_8_
  342.1 6.5 chain_step.49
  351.4 7.5 %side_step.42 = (bf16[768,512]{1,0:T(8,128)(2,1)}, f32[1152,1024]{1,0:T(8,128)}) custom-call(s32[11]{0:T(128)} %stack.1129.refs_0_, bf16[11008,512]{1,0:T(8,128)(2,1)} %bitcast.241, bf16[11008,512]{1,0:T(8,128)(2,1)} %bitcast.297, bf16[11008,512]{1,0:T(8,128)(2,1)} %bitcast.337, ...), custom_call_target="tpu_custom_call", output_to_operand_aliasing={{1}: (14, {})} | custom-call | flops 1207959552 | bytes 12582912 | tf_op jit(solution)/shard_map/side_step/pallas_call | solution.py:256
  361.3 6.5 chain_step.50
  374.5 5.4 collective-permute-done.52.refs_8_
  380.0 6.5 chain_step.51
  389.3 7.3 side_step.44
  400.3 6.6 chain_step.52
  411.3 6.6 collective-permute-done.59.refs_8_
  417.9 6.5 chain_step.53
  428.5 6.6 side_step.46.refs_14_
  437.7 6.9 chain_step.61
  446.4 9.4 %collective-permute-done.61.refs_8_ = bf16[576,768]{1,0:T(8,128)(2,1)} collective-permute-done((bf16[576,768]{1,0:T(8,128)(2,1)}, bf16[576,768]{1,0:T(8,128)(2,1)}, u32[]{:S(2)}, u32[]{:S(2)}) %collective-permute-start.61) | collective-permute-done | bytes 884768 | tf_op jit(solution)/shard_map/ppermute | solution.py:310
  455.8 6.5 chain_step.54
  466.0 6.6 side_step.47.refs_14_
  476.6 6.5 chain_step.62
  484.6 9.2 %collective-permute-done.63.refs_8_ = bf16[576,768]{1,0:T(8,128)(2,1)} collective-permute-done((bf16[576,768]{1,0:T(8,128)(2,1)}, bf16[576,768]{1,0:T(8,128)(2,1)}, u32[]{:S(2)}, u32[]{:S(2)}) %collective-permute-start.63) | collective-permute-done | bytes 884768 | tf_op jit(solution)/shard_map/ppermute | solution.py:310
  493.7 6.5 chain_step.55
  503.9 6.7 side_step.48.refs_14_
  514.5 6.5 chain_step.63
  522.5 9.1 %collective-permute-done.65.refs_8_ = bf16[576,768]{1,0:T(8,128)(2,1)S(1)} collective-permute-done((bf16[576,768]{1,0:T(8,128)(2,1)}, bf16[576,768]{1,0:T(8,128)(2,1)S(1)}, u32[]{:S(2)}, u32[]{:S(2)}) %collective-permute-start.65) | collective-permute-done | bytes 884768 | tf_op jit(solution)/shard_map/ppermute | solution.py:310
  532.5 6.6 chain_step.56
  542.6 6.6 side_step.49.refs_14_
  552.4 6.5 chain_step.64
  560.4 9.1 %collective-permute-done.67.refs_8_ = bf16[576,768]{1,0:T(8,128)(2,1)S(1)} collective-permute-done((bf16[576,768]{1,0:T(8,128)(2,1)}, bf16[576,768]{1,0:T(8,128)(2,1)S(1)}, u32[]{:S(2)}, u32[]{:S(2)}) %collective-permute-start.67) | collective-permute-done | bytes 884768 | tf_op jit(solution)/shard_map/ppermute | solution.py:310
  570.4 6.5 chain_step.57
  580.2 6.7 side_step.50.refs_14_
  595.3 12.1 %collective-permute-done.69.refs_1_ = bf16[576,768]{1,0:T(8,128)(2,1)S(1)} collective-permute-done((bf16[576,768]{1,0:T(8,128)(2,1)}, bf16[576,768]{1,0:T(8,128)(2,1)S(1)}, u32[]{:S(2)}, u32[]{:S(2)}) %collective-permute-start.69) | collective-permute-done | bytes 884768 | tf_op jit(solution)/shard_map/ppermute | solution.py:310
  613.4 6.7 side_step.51.refs_14_
  638.9 6.7 side_step.52.refs_14_
  654.5 7.1 side_step.53
  668.0 10.8 %collective-permute-done.91 = bf16[576,512]{1,0:T(8,128)(2,1)S(1)} collective-permute-done((bf16[576,512]{1,0:T(8,128)(2,1)S(1)}, bf16[576,512]{1,0:T(8,128)(2,1)S(1)}, u32[]{:S(2)}, u32[]{:S(2)}) %collective-permute-start.91) | collective-permute-done | bytes 589856 | tf_op jit(solution)/shard_map/ppermute | solution.py:298
  693.1 10.6 %collective-permute-done.93 = bf16[1,384,512]{2,1,0:T(8,128)(2,1)S(1)} collective-permute-done((bf16[1,384,512]{2,1,0:T(8,128)(2,1)S(1)}, bf16[1,384,512]{2,1,0:T(8,128)(2,1)S(1)}, u32[]{:S(2)}, u32[]{:S(2)}) %collective-permute-start.93) | collective-permute-done | bytes 393248 | tf_op jit(solution)/shard_map/ppermute | solution.py:554
  705.9 5.0 collective-permute-start.94
  710.9 11.1 %collective-permute-done.95 = bf16[192,512]{1,0:T(8,128)(2,1)S(1)} collective-permute-done((bf16[192,512]{1,0:T(8,128)(2,1)S(1)}, bf16[192,512]{1,0:T(8,128)(2,1)S(1)}, u32[]{:S(2)}, u32[]{:S(2)}) %collective-permute-start.95) | collective-permute-done | bytes 196640 | tf_op jit(solution)/shard_map/ppermute | solution.py:566
  722.0 4.3 collective-permute-done.94
  (405 shorter events, 258.2 us)
Async XLA Ops:
  32.5 32.2 %collective-permute-start.4 = (bf16[576,1152]{1,0:T(8,128)(2,1)S(1)}, bf16[576,1152]{1,0:T(8,128)(2,1)}, u32[]{:S(2)}, u32[]{:S(2)}) collective-permute-start(bf16[576,1152]{1,0:T(8,128)(2,1)S(1)} %pad_maximum_fusion.3), channel_id=1, source_target_pairs={{0,1},{1,0},{2,3},{3,2},{4,5},{5,4},{6,7},{7,6},{8,9},{9,8},{10,11... | collective-permute-start | bytes 3981320 | tf_op jit(solution)/shard_map/ppermute | solution.py:298
  35.0 54.5 %collective-permute-start.5 = (bf16[768,512]{1,0:T(8,128)(2,1)}, bf16[768,512]{1,0:T(8,128)(2,1)S(1)}, u32[]{:S(2)}, u32[]{:S(2)}) collective-permute-start(bf16[768,512]{1,0:T(8,128)(2,1)} %pad_maximum_fusion.5), channel_id=1, source_target_pairs={{0,1},{1,0},{2,3},{3,2},{4,5},{5,4},{6,7},{7,6},{8,9},{9,8},{10,11... | collective-permute-start | bytes 2359304 | tf_op jit(solution)/shard_map/ppermute | solution.py:298
  88.3 32.6 %collective-permute-start.9 = (bf16[768,512]{1,0:T(8,128)(2,1)}, bf16[768,512]{1,0:T(8,128)(2,1)S(1)}, u32[]{:S(2)}, u32[]{:S(2)}) collective-permute-start(bf16[768,512]{1,0:T(8,128)(2,1)} %side_step.27), channel_id=1, source_target_pairs={{0,1},{1,0},{2,3},{3,2},{4,5},{5,4},{6,7},{7,6},{8,9},{9,8},{10,11... | collective-permute-start | bytes 2359304 | tf_op jit(solution)/shard_map/ppermute | solution.py:298
  100.9 36.8 %collective-permute-start.12 = (bf16[768,512]{1,0:T(8,128)(2,1)}, bf16[768,512]{1,0:T(8,128)(2,1)S(1)}, u32[]{:S(2)}, u32[]{:S(2)}) collective-permute-start(bf16[768,512]{1,0:T(8,128)(2,1)} %side_step.28), channel_id=1, source_target_pairs={{0,1},{1,0},{2,3},{3,2},{4,5},{5,4},{6,7},{7,6},{8,9},{9,8},{10,11... | collective-permute-start | bytes 2359304 | tf_op jit(solution)/shard_map/ppermute | solution.py:298
  110.5 30.7 %collective-permute-start.13 = (bf16[576,512]{1,0:T(8,128)(2,1)}, bf16[576,512]{1,0:T(8,128)(2,1)S(1)}, u32[]{:S(2)}, u32[]{:S(2)}) collective-permute-start(bf16[576,512]{1,0:T(8,128)(2,1)} %get-tuple-element.284), channel_id=1, source_target_pairs={{0,2},{1,3},{2,0},{3,1},{4,6},{5,7},{6,4},{7,5},{8,10},{9,11},{10,... | collective-permute-start | bytes 1769480 | tf_op jit(solution)/shard_map/ppermute | solution.py:310
  115.7 27.1 %collective-permute-start.14 = (bf16[576,512]{1,0:T(8,128)(2,1)}, bf16[576,512]{1,0:T(8,128)(2,1)}, u32[]{:S(2)}, u32[]{:S(2)}) collective-permute-start(bf16[576,512]{1,0:T(8,128)(2,1)} %get-tuple-element.285), channel_id=1, source_target_pairs={{0,8},{1,9},{2,4},{3,5},{4,2},{5,3},{6,14},{7,15},{8,0},{9,1},{10,... | collective-permute-start | bytes 1769480 | tf_op jit(solution)/shard_map/ppermute | solution.py:310
  115.7 38.8 %collective-permute-start.15 = (bf16[768,512]{1,0:T(8,128)(2,1)}, bf16[768,512]{1,0:T(8,128)(2,1)S(1)}, u32[]{:S(2)}, u32[]{:S(2)}) collective-permute-start(bf16[768,512]{1,0:T(8,128)(2,1)} %side_step.29), channel_id=1, source_target_pairs={{0,1},{1,0},{2,3},{3,2},{4,5},{5,4},{6,7},{7,6},{8,9},{9,8},{10,11... | collective-permute-start | bytes 2359304 | tf_op jit(solution)/shard_map/ppermute | solution.py:298
  141.2 30.2 %collective-permute-start.18 = (bf16[768,512]{1,0:T(8,128)(2,1)}, bf16[768,512]{1,0:T(8,128)(2,1)S(1)}, u32[]{:S(2)}, u32[]{:S(2)}) collective-permute-start(bf16[768,512]{1,0:T(8,128)(2,1)} %side_step.30), channel_id=1, source_target_pairs={{0,1},{1,0},{2,3},{3,2},{4,5},{5,4},{6,7},{7,6},{8,9},{9,8},{10,11... | collective-permute-start | bytes 2359304 | tf_op jit(solution)/shard_map/ppermute | solution.py:298
  148.3 26.6 %collective-permute-start.19 = (bf16[576,512]{1,0:T(8,128)(2,1)}, bf16[576,512]{1,0:T(8,128)(2,1)S(1)}, u32[]{:S(2)}, u32[]{:S(2)}) collective-permute-start(bf16[576,512]{1,0:T(8,128)(2,1)} %get-tuple-element.298), channel_id=1, source_target_pairs={{0,2},{1,3},{2,0},{3,1},{4,6},{5,7},{6,4},{7,5},{8,10},{9,11},{10,... | collective-permute-start | bytes 1769480 | tf_op jit(solution)/shard_map/ppermute | solution.py:310
  150.4 26.1 %collective-permute-start.20 = (bf16[576,512]{1,0:T(8,128)(2,1)}, bf16[576,512]{1,0:T(8,128)(2,1)}, u32[]{:S(2)}, u32[]{:S(2)}) collective-permute-start(bf16[576,512]{1,0:T(8,128)(2,1)} %get-tuple-element.299), channel_id=1, source_target_pairs={{0,8},{1,9},{2,4},{3,5},{4,2},{5,3},{6,14},{7,15},{8,0},{9,1},{10,... | collective-permute-start | bytes 1769480 | tf_op jit(solution)/shard_map/ppermute | solution.py:310
  162.8 27.3 %collective-permute-start.21 = (bf16[768,512]{1,0:T(8,128)(2,1)}, bf16[768,512]{1,0:T(8,128)(2,1)S(1)}, u32[]{:S(2)}, u32[]{:S(2)}) collective-permute-start(bf16[768,512]{1,0:T(8,128)(2,1)} %side_step.31), channel_id=1, source_target_pairs={{0,1},{1,0},{2,3},{3,2},{4,5},{5,4},{6,7},{7,6},{8,9},{9,8},{10,11... | collective-permute-start | bytes 2359304 | tf_op jit(solution)/shard_map/ppermute | solution.py:298
  174.9 30.2 %collective-permute-start.24 = (bf16[768,512]{1,0:T(8,128)(2,1)}, bf16[768,512]{1,0:T(8,128)(2,1)S(1)}, u32[]{:S(2)}, u32[]{:S(2)}) collective-permute-start(bf16[768,512]{1,0:T(8,128)(2,1)} %side_step.32), channel_id=1, source_target_pairs={{0,1},{1,0},{2,3},{3,2},{4,5},{5,4},{6,7},{7,6},{8,9},{9,8},{10,11... | collective-permute-start | bytes 2359304 | tf_op jit(solution)/shard_map/ppermute | solution.py:298
  183.1 32.9 %collective-permute-start.25 = (bf16[576,768]{1,0:T(8,128)(2,1)}, bf16[576,768]{1,0:T(8,128)(2,1)}, u32[]{:S(2)}, u32[]{:S(2)}) collective-permute-start(bf16[576,768]{1,0:T(8,128)(2,1)} %get-tuple-element.316), channel_id=1, source_target_pairs={{0,2},{1,3},{2,0},{3,1},{4,6},{5,7},{6,4},{7,5},{8,10},{9,11},{10,... | collective-permute-start | bytes 2654216 | tf_op jit(solution)/shard_map/ppermute | solution.py:310
  185.1 32.8 %collective-permute-start.26 = (bf16[576,768]{1,0:T(8,128)(2,1)}, bf16[576,768]{1,0:T(8,128)(2,1)}, u32[]{:S(2)}, u32[]{:S(2)}) collective-permute-start(bf16[576,768]{1,0:T(8,128)(2,1)} %get-tuple-element.317), channel_id=1, source_target_pairs={{0,8},{1,9},{2,4},{3,5},{4,2},{5,3},{6,14},{7,15},{8,0},{9,1},{10,... | collective-permute-start | bytes 2654216 | tf_op jit(solution)/shard_map/ppermute | solution.py:310
  188.7 37.4 %collective-permute-start.27 = (bf16[768,512]{1,0:T(8,128)(2,1)}, bf16[768,512]{1,0:T(8,128)(2,1)S(1)}, u32[]{:S(2)}, u32[]{:S(2)}) collective-permute-start(bf16[768,512]{1,0:T(8,128)(2,1)} %side_step.33), channel_id=1, source_target_pairs={{0,1},{1,0},{2,3},{3,2},{4,5},{5,4},{6,7},{7,6},{8,9},{9,8},{10,11... | collective-permute-start | bytes 2359304 | tf_op jit(solution)/shard_map/ppermute | solution.py:298
  197.4 32.1 %collective-permute-start.28 = (bf16[576,768]{1,0:T(8,128)(2,1)}, bf16[576,768]{1,0:T(8,128)(2,1)}, u32[]{:S(2)}, u32[]{:S(2)}) collective-permute-start(bf16[576,768]{1,0:T(8,128)(2,1)} %get-tuple-element.324), channel_id=1, source_target_pairs={{0,2},{1,3},{2,0},{3,1},{4,6},{5,7},{6,4},{7,5},{8,10},{9,11},{10,... | collective-permute-start | bytes 2654216 | tf_op jit(solution)/shard_map/ppermute | solution.py:310
  229.5 27.9 %collective-permute-start.33 = (bf16[768,512]{1,0:T(8,128)(2,1)}, bf16[768,512]{1,0:T(8,128)(2,1)S(1)}, u32[]{:S(2)}, u32[]{:S(2)}) collective-permute-start(bf16[768,512]{1,0:T(8,128)(2,1)} %side_step.35), channel_id=1, source_target_pairs={{0,1},{1,0},{2,3},{3,2},{4,5},{5,4},{6,7},{7,6},{8,9},{9,8},{10,11... | collective-permute-start | bytes 2359304 | tf_op jit(solution)/shard_map/ppermute | solution.py:298
  237.3 28.9 %collective-permute-start.34 = (bf16[576,768]{1,0:T(8,128)(2,1)}, bf16[576,768]{1,0:T(8,128)(2,1)}, u32[]{:S(2)}, u32[]{:S(2)}) collective-permute-start(bf16[576,768]{1,0:T(8,128)(2,1)} %get-tuple-element.343), channel_id=1, source_target_pairs={{0,2},{1,3},{2,0},{3,1},{4,6},{5,7},{6,4},{7,5},{8,10},{9,11},{10,... | collective-permute-start | bytes 2654216 | tf_op jit(solution)/shard_map/ppermute | solution.py:310
  239.2 27.9 %collective-permute-start.35 = (bf16[576,768]{1,0:T(8,128)(2,1)}, bf16[576,768]{1,0:T(8,128)(2,1)}, u32[]{:S(2)}, u32[]{:S(2)}) collective-permute-start(bf16[576,768]{1,0:T(8,128)(2,1)} %get-tuple-element.344), channel_id=1, source_target_pairs={{0,8},{1,9},{2,4},{3,5},{4,2},{5,3},{6,14},{7,15},{8,0},{9,1},{10,... | collective-permute-start | bytes 2654216 | tf_op jit(solution)/shard_map/ppermute | solution.py:310
  247.3 28.9 %collective-permute-start.36 = (bf16[768,512]{1,0:T(8,128)(2,1)}, bf16[768,512]{1,0:T(8,128)(2,1)S(1)}, u32[]{:S(2)}, u32[]{:S(2)}) collective-permute-start(bf16[768,512]{1,0:T(8,128)(2,1)} %get-tuple-element.353), channel_id=1, source_target_pairs={{0,1},{1,0},{2,3},{3,2},{4,5},{5,4},{6,7},{7,6},{8,9},{9,8},{10,11... | collective-permute-start | bytes 2359304 | tf_op jit(solution)/shard_map/ppermute | solution.py:298
  255.4 29.7 %collective-permute-start.37 = (bf16[576,768]{1,0:T(8,128)(2,1)}, bf16[576,768]{1,0:T(8,128)(2,1)}, u32[]{:S(2)}, u32[]{:S(2)}) collective-permute-start(bf16[576,768]{1,0:T(8,128)(2,1)} %get-tuple-element.354), channel_id=1, source_target_pairs={{0,2},{1,3},{2,0},{3,1},{4,6},{5,7},{6,4},{7,5},{8,10},{9,11},{10,... | collective-permute-start | bytes 2654216 | tf_op jit(solution)/shard_map/ppermute | solution.py:310
  257.4 28.0 %collective-permute-start.38 = (bf16[576,768]{1,0:T(8,128)(2,1)}, bf16[576,768]{1,0:T(8,128)(2,1)}, u32[]{:S(2)}, u32[]{:S(2)}) collective-permute-start(bf16[576,768]{1,0:T(8,128)(2,1)} %get-tuple-element.355), channel_id=1, source_target_pairs={{0,8},{1,9},{2,4},{3,5},{4,2},{5,3},{6,14},{7,15},{8,0},{9,1},{10,... | collective-permute-start | bytes 2654216 | tf_op jit(solution)/shard_map/ppermute | solution.py:310
  266.2 27.8 %collective-permute-start.39 = (bf16[768,512]{1,0:T(8,128)(2,1)}, bf16[768,512]{1,0:T(8,128)(2,1)S(1)}, u32[]{:S(2)}, u32[]{:S(2)}) collective-permute-start(bf16[768,512]{1,0:T(8,128)(2,1)} %side_step.37), channel_id=1, source_target_pairs={{0,1},{1,0},{2,3},{3,2},{4,5},{5,4},{6,7},{7,6},{8,9},{9,8},{10,11... | collective-permute-start | bytes 2359304 | tf_op jit(solution)/shard_map/ppermute | solution.py:298
  273.7 30.4 %collective-permute-start.40 = (bf16[576,768]{1,0:T(8,128)(2,1)}, bf16[576,768]{1,0:T(8,128)(2,1)}, u32[]{:S(2)}, u32[]{:S(2)}) collective-permute-start(bf16[576,768]{1,0:T(8,128)(2,1)} %get-tuple-element.362), channel_id=1, source_target_pairs={{0,2},{1,3},{2,0},{3,1},{4,6},{5,7},{6,4},{7,5},{8,10},{9,11},{10,... | collective-permute-start | bytes 2654216 | tf_op jit(solution)/shard_map/ppermute | solution.py:310
  276.2 29.4 %collective-permute-start.41 = (bf16[576,768]{1,0:T(8,128)(2,1)}, bf16[576,768]{1,0:T(8,128)(2,1)}, u32[]{:S(2)}, u32[]{:S(2)}) collective-permute-start(bf16[576,768]{1,0:T(8,128)(2,1)} %get-tuple-element.363), channel_id=1, source_target_pairs={{0,8},{1,9},{2,4},{3,5},{4,2},{5,3},{6,14},{7,15},{8,0},{9,1},{10,... | collective-permute-start | bytes 2654216 | tf_op jit(solution)/shard_map/ppermute | solution.py:310
  285.2 28.7 %collective-permute-start.42 = (bf16[768,512]{1,0:T(8,128)(2,1)}, bf16[768,512]{1,0:T(8,128)(2,1)S(1)}, u32[]{:S(2)}, u32[]{:S(2)}) collective-permute-start(bf16[768,512]{1,0:T(8,128)(2,1)} %get-tuple-element.372), channel_id=1, source_target_pairs={{0,1},{1,0},{2,3},{3,2},{4,5},{5,4},{6,7},{7,6},{8,9},{9,8},{10,11... | collective-permute-start | bytes 2359304 | tf_op jit(solution)/shard_map/ppermute | solution.py:298
  292.0 31.1 %collective-permute-start.43 = (bf16[576,768]{1,0:T(8,128)(2,1)}, bf16[576,768]{1,0:T(8,128)(2,1)}, u32[]{:S(2)}, u32[]{:S(2)}) collective-permute-start(bf16[576,768]{1,0:T(8,128)(2,1)} %get-tuple-element.373), channel_id=1, source_target_pairs={{0,2},{1,3},{2,0},{3,1},{4,6},{5,7},{6,4},{7,5},{8,10},{9,11},{10,... | collective-permute-start | bytes 2654216 | tf_op jit(solution)/shard_map/ppermute | solution.py:310
  294.0 30.0 %collective-permute-start.44 = (bf16[576,768]{1,0:T(8,128)(2,1)}, bf16[576,768]{1,0:T(8,128)(2,1)}, u32[]{:S(2)}, u32[]{:S(2)}) collective-permute-start(bf16[576,768]{1,0:T(8,128)(2,1)} %get-tuple-element.374), channel_id=1, source_target_pairs={{0,8},{1,9},{2,4},{3,5},{4,2},{5,3},{6,14},{7,15},{8,0},{9,1},{10,... | collective-permute-start | bytes 2654216 | tf_op jit(solution)/shard_map/ppermute | solution.py:310
  304.1 28.3 %collective-permute-start.45 = (bf16[768,512]{1,0:T(8,128)(2,1)}, bf16[768,512]{1,0:T(8,128)(2,1)S(1)}, u32[]{:S(2)}, u32[]{:S(2)}) collective-permute-start(bf16[768,512]{1,0:T(8,128)(2,1)} %side_step.39), channel_id=1, source_target_pairs={{0,1},{1,0},{2,3},{3,2},{4,5},{5,4},{6,7},{7,6},{8,9},{9,8},{10,11... | collective-permute-start | bytes 2359304 | tf_op jit(solution)/shard_map/ppermute | solution.py:298
  312.2 29.8 %collective-permute-start.46 = (bf16[576,768]{1,0:T(8,128)(2,1)}, bf16[576,768]{1,0:T(8,128)(2,1)}, u32[]{:S(2)}, u32[]{:S(2)}) collective-permute-start(bf16[576,768]{1,0:T(8,128)(2,1)} %get-tuple-element.381), channel_id=1, source_target_pairs={{0,2},{1,3},{2,0},{3,1},{4,6},{5,7},{6,4},{7,5},{8,10},{9,11},{10,... | collective-permute-start | bytes 2654216 | tf_op jit(solution)/shard_map/ppermute | solution.py:310
  313.9 28.2 %collective-permute-start.47 = (bf16[576,768]{1,0:T(8,128)(2,1)}, bf16[576,768]{1,0:T(8,128)(2,1)}, u32[]{:S(2)}, u32[]{:S(2)}) collective-permute-start(bf16[576,768]{1,0:T(8,128)(2,1)} %get-tuple-element.382), channel_id=1, source_target_pairs={{0,8},{1,9},{2,4},{3,5},{4,2},{5,3},{6,14},{7,15},{8,0},{9,1},{10,... | collective-permute-start | bytes 2654216 | tf_op jit(solution)/shard_map/ppermute | solution.py:310
  323.1 27.4 %collective-permute-start.48 = (bf16[768,512]{1,0:T(8,128)(2,1)}, bf16[768,512]{1,0:T(8,128)(2,1)S(1)}, u32[]{:S(2)}, u32[]{:S(2)}) collective-permute-start(bf16[768,512]{1,0:T(8,128)(2,1)} %get-tuple-element.391), channel_id=1, source_target_pairs={{0,1},{1,0},{2,3},{3,2},{4,5},{5,4},{6,7},{7,6},{8,9},{9,8},{10,11... | collective-permute-start | bytes 2359304 | tf_op jit(solution)/shard_map/ppermute | solution.py:298
  330.4 30.6 %collective-permute-start.49 = (bf16[576,768]{1,0:T(8,128)(2,1)}, bf16[576,768]{1,0:T(8,128)(2,1)}, u32[]{:S(2)}, u32[]{:S(2)}) collective-permute-start(bf16[576,768]{1,0:T(8,128)(2,1)} %get-tuple-element.392), channel_id=1, source_target_pairs={{0,2},{1,3},{2,0},{3,1},{4,6},{5,7},{6,4},{7,5},{8,10},{9,11},{10,... | collective-permute-start | bytes 2654216 | tf_op jit(solution)/shard_map/ppermute | solution.py:310
  332.4 28.8 %collective-permute-start.50 = (bf16[576,768]{1,0:T(8,128)(2,1)}, bf16[576,768]{1,0:T(8,128)(2,1)}, u32[]{:S(2)}, u32[]{:S(2)}) collective-permute-start(bf16[576,768]{1,0:T(8,128)(2,1)} %get-tuple-element.393), channel_id=1, source_target_pairs={{0,8},{1,9},{2,4},{3,5},{4,2},{5,3},{6,14},{7,15},{8,0},{9,1},{10,... | collective-permute-start | bytes 2654216 | tf_op jit(solution)/shard_map/ppermute | solution.py:310
  348.6 31.4 %collective-permute-start.52 = (bf16[576,768]{1,0:T(8,128)(2,1)}, bf16[576,768]{1,0:T(8,128)(2,1)}, u32[]{:S(2)}, u32[]{:S(2)}) collective-permute-start(bf16[576,768]{1,0:T(8,128)(2,1)} %get-tuple-element.400), channel_id=1, source_target_pairs={{0,2},{1,3},{2,0},{3,1},{4,6},{5,7},{6,4},{7,5},{8,10},{9,11},{10,... | collective-permute-start | bytes 2654216 | tf_op jit(solution)/shard_map/ppermute | solution.py:310
  350.5 29.5 %collective-permute-start.53 = (bf16[576,768]{1,0:T(8,128)(2,1)}, bf16[576,768]{1,0:T(8,128)(2,1)}, u32[]{:S(2)}, u32[]{:S(2)}) collective-permute-start(bf16[576,768]{1,0:T(8,128)(2,1)} %get-tuple-element.401), channel_id=1, source_target_pairs={{0,8},{1,9},{2,4},{3,5},{4,2},{5,3},{6,14},{7,15},{8,0},{9,1},{10,... | collective-permute-start | bytes 2654216 | tf_op jit(solution)/shard_map/ppermute | solution.py:310
  361.0 27.4 %collective-permute-start.54 = (bf16[768,512]{1,0:T(8,128)(2,1)}, bf16[768,512]{1,0:T(8,128)(2,1)S(1)}, u32[]{:S(2)}, u32[]{:S(2)}) collective-permute-start(bf16[768,512]{1,0:T(8,128)(2,1)} %get-tuple-element.410), channel_id=1, source_target_pairs={{0,1},{1,0},{2,3},{3,2},{4,5},{5,4},{6,7},{7,6},{8,9},{9,8},{10,11... | collective-permute-start | bytes 2359304 | tf_op jit(solution)/shard_map/ppermute | solution.py:298
  367.8 31.0 %collective-permute-start.55 = (bf16[576,768]{1,0:T(8,128)(2,1)}, bf16[576,768]{1,0:T(8,128)(2,1)S(1)}, u32[]{:S(2)}, u32[]{:S(2)}) collective-permute-start(bf16[576,768]{1,0:T(8,128)(2,1)} %get-tuple-element.411), channel_id=1, source_target_pairs={{0,2},{1,3},{2,0},{3,1},{4,6},{5,7},{6,4},{7,5},{8,10},{9,11},{10,... | collective-permute-start | bytes 2654216 | tf_op jit(solution)/shard_map/ppermute | solution.py:310
  371.1 29.2 %collective-permute-start.56 = (bf16[576,768]{1,0:T(8,128)(2,1)}, bf16[576,768]{1,0:T(8,128)(2,1)}, u32[]{:S(2)}, u32[]{:S(2)}) collective-permute-start(bf16[576,768]{1,0:T(8,128)(2,1)} %get-tuple-element.412), channel_id=1, source_target_pairs={{0,8},{1,9},{2,4},{3,5},{4,2},{5,3},{6,14},{7,15},{8,0},{9,1},{10,... | collective-permute-start | bytes 2654216 | tf_op jit(solution)/shard_map/ppermute | solution.py:310
  386.5 31.4 %collective-permute-start.59 = (bf16[576,768]{1,0:T(8,128)(2,1)}, bf16[576,768]{1,0:T(8,128)(2,1)}, u32[]{:S(2)}, u32[]{:S(2)}) collective-permute-start(bf16[576,768]{1,0:T(8,128)(2,1)} %get-tuple-element.420), channel_id=1, source_target_pairs={{0,2},{1,3},{2,0},{3,1},{4,6},{5,7},{6,4},{7,5},{8,10},{9,11},{10,... | collective-permute-start | bytes 2654216 | tf_op jit(solution)/shard_map/ppermute | solution.py:310
  388.4 29.5 %collective-permute-start.60 = (bf16[576,768]{1,0:T(8,128)(2,1)}, bf16[576,768]{1,0:T(8,128)(2,1)}, u32[]{:S(2)}, u32[]{:S(2)}) collective-permute-start(bf16[576,768]{1,0:T(8,128)(2,1)} %get-tuple-element.421), channel_id=1, source_target_pairs={{0,8},{1,9},{2,4},{3,5},{4,2},{5,3},{6,14},{7,15},{8,0},{9,1},{10,... | collective-permute-start | bytes 2654216 | tf_op jit(solution)/shard_map/ppermute | solution.py:310
  398.8 27.4 %collective-permute-start.75 = (bf16[768,512]{1,0:T(8,128)(2,1)}, bf16[768,512]{1,0:T(8,128)(2,1)S(1)}, u32[]{:S(2)}, u32[]{:S(2)}) collective-permute-start(bf16[768,512]{1,0:T(8,128)(2,1)} %get-tuple-element.468), channel_id=1, source_target_pairs={{0,1},{1,0},{2,3},{3,2},{4,5},{5,4},{6,7},{7,6},{8,9},{9,8},{10,11... | collective-permute-start | bytes 2359304 | tf_op jit(solution)/shard_map/ppermute | solution.py:298
  409.6 27.2 %collective-permute-start.76 = (bf16[576,768]{1,0:T(8,128)(2,1)}, bf16[576,768]{1,0:T(8,128)(2,1)S(1)}, u32[]{:S(2)}, u32[]{:S(2)}) collective-permute-start(bf16[576,768]{1,0:T(8,128)(2,1)} %get-tuple-element.469), channel_id=1, source_target_pairs={{0,2},{1,3},{2,0},{3,1},{4,6},{5,7},{6,4},{7,5},{8,10},{9,11},{10,... | collective-permute-start | bytes 2654216 | tf_op jit(solution)/shard_map/ppermute | solution.py:310
  424.4 31.4 %collective-permute-start.61 = (bf16[576,768]{1,0:T(8,128)(2,1)}, bf16[576,768]{1,0:T(8,128)(2,1)}, u32[]{:S(2)}, u32[]{:S(2)}) collective-permute-start(bf16[576,768]{1,0:T(8,128)(2,1)} %get-tuple-element.425), channel_id=1, source_target_pairs={{0,2},{1,3},{2,0},{3,1},{4,6},{5,7},{6,4},{7,5},{8,10},{9,11},{10,... | collective-permute-start | bytes 2654216 | tf_op jit(solution)/shard_map/ppermute | solution.py:310
  426.3 29.6 %collective-permute-start.62 = (bf16[576,768]{1,0:T(8,128)(2,1)}, bf16[576,768]{1,0:T(8,128)(2,1)}, u32[]{:S(2)}, u32[]{:S(2)}) collective-permute-start(bf16[576,768]{1,0:T(8,128)(2,1)} %get-tuple-element.426), channel_id=1, source_target_pairs={{0,8},{1,9},{2,4},{3,5},{4,2},{5,3},{6,14},{7,15},{8,0},{9,1},{10,... | collective-permute-start | bytes 2654216 | tf_op jit(solution)/shard_map/ppermute | solution.py:310
  444.6 30.0 %collective-permute-start.78 = (bf16[576,768]{1,0:T(8,128)(2,1)}, bf16[576,768]{1,0:T(8,128)(2,1)S(1)}, u32[]{:S(2)}, u32[]{:S(2)}) collective-permute-start(bf16[576,768]{1,0:T(8,128)(2,1)} %get-tuple-element.474), channel_id=1, source_target_pairs={{0,2},{1,3},{2,0},{3,1},{4,6},{5,7},{6,4},{7,5},{8,10},{9,11},{10,... | collective-permute-start | bytes 2654216 | tf_op jit(solution)/shard_map/ppermute | solution.py:310
  446.1 28.6 %collective-permute-start.79 = (bf16[576,768]{1,0:T(8,128)(2,1)}, bf16[576,768]{1,0:T(8,128)(2,1)S(1)}, u32[]{:S(2)}, u32[]{:S(2)}) collective-permute-start(bf16[576,768]{1,0:T(8,128)(2,1)} %get-tuple-element.475), channel_id=1, source_target_pairs={{0,8},{1,9},{2,4},{3,5},{4,2},{5,3},{6,14},{7,15},{8,0},{9,1},{10,... | collective-permute-start | bytes 2654216 | tf_op jit(solution)/shard_map/ppermute | solution.py:310
  462.3 31.4 %collective-permute-start.63 = (bf16[576,768]{1,0:T(8,128)(2,1)}, bf16[576,768]{1,0:T(8,128)(2,1)}, u32[]{:S(2)}, u32[]{:S(2)}) collective-permute-start(bf16[576,768]{1,0:T(8,128)(2,1)} %get-tuple-element.430), channel_id=1, source_target_pairs={{0,2},{1,3},{2,0},{3,1},{4,6},{5,7},{6,4},{7,5},{8,10},{9,11},{10,... | collective-permute-start | bytes 2654216 | tf_op jit(solution)/shard_map/ppermute | solution.py:310
  464.1 29.6 %collective-permute-start.64 = (bf16[576,768]{1,0:T(8,128)(2,1)}, bf16[576,768]{1,0:T(8,128)(2,1)}, u32[]{:S(2)}, u32[]{:S(2)}) collective-permute-start(bf16[576,768]{1,0:T(8,128)(2,1)} %get-tuple-element.431), channel_id=1, source_target_pairs={{0,8},{1,9},{2,4},{3,5},{4,2},{5,3},{6,14},{7,15},{8,0},{9,1},{10,... | collective-permute-start | bytes 2654216 | tf_op jit(solution)/shard_map/ppermute | solution.py:310
  483.1 29.5 %collective-permute-start.80 = (bf16[576,768]{1,0:T(8,128)(2,1)}, bf16[576,768]{1,0:T(8,128)(2,1)S(1)}, u32[]{:S(2)}, u32[]{:S(2)}) collective-permute-start(bf16[576,768]{1,0:T(8,128)(2,1)} %get-tuple-element.479), channel_id=1, source_target_pairs={{0,2},{1,3},{2,0},{3,1},{4,6},{5,7},{6,4},{7,5},{8,10},{9,11},{10,... | collective-permute-start | bytes 2654216 | tf_op jit(solution)/shard_map/ppermute | solution.py:310
  484.6 28.0 %collective-permute-start.81 = (bf16[576,768]{1,0:T(8,128)(2,1)}, bf16[576,768]{1,0:T(8,128)(2,1)S(1)}, u32[]{:S(2)}, u32[]{:S(2)}) collective-permute-start(bf16[576,768]{1,0:T(8,128)(2,1)} %get-tuple-element.480), channel_id=1, source_target_pairs={{0,8},{1,9},{2,4},{3,5},{4,2},{5,3},{6,14},{7,15},{8,0},{9,1},{10,... | collective-permute-start | bytes 2654216 | tf_op jit(solution)/shard_map/ppermute | solution.py:310
  500.3 31.3 %collective-permute-start.65 = (bf16[576,768]{1,0:T(8,128)(2,1)}, bf16[576,768]{1,0:T(8,128)(2,1)S(1)}, u32[]{:S(2)}, u32[]{:S(2)}) collective-permute-start(bf16[576,768]{1,0:T(8,128)(2,1)} %get-tuple-element.435), channel_id=1, source_target_pairs={{0,2},{1,3},{2,0},{3,1},{4,6},{5,7},{6,4},{7,5},{8,10},{9,11},{10,... | collective-permute-start | bytes 2654216 | tf_op jit(solution)/shard_map/ppermute | solution.py:310
  502.1 29.4 %collective-permute-start.66 = (bf16[576,768]{1,0:T(8,128)(2,1)}, bf16[576,768]{1,0:T(8,128)(2,1)}, u32[]{:S(2)}, u32[]{:S(2)}) collective-permute-start(bf16[576,768]{1,0:T(8,128)(2,1)} %get-tuple-element.436), channel_id=1, source_target_pairs={{0,8},{1,9},{2,4},{3,5},{4,2},{5,3},{6,14},{7,15},{8,0},{9,1},{10,... | collective-permute-start | bytes 2654216 | tf_op jit(solution)/shard_map/ppermute | solution.py:310
  521.0 29.5 %collective-permute-start.82 = (bf16[576,768]{1,0:T(8,128)(2,1)}, bf16[576,768]{1,0:T(8,128)(2,1)S(1)}, u32[]{:S(2)}, u32[]{:S(2)}) collective-permute-start(bf16[576,768]{1,0:T(8,128)(2,1)} %get-tuple-element.484), channel_id=1, source_target_pairs={{0,2},{1,3},{2,0},{3,1},{4,6},{5,7},{6,4},{7,5},{8,10},{9,11},{10,... | collective-permute-start | bytes 2654216 | tf_op jit(solution)/shard_map/ppermute | solution.py:310
  522.5 28.0 %collective-permute-start.83 = (bf16[576,768]{1,0:T(8,128)(2,1)}, bf16[576,768]{1,0:T(8,128)(2,1)S(1)}, u32[]{:S(2)}, u32[]{:S(2)}) collective-permute-start(bf16[576,768]{1,0:T(8,128)(2,1)} %get-tuple-element.485), channel_id=1, source_target_pairs={{0,8},{1,9},{2,4},{3,5},{4,2},{5,3},{6,14},{7,15},{8,0},{9,1},{10,... | collective-permute-start | bytes 2654216 | tf_op jit(solution)/shard_map/ppermute | solution.py:310
  539.0 30.4 %collective-permute-start.67 = (bf16[576,768]{1,0:T(8,128)(2,1)}, bf16[576,768]{1,0:T(8,128)(2,1)S(1)}, u32[]{:S(2)}, u32[]{:S(2)}) collective-permute-start(bf16[576,768]{1,0:T(8,128)(2,1)} %get-tuple-element.440), channel_id=1, source_target_pairs={{0,2},{1,3},{2,0},{3,1},{4,6},{5,7},{6,4},{7,5},{8,10},{9,11},{10,... | collective-permute-start | bytes 2654216 | tf_op jit(solution)/shard_map/ppermute | solution.py:310
  540.5 29.0 %collective-permute-start.68 = (bf16[576,768]{1,0:T(8,128)(2,1)}, bf16[576,768]{1,0:T(8,128)(2,1)}, u32[]{:S(2)}, u32[]{:S(2)}) collective-permute-start(bf16[576,768]{1,0:T(8,128)(2,1)} %get-tuple-element.441), channel_id=1, source_target_pairs={{0,8},{1,9},{2,4},{3,5},{4,2},{5,3},{6,14},{7,15},{8,0},{9,1},{10,... | collective-permute-start | bytes 2654216 | tf_op jit(solution)/shard_map/ppermute | solution.py:310
  558.9 29.5 %collective-permute-start.84 = (bf16[576,768]{1,0:T(8,128)(2,1)}, bf16[576,768]{1,0:T(8,128)(2,1)S(1)}, u32[]{:S(2)}, u32[]{:S(2)}) collective-permute-start(bf16[576,768]{1,0:T(8,128)(2,1)} %get-tuple-element.489), channel_id=1, source_target_pairs={{0,2},{1,3},{2,0},{3,1},{4,6},{5,7},{6,4},{7,5},{8,10},{9,11},{10,... | collective-permute-start | bytes 2654216 | tf_op jit(solution)/shard_map/ppermute | solution.py:310
  560.4 28.0 %collective-permute-start.85 = (bf16[576,768]{1,0:T(8,128)(2,1)}, bf16[576,768]{1,0:T(8,128)(2,1)S(1)}, u32[]{:S(2)}, u32[]{:S(2)}) collective-permute-start(bf16[576,768]{1,0:T(8,128)(2,1)} %get-tuple-element.490), channel_id=1, source_target_pairs={{0,8},{1,9},{2,4},{3,5},{4,2},{5,3},{6,14},{7,15},{8,0},{9,1},{10,... | collective-permute-start | bytes 2654216 | tf_op jit(solution)/shard_map/ppermute | solution.py:310
  576.9 30.5 %collective-permute-start.69 = (bf16[576,768]{1,0:T(8,128)(2,1)}, bf16[576,768]{1,0:T(8,128)(2,1)S(1)}, u32[]{:S(2)}, u32[]{:S(2)}) collective-permute-start(bf16[576,768]{1,0:T(8,128)(2,1)} %get-tuple-element.445), channel_id=1, source_target_pairs={{0,2},{1,3},{2,0},{3,1},{4,6},{5,7},{6,4},{7,5},{8,10},{9,11},{10,... | collective-permute-start | bytes 2654216 | tf_op jit(solution)/shard_map/ppermute | solution.py:310
  578.4 29.0 %collective-permute-start.70 = (bf16[576,768]{1,0:T(8,128)(2,1)}, bf16[576,768]{1,0:T(8,128)(2,1)}, u32[]{:S(2)}, u32[]{:S(2)}) collective-permute-start(bf16[576,768]{1,0:T(8,128)(2,1)} %get-tuple-element.446), channel_id=1, source_target_pairs={{0,8},{1,9},{2,4},{3,5},{4,2},{5,3},{6,14},{7,15},{8,0},{9,1},{10,... | collective-permute-start | bytes 2654216 | tf_op jit(solution)/shard_map/ppermute | solution.py:310
  593.6 37.1 %collective-permute-start.86 = (bf16[576,256]{1,0:T(8,128)(2,1)}, bf16[576,256]{1,0:T(8,128)(2,1)S(1)}, u32[]{:S(2)}, u32[]{:S(2)}) collective-permute-start(bf16[576,256]{1,0:T(8,128)(2,1)} %get-tuple-element.494), channel_id=1, source_target_pairs={{0,2},{1,3},{2,0},{3,1},{4,6},{5,7},{6,4},{7,5},{8,10},{9,11},{10,... | collective-permute-start | bytes 884744 | tf_op jit(solution)/shard_map/ppermute | solution.py:310
  595.3 35.4 %collective-permute-start.87 = (bf16[576,256]{1,0:T(8,128)(2,1)}, bf16[576,256]{1,0:T(8,128)(2,1)S(1)}, u32[]{:S(2)}, u32[]{:S(2)}) collective-permute-start(bf16[576,256]{1,0:T(8,128)(2,1)} %get-tuple-element.495), channel_id=1, source_target_pairs={{0,8},{1,9},{2,4},{3,5},{4,2},{5,3},{6,14},{7,15},{8,0},{9,1},{10,... | collective-permute-start | bytes 884744 | tf_op jit(solution)/shard_map/ppermute | solution.py:310
  621.5 28.6 %collective-permute-start.88 = (bf16[576,512]{1,0:T(8,128)(2,1)S(1)}, bf16[576,512]{1,0:T(8,128)(2,1)S(1)}, u32[]{:S(2)}, u32[]{:S(2)}) collective-permute-start(bf16[576,512]{1,0:T(8,128)(2,1)S(1)} %dynamic-slice.17), channel_id=1, source_target_pairs={{0,1},{1,0},{2,3},{3,2},{4,5},{5,4},{6,7},{7,6},{8,9},{9,8},{10,11... | collective-permute-start | bytes 1769480 | tf_op jit(solution)/shard_map/ppermute | solution.py:298
  (86 other events, 889.8 us)

commit v2 on v1

--- a/solution.py
+++ b/solution.py
@@ -11,7 +11,7 @@
 HOP = 2
 AHEAD = 3
 BATCH = 2
-VMEM = 58 * 1024 * 1024
+VMEM = 62 * 1024 * 1024
 
 
 def grid_of(size):
@@ -43,7 +43,7 @@
 
 
 def chain_kernel(cfg, *refs):
-    deep, across, width, sums, sums_in, back, back_in = cfg
+    deep, across, width, sums, sums_in, sums_out, back, back_in = cfg
     take = taker(refs)
     (info,) = take()
     if sums:
@@ -61,7 +61,7 @@
         hid_v, hid_sem = take(2)
     place = info[0]
     odd = lax.rem(place, 2)
-    wide = 2 * width if sums else 0
+    wide = 2 * width if sums_out else 0
     in_wide = came[0].shape[1] - (width if back_in else 0) if came else 0
     half = sent[0].shape[0]
     copies = []
@@ -130,7 +130,8 @@
             first = place == (0 if s == 0 else deep - 1)
             before = came_v[s, :, : 2 * width].astype(jnp.float32)
             total = total + jnp.where(first, 0.0, before)
-        sent_v[s, :, : 2 * width] = total.astype(jnp.bfloat16)
+        if sums_out:
+            sent_v[s, :, : 2 * width] = total.astype(jnp.bfloat16)
         if back:
             value, upper = total[:, :width], total[:, width:]
             hidden = value / (1.0 + jnp.exp(-value)) * upper
@@ -160,11 +161,12 @@
 
 
 def side_kernel(cfg, *refs):
-    deep, across, width, steps, n_send = cfg
+    deep, across, width, steps_direct, offsets, n_send, kinds = cfg
+    steps = len(steps_direct)
     take = taker(refs)
     (info,) = take()
     gate, up, down = take(3)
-    hids = take(steps)
+    hids = [take(2) if direct else take() for direct in steps_direct]
     got = [[take(across - 1) for _ in range(deep)] for _ in range(steps)]
     acc_in = take() if steps else None
     sent = take(n_send)
@@ -180,7 +182,19 @@
         acc_in, acc_out = acc_in[0], acc_out[0]
         half = acc_in.shape[0] // 2
         for n in range(steps):
-            waits.append(begin(hids[n], hid_v.at[n], hid_sem.at[n]))
+            for s in range(2):
+                here = hid_v.at[n, pl.ds(s * half, half)]
+                sem = hid_sem.at[n, s]
+                if len(hids[n]) == 1:
+                    waits.append(begin(hids[n][0].at[pl.ds(s * half, half)], here, sem))
+                    continue
+                for slot in range(2):
+
+                    @pl.when(lax.rem(place + s, 2) == 1 - slot)
+                    def _(src=hids[n][slot], here=here, sem=sem):
+                        pltpu.make_async_copy(src, here, sem).start()
+
+                waits.append(pltpu.make_async_copy(hids[n][0], here, sem))
             for s in range(2):
                 own = info[1] * part_rows + info[2 + 4 * n + s]
                 waits.append(
@@ -192,31 +206,41 @@
                         here = i if s == 0 else deep - 1 - i
 
                         @pl.when(place == here)
-                        def _(src=got[n][i][j - 1], dst=dst, sem=sem):
-                            pltpu.make_async_copy(
-                                src.at[pl.ds(2 * width, width)], dst, sem
-                            ).start()
-
-                    waits.append(
-                        pltpu.make_async_copy(
-                            got[n][0][j - 1].at[pl.ds(2 * width, width)], dst, sem
-                        )
-                    )
+                        def _(src=got[n][i][j - 1], at=offsets[n][i], dst=dst, sem=sem):
+                            pltpu.make_async_copy(src.at[pl.ds(at, width)], dst, sem).start()
+
+                    src = got[n][0][j - 1].at[pl.ds(offsets[n][0], width)]
+                    waits.append(pltpu.make_async_copy(src, dst, sem))
         tile = half // 2
-        acc_copies = [
-            begin(
-                acc_in.at[pl.ds(i * tile, tile)],
-                acc_v.at[pl.ds(i * tile, tile)],
-                acc_sem.at[i],
+        acc_loads = [
+            pltpu.make_async_copy(
+                acc_in.at[pl.ds(i * tile, tile)], acc_v.at[pl.ds(i * tile, tile)], acc_sem.at[i]
             )
             for i in range(4)
         ]
+        acc_stores = [
+            pltpu.make_async_copy(
+                acc_v.at[pl.ds(i * tile, tile)], acc_out.at[pl.ds(i * tile, tile)], acco_sem.at[i]
+            )
+            for i in range(4)
+        ]
+        needed = []
+        for s in range(2):
+            flags = [info[4 + 4 * n + s] for n in range(steps)]
+            needed.append(functools.reduce(jnp.maximum, flags) > 0)
+
+            @pl.when(needed[s])
+            def _(s=s):
+                for i in (2 * s, 2 * s + 1):
+                    acc_loads[i].start()
+
     base = 2 + 4 * steps
     for j in range(n_send):
-        for k, ref in enumerate((gate, up, down)):
+        for k, kind in enumerate(kinds):
+            ref = (gate, up, down)[kind]
             sends.append(
                 begin(
-                    rows_at(ref, info[base + j], width),
+                    rows_at(ref, info[base + 2 * j + kind // 2], width),
                     send_v.at[j, pl.ds(k * width, width)],
                     send_sem.at[j, k],
                 )
@@ -229,24 +253,35 @@
         for copy in waits:
             copy.wait()
         feat = d_v.shape[-1]
-        for i in range(4):
-            s = i // 2
-            here = pl.ds(i * tile, tile)
-            acc_copies[i].wait()
-            for j in range(across):
-                total = acc_v[here, pl.ds(j * feat, feat)]
-                for n in range(steps):
-                    hidden = hid_v[n, here, :]
-                    valid = info[4 + 4 * n + s] > 0
-                    hidden = jnp.where(valid, hidden, jnp.zeros_like(hidden))
-                    total += lax.dot_general(
-                        hidden,
-                        d_v[n, s, j],
-                        (((1,), (0,)), ((), ())),
-                        preferred_element_type=jnp.float32,
-                    )
-                acc_v[here, pl.ds(j * feat, feat)] = total
-            copies.append(begin(acc_v.at[here], acc_out.at[here], acco_sem.at[i]))
+        for s in range(2):
+
+            @pl.when(needed[s])
+            def _(s=s):
+                for i in (2 * s, 2 * s + 1):
+                    here = pl.ds(i * tile, tile)
+                    acc_loads[i].wait()
+                    for j in range(across):
+                        total = acc_v[here, pl.ds(j * feat, feat)]
+                        for n in range(steps):
+                            hidden = hid_v[n, here, :]
+                            valid = info[4 + 4 * n + s] > 0
+                            hidden = jnp.where(valid, hidden, jnp.zeros_like(hidden))
+                            total += lax.dot_general(
+                                hidden,
+                                d_v[n, s, j],
+                                (((1,), (0,)), ((), ())),
+                                preferred_element_type=jnp.float32,
+                            )
+                        acc_v[here, pl.ds(j * feat, feat)] = total
+                    acc_stores[i].start()
+
+        for s in range(2):
+
+            @pl.when(needed[s])
+            def _(s=s):
+                for i in (2 * s, 2 * s + 1):
+                    acc_stores[i].wait()
+
     for copy in copies:
         copy.wait()
 
@@ -320,21 +355,35 @@
     def send_start(k, j):
         return (x ^ j) * part_rows + min(k * width, part_rows - width)
 
-    def hand_over_early(k, weights):
-        hand_over(
-            k,
-            [
-                jnp.concatenate(
-                    [lax.dynamic_slice_in_dim(w, send_start(k, j), width, 0) for w in weights]
-                )
-                for j in range(1, across)
-            ],
+    reach = hop * (deep - 1)
+
+    def kinds_of(k):
+        return (0, 1) * (k < n_chunks) + (2,) * (reach <= k < n_chunks + reach)
+
+    def send_starts(k):
+        return [send_start(c, j) for j in range(1, across) for c in (k, max(k - reach, 0))]
+
+    def message(k):
+        return [jax.ShapeDtypeStruct((len(kinds_of(k)) * width, feat), bf)] * (across - 1)
+
+    def lay_out(k, weights):
+        n_send, rows = across - 1, len(kinds_of(k)) * width
+        return call(
+            functools.partial(side_kernel, (deep, across, width, (), (), n_send, kinds_of(k))),
+            [jnp.stack([z, x] + send_starts(k)).astype(jnp.int32)] + list(weights),
+            message(k),
+            [pltpu.VMEM((n_send, rows, feat), bf), dma((n_send, 3)), dma((n_send,))],
+            {},
+            0,
+            2 * 1024 * 1024,
+            "side_step",
         )
 
     weights = (gate_weight, up_weight, down_weight)
     early = min(ahead, n_chunks)
-    for k in range(min(2, early)):
-        hand_over_early(k, weights)
+    firsts = [lay_out(k, weights) for k in range(early)]
+    firsts[0], tokens = lax.optimization_barrier((firsts[0], tokens))
+    hand_over(0, firsts[0])
 
     picked = routes == expert
     chosen = jnp.any(picked, axis=1)
@@ -370,9 +419,9 @@
     mine = jnp.concatenate([pick(pieces, z ^ a) for a in range(deep)])
     mine, got[0] = lax.optimization_barrier((mine, got[0]))
     by_group = [swap(mine, 0, i) if i else mine for i in range(across)]
-    by_group, weights = lax.optimization_barrier((by_group, weights))
-    for k in range(2, early):
-        hand_over_early(k, weights)
+    by_group, firsts = lax.optimization_barrier((by_group, firsts))
+    for k in range(1, early):
+        hand_over(k, firsts[k])
     toks = jnp.stack(
         [jnp.concatenate([columns(g, x ^ j, feat) for g in by_group]) for j in range(across)]
     )
@@ -381,7 +430,6 @@
     came_from = (notes[0] * 128.0 + notes[1]).astype(jnp.int32) - 1
     weight = notes[2] + notes[3] + notes[4]
 
-    reach = hop * (deep - 1)
     n_steps = n_chunks + 2 * reach
     acc = jnp.zeros((total_rows, across * feat), f32)
     msgs, waiting, order = {}, [], None
@@ -396,68 +444,79 @@
 
     last_skip = n_chunks * width - part_rows
 
-    def candidates(base):
-        return [a for i in range(deep) for a in got[min(max(base - hop * i, 0), n_chunks - 1)]]
+    def send_on(t, res):
+        if t == n_chunks + reach - 1:
+            msgs[t - 1], res = lax.optimization_barrier((msgs[t - 1], res))
+        msgs[t] = (pairing(res[0], 0), pairing(res[1], 1))
+        if t == n_chunks + reach - 1:
+            for u in range(t + 1, n_steps - hop):
+                msgs[u] = (pairing(msgs[u - hop][1], 0), pairing(msgs[u - hop][0], 1))
+
+    def chunks(base):
+        return [min(max(base - hop * i, 0), n_chunks - 1) for i in range(deep)]
 
     for t in range(n_steps):
         sums = t < n_chunks + reach
         back = t >= reach
-        before = t - hop
-        sums_in = sums and before >= 0
-        back_in = back and before >= reach
-        cfg = (deep, across, width, sums, sums_in, back, back_in)
-        skip = last_skip if t - reach == n_chunks - 1 else 0
-        up_c, dn_c = t - hop * z, t - hop * (deep - 1 - z)
-        info = jnp.stack([z, x, start_of(up_c), start_of(dn_c), jnp.int32(skip)]).astype(
-            jnp.int32
-        )
-        if order is not None:
-            info, order = lax.optimization_barrier((info, order))
-            if "acc" in order:
-                acc = order["acc"]
-            if "sent" in order:
-                hand_over(t - 1 + early, order["sent"])
-            order = None
-        if t == early_at + 3:
-            info, early_parts = lax.optimization_barrier((info, early_parts))
-        args, outs, scratch = [info], [], []
+        if not sums:
+            waiting.append((t, msgs[t - hop]))
         if sums:
-            args += [gate_weight, up_weight, toks] + candidates(t)
-            scratch += [
-                pltpu.VMEM((across, total_rows, feat), bf),
-                pltpu.VMEM((2, across, 2 * width, feat), bf),
-                dma((2,)),
-                dma((2, across, 2)),
-            ]
-        if sums_in or back_in:
-            args += list(msgs[before])
-            scratch += [pltpu.VMEM((2,) + msgs[before][0].shape, bf), dma((2,))]
-        out_width = 2 * width * sums + width * back
-        outs += [jax.ShapeDtypeStruct((half_rows, out_width), bf)] * 2
-        scratch += [pltpu.VMEM((2, half_rows, out_width), bf), dma((2,))]
-        if back:
-            outs += [jax.ShapeDtypeStruct((total_rows, width), bf)]
-            scratch += [pltpu.VMEM((total_rows, width), bf), dma]
-        res = call(
-            functools.partial(chain_kernel, cfg),
-            args,
-            outs,
-            scratch,
-            {},
-            4 * total_rows * width * across * feat * sums,
-            8 * 1024 * 1024,
-            "chain_step",
-        )
-        if back:
-            waiting.append((t, res[2]))
+            before = t - hop
+            sums_in = sums and before >= 0
+            sums_out = t + hop < n_chunks + reach
+            back_in = back and before >= reach
+            cfg = (deep, across, width, sums, sums_in, sums_out, back, back_in)
+            skip = last_skip if t - reach == n_chunks - 1 else 0
+            up_c, dn_c = t - hop * z, t - hop * (deep - 1 - z)
+            info = jnp.stack([z, x, start_of(up_c), start_of(dn_c), jnp.int32(skip)]).astype(
+                jnp.int32
+            )
+            if order is not None:
+                info, order = lax.optimization_barrier((info, order))
+                if "acc" in order:
+                    acc = order["acc"]
+                if "sent" in order:
+                    hand_over(t - 1 + early, order["sent"])
+                order = None
+            args, outs, scratch = [info], [], []
+            if sums:
+                args += [gate_weight, up_weight, toks] + [a for c in chunks(t) for a in got[c]]
+                scratch += [
+                    pltpu.VMEM((across, total_rows, feat), bf),
+                    pltpu.VMEM((2, across, 2 * width, feat), bf),
+                    dma((2,)),
+                    dma((2, across, 2)),
+                ]
+            if sums_in or back_in:
+                args += list(msgs[before])
+                scratch += [pltpu.VMEM((2,) + msgs[before][0].shape, bf), dma((2,))]
+            out_width = 2 * width * sums_out + width * back
+            outs += [jax.ShapeDtypeStruct((half_rows, out_width), bf)] * 2
+            scratch += [pltpu.VMEM((2, half_rows, out_width), bf), dma((2,))]
+            if back:
+                outs += [jax.ShapeDtypeStruct((total_rows, width), bf)]
+                scratch += [pltpu.VMEM((total_rows, width), bf), dma]
+            res = call(
+                functools.partial(chain_kernel, cfg),
+                args,
+                outs,
+                scratch,
+                {},
+                4 * total_rows * width * across * feat * sums,
+                8 * 1024 * 1024,
+                "chain_step",
+            )
+            if back:
+                waiting.append((t, [res[2]]))
 
         next_k = t + early
-        n_send = across - 1 if next_k < n_chunks else 0
-        flush = len(waiting) == batch or t in (early_at, n_steps - 1)
+        kinds = kinds_of(next_k)
+        n_send = across - 1 if kinds else 0
+        flush = (len(waiting) == batch and t < early_at) or t in (early_at, n_steps - 1)
         steps = len(waiting) if flush else 0
         if not steps and not n_send:
-            if t + hop < n_steps:
-                msgs[t] = (pairing(res[0], 0), pairing(res[1], 1))
+            if sums:
+                send_on(t, res)
             continue
         done, entries = [], [z, x]
         if steps:
@@ -466,20 +525,29 @@
             up_c, dn_c = at - reach - hop * z, at - reach - hop * (deep - 1 - z)
             entries += [start_of(up_c), start_of(dn_c)]
             entries += [((c >= 0) & (c < n_chunks)).astype(jnp.int32) for c in (up_c, dn_c)]
-        entries += [send_start(next_k, j + 1) for j in range(n_send)]
+        if n_send:
+            entries += send_starts(next_k)
         side_info = jnp.stack([jnp.int32(e) for e in entries]).astype(jnp.int32)
-        side_info, res = lax.optimization_barrier((side_info, res))
-        if t + hop < n_steps:
-            msgs[t] = (pairing(res[0], 0), pairing(res[1], 1))
+        if t == n_steps - 1:
+            side_info, early_parts = lax.optimization_barrier((side_info, early_parts))
+        if sums:
+            side_info, res = lax.optimization_barrier((side_info, res))
+            send_on(t, res)
+        if t >= n_chunks + reach - 1 and t + 1 in msgs:
+            side_info, msgs[t + 1] = lax.optimization_barrier((side_info, msgs[t + 1]))
         args = [side_info]
-        args += [gate_weight, up_weight, down_weight] + [hid for _, hid in done]
+        args += [gate_weight, up_weight, down_weight] + [h for _, hid in done for h in hid]
+        offsets = []
         for at, _ in done:
-            args += candidates(at - reach)
+            args += [a for c in chunks(at - reach) for a in got[c + reach]]
+            offsets.append(
+                tuple(2 * width * (c + reach < n_chunks) for c in chunks(at - reach))
+            )
         aliases, outs, scratch = {}, [], []
-        outs += [jax.ShapeDtypeStruct((3 * width, feat), bf)] * n_send
         if n_send:
+            outs += message(next_k)
             scratch += [
-                pltpu.VMEM((n_send, 3 * width, feat), bf),
+                pltpu.VMEM((n_send, len(kinds) * width, feat), bf),
                 dma((n_send, 3)),
                 dma((n_send,)),
             ]
@@ -491,13 +559,24 @@
                 pltpu.VMEM((steps, total_rows, width), bf),
                 pltpu.VMEM((steps, 2, across, width, feat), bf),
                 pltpu.VMEM(acc.shape, f32),
-                dma((steps,)),
+                dma((steps, 2)),
                 dma((steps, 2, across)),
                 dma((4,)),
                 dma((4,)),
             ]
         res = call(
-            functools.partial(side_kernel, (deep, across, width, steps, n_send)),
+            functools.partial(
+                side_kernel,
+                (
+                    deep,
+                    across,
+                    width,
+                    tuple(len(h) == 2 for _, h in done),
+                    tuple(offsets),
+                    n_send,
+                    kinds,
+                ),
+            ),
             args,
             outs,
             scratch,

time: 738 us -> 683 us (0.925)
  waiting for transfers between devices: 209 us -> 151 us
  starting transfers between devices: 97.4 us -> 141 us
  local copies, waits for them, and re-layouts: 70.5 us -> 46.8 us
  Pallas kernels: 327 us -> 310 us
    ppermute x64, waiting for transfers between devices: 94.4 us -> 47.5 us  [pairing(): return lax.ppermute(array, ('member', 'fsdp'), perm)]
    ppermute x64, starting transfers between devices: 61.9 us -> 92.8 us  [pairing(): return lax.ppermute(array, ('member', 'fsdp'), perm)]
    pallas_call x61 -> x60, Pallas kernels: 327 us -> 310 us  [call(): pl.pallas_call(kernel, out_shape=outs, in_specs=[pl.BlockSpec(memory_spac...]
    unnamed x108 -> x90, local copies, waits for them, and re-layouts: 23.4 us -> 8.73 us
    ppermute x28 -> x34, starting transfers between devices: 27.9 us -> 41.5 us  [swap(): return lax.ppermute(array, 'fsdp', perm)]
    ppermute x28 -> x34, waiting for transfers between devices: 85.2 us -> 74.5 us  [swap(): return lax.ppermute(array, 'fsdp', perm)]
    another operation x34 -> x28, local copies, waits for them, and re-layouts: 22.2 us -> 18.5 us  [body(): jnp.stack([z, x, start_of(up_c), start_of(dn_c), jnp.int32(skip)])]
  transfers between devices with their start and end apart: 96 -> 102, of which waited for: 35 -> 33; matrix products, arithmetic and copies ran while one was open for 7% -> 6% of each run, Pallas kernels for 44% -> 44%
where the time goes in v2:
time: 683 us; the launch traced here: 673 us
  Pallas kernels  310 us (45%)
  waiting for transfers between devices  151 us (22%)
  starting transfers between devices  141 us (21%)
  local copies, waits for them, and re-layouts  46.8 us (7%)
  other arithmetic  16.8 us (2%)
    pallas_call x60, Pallas kernels, call(): pl.pallas_call(kernel, out_shape=outs, in_specs=[pl.BlockSpec(memory_spac...  310 us
    ppermute x64, starting transfers between devices, pairing(): return lax.ppermute(array, ('member', 'fsdp'), perm)  92.8 us
    ppermute x34, waiting for transfers between devices, swap(): return lax.ppermute(array, 'fsdp', perm)  74.5 us
    ppermute x64, waiting for transfers between devices, pairing(): return lax.ppermute(array, ('member', 'fsdp'), perm)  47.5 us
    ppermute x34, starting transfers between devices, swap(): return lax.ppermute(array, 'fsdp', perm)  41.5 us
    another operation x28, local copies, waits for them, and re-layouts, body(): jnp.stack([z, x, start_of(up_c), start_of(dn_c), jnp.int32(skip)])  18.5 us
    ppermute x2, waiting for transfers between devices, body(): parts.append(lax.ppermute(pick(mixed, slot ^ j), ('member', 'fsdp'), perm))  15.5 us
    ppermute x2, waiting for transfers between devices, body(): came = lax.ppermute(give, 'member', [(m, m ^ bit) for m in range(members)])  14 us
  transfers between devices with their start and end apart: 102, of which 33 were waited for; matrix products, arithmetic and copies ran while one was open for 6% of the time, Pallas kernels for 44%

profile of v2, /device:TPU:4, one launch (start us, length us, event | category | flops | bytes accessed | tf_op | source)
XLA Modules:
  0.0 673.3 jit_solution(4590051365409038360)
XLA Ops:
  13.2 10.0 %collective-permute-done = bf16[144,1152]{1,0:T(8,128)(2,1)S(1)} collective-permute-done((bf16[144,1152]{1,0:T(8,128)(2,1)S(1)}, bf16[144,1152]{1,0:T(8,128)(2,1)S(1)}, u32[]{:S(2)}, u32[]{:S(2)}) %collective-permute-start) | collective-permute-done | bytes 331808 | tf_op jit(solution)/shard_map/ppermute | solution.py:333
  23.2 11.5 %collective-permute-done.1 = bf16[144,1152]{1,0:T(8,128)(2,1)S(1)} collective-permute-done((bf16[144,1152]{1,0:T(8,128)(2,1)S(1)}, bf16[144,1152]{1,0:T(8,128)(2,1)S(1)}, u32[]{:S(2)}, u32[]{:S(2)}) %collective-permute-start.1) | collective-permute-done | bytes 331808 | tf_op jit(solution)/shard_map/ppermute | solution.py:333
  45.0 21.0 %collective-permute-done.4 = bf16[576,1152]{1,0:T(8,128)(2,1)} collective-permute-done((bf16[576,1152]{1,0:T(8,128)(2,1)}, bf16[576,1152]{1,0:T(8,128)(2,1)}, u32[]{:S(2)}, u32[]{:S(2)}) %collective-permute-start.4) | collective-permute-done | bytes 1327136 | tf_op jit(solution)/shard_map/ppermute | solution.py:333
  72.6 5.2 chain_step.28
  77.8 7.6 %collective-permute-start.7 = (bf16[576,512]{1,0:T(8,128)(2,1)}, bf16[576,512]{1,0:T(8,128)(2,1)}, u32[]{:S(2)}, u32[]{:S(2)}) collective-permute-start(bf16[576,512]{1,0:T(8,128)(2,1)} %get-tuple-element.279), channel_id=1, source_target_pairs={{0,2},{1,3},{2,0},{3,1},{4,6},{5,7},{6,4},{7,5},{8,10},{9,11},{10,... | collective-permute-start | bytes 1769480 | tf_op jit(solution)/shard_map/ppermute | solution.py:345
  90.9 5.2 chain_step.29
  101.3 5.5 chain_step.30
  106.8 6.0 collective-permute-start.13
  118.2 5.6 chain_step.31
  130.7 5.6 chain_step.32
  142.4 5.5 chain_step.33
  156.3 6.8 %chain_step.34 = (bf16[576,768]{1,0:T(8,128)(2,1)}, bf16[576,768]{1,0:T(8,128)(2,1)}, bf16[1152,256]{1,0:T(8,128)(2,1)}) custom-call(s32[5]{0:T(128)} %stack.1250.refs_0_, bf16[11008,512]{1,0:T(8,128)(2,1)} %bitcast.203, bf16[11008,512]{1,0:T(8,128)(2,1)} %bitcast.263, bf16[2,1152,512]{2,1,0:T(8,128)(2,1)} %pad_maximum_fusion.1.refs_3_, ...), custom_call_target="tpu_custom_call" | custom-call | flops 1207959552 | bytes 8388608 | tf_op jit(solution)/shard_map/chain_step/pallas_call | solution.py:291
  175.0 6.4 chain_step.35
  188.8 5.7 side_step.42
  197.0 6.5 chain_step.36
  208.6 6.5 chain_step.37
  220.4 5.7 side_step.44
  228.4 6.5 chain_step.38
  240.1 5.2 collective-permute-done.34.refs_8_
  246.0 6.5 chain_step.39
  256.1 5.7 side_step.46
  264.3 6.5 chain_step.40
  277.8 5.4 collective-permute-done.40.refs_8_
  283.9 6.5 chain_step.41
  293.9 7.3 %side_step.48 = (bf16[768,512]{1,0:T(8,128)(2,1)}, f32[1152,1024]{1,0:T(8,128)}) custom-call(s32[12]{0:T(128)} %stack.1192.refs_0_, bf16[11008,512]{1,0:T(8,128)(2,1)} %bitcast.218, bf16[11008,512]{1,0:T(8,128)(2,1)} %bitcast.278, bf16[11008,512]{1,0:T(8,128)(2,1)} %bitcast.324, ...), custom_call_target="tpu_custom_call", output_to_operand_aliasing={{1}: (14, {})} | custom-call | flops 1207959552 | bytes 12582912 | tf_op jit(solution)/shard_map/side_step/pallas_call | solution.py:291
  303.5 6.5 chain_step.42
  316.4 4.8 collective-permute-done.46.refs_8_
  321.2 6.5 chain_step.43
  332.0 7.3 %side_step.50 = (bf16[768,512]{1,0:T(8,128)(2,1)}, f32[1152,1024]{1,0:T(8,128)}) custom-call(s32[12]{0:T(128)} %stack.1174.refs_0_, bf16[11008,512]{1,0:T(8,128)(2,1)} %bitcast.222, bf16[11008,512]{1,0:T(8,128)(2,1)} %bitcast.282, bf16[11008,512]{1,0:T(8,128)(2,1)} %bitcast.326, ...), custom_call_target="tpu_custom_call", output_to_operand_aliasing={{1}: (14, {})} | custom-call | flops 1207959552 | bytes 12582912 | tf_op jit(solution)/shard_map/side_step/pallas_call | solution.py:291
  341.6 6.5 chain_step.44
  354.3 4.7 collective-permute-done.52.refs_8_
  359.1 6.5 chain_step.45
  369.9 7.3 %side_step.52 = (bf16[768,512]{1,0:T(8,128)(2,1)}, f32[1152,1024]{1,0:T(8,128)}) custom-call(s32[12]{0:T(128)} %stack.1156.refs_0_, bf16[11008,512]{1,0:T(8,128)(2,1)} %bitcast.226, bf16[11008,512]{1,0:T(8,128)(2,1)} %bitcast.286, bf16[11008,512]{1,0:T(8,128)(2,1)} %bitcast.328, ...), custom_call_target="tpu_custom_call", output_to_operand_aliasing={{1}: (14, {})} | custom-call | flops 1207959552 | bytes 12582912 | tf_op jit(solution)/shard_map/side_step/pallas_call | solution.py:291
  379.5 6.5 chain_step.46
  392.1 4.9 collective-permute-done.58.refs_8_
  397.0 6.5 chain_step.47
  409.8 7.2 %side_step.54 = (bf16[256,512]{1,0:T(8,128)(2,1)}, f32[1152,1024]{1,0:T(8,128)}) custom-call(s32[12]{0:T(128)} %stack.1138.refs_0_, bf16[11008,512]{1,0:T(8,128)(2,1)} %bitcast.230, bf16[11008,512]{1,0:T(8,128)(2,1)} %bitcast.290, bf16[11008,512]{1,0:T(8,128)(2,1)} %bitcast.330, ...), custom_call_target="tpu_custom_call", output_to_operand_aliasing={{1}: (14, {})} | custom-call | flops 1207959552 | bytes 12582912 | tf_op jit(solution)/shard_map/side_step/pallas_call | solution.py:291
  417.0 6.6 chain_step.48
  429.7 5.2 collective-permute-done.64.refs_8_
  434.9 6.4 chain_step.49
  446.2 7.2 %side_step.56 = (bf16[256,512]{1,0:T(8,128)(2,1)}, f32[1152,1024]{1,0:T(8,128)}) custom-call(s32[12]{0:T(128)} %stack.1116.refs_0_, bf16[11008,512]{1,0:T(8,128)(2,1)} %bitcast.234, bf16[11008,512]{1,0:T(8,128)(2,1)} %bitcast.294, bf16[11008,512]{1,0:T(8,128)(2,1)} %bitcast.332, ...), custom_call_target="tpu_custom_call", output_to_operand_aliasing={{1}: (14, {})} | custom-call | flops 1207959552 | bytes 12582912 | tf_op jit(solution)/shard_map/side_step/pallas_call | solution.py:291
  453.9 6.5 chain_step.50
  473.7 6.5 chain_step.51
  485.7 6.4 collective-permute-done.71.refs_10_.refs_11_.refs_12_.refs_15_
  492.7 7.2 %side_step.58 = (bf16[256,512]{1,0:T(8,128)(2,1)}, f32[1152,1024]{1,0:T(8,128)}) custom-call(s32[12]{0:T(128)} %stack.1098.refs_0_, bf16[11008,512]{1,0:T(8,128)(2,1)} %bitcast.238, bf16[11008,512]{1,0:T(8,128)(2,1)} %bitcast.298, bf16[11008,512]{1,0:T(8,128)(2,1)} %bitcast.334, ...), custom_call_target="tpu_custom_call", output_to_operand_aliasing={{1}: (14, {})} | custom-call | flops 1207959552 | bytes 12582912 | tf_op jit(solution)/shard_map/side_step/pallas_call | solution.py:291
  500.0 6.6 chain_step.52
  512.3 6.6 chain_step.53
  523.3 7.7 %collective-permute-done.77.refs_10_.refs_11_.refs_14_.refs_19_ = bf16[256,512]{1,0:T(8,128)(2,1)S(1)} collective-permute-done((bf16[256,512]{1,0:T(8,128)(2,1)S(1)}, bf16[256,512]{1,0:T(8,128)(2,1)S(1)}, u32[]{:S(2)}, u32[]{:S(2)}) %collective-permute-start.77) | collective-permute-done | bytes 262176 | tf_op jit(solution)/shard_map/ppermute | solution.py:333
  531.7 6.4 side_step.60.refs_14_
  538.1 6.0 chain_step.54
  548.4 6.1 chain_step.55
  554.6 4.5 collective-permute-start.86
  561.2 3.8 collective-permute-start.85
  571.6 6.4 side_step.61.refs_16_
  578.7 5.1 side_step.62.refs_28_
  586.7 3.8 collective-permute-start.93
  590.5 7.9 %collective-permute-start.95 = (bf16[576,256]{1,0:T(8,128)(2,1)S(1)}, bf16[576,256]{1,0:T(8,128)(2,1)S(1)}, u32[]{:S(2)}, u32[]{:S(2)}) collective-permute-start(bf16[576,256]{1,0:T(8,128)(2,1)S(1)} %collective-permute-done.94.refs_7_), channel_id=1, source_target_pairs={{0,2},{1,3},{2,0},{3,1},{4,6},{5,7},{6,4},{7,5},{8,10},{9,11},{10,... | collective-permute-start | bytes 884744 | tf_op jit(solution)/shard_map/ppermute | solution.py:345
  599.4 3.7 collective-permute-done.95.refs_10_
  603.8 7.5 %side_step.63 = f32[1152,1024]{1,0:T(8,128)} custom-call(s32[18]{0:T(128)} %stack.1053.refs_0_, bf16[11008,512]{1,0:T(8,128)(2,1)} %bitcast.247, bf16[11008,512]{1,0:T(8,128)(2,1)} %bitcast.307, bf16[11008,512]{1,0:T(8,128)(2,1)} %bitcast.339, bf16[576,256]{1,0:T(8,128)(2,1)} %copy-done.31, ...), custom_call_target="tpu_custom_call", output_to_operand_aliasing={{}: (28, {})} | custom-call | flops 2415919104 | bytes 12582912 | tf_op jit(solution)/shard_map/side_step/pallas_call | solution.py:291
  616.3 8.5 %collective-permute-done.97 = bf16[576,512]{1,0:T(8,128)(2,1)S(1)} collective-permute-done((bf16[576,512]{1,0:T(8,128)(2,1)S(1)}, bf16[576,512]{1,0:T(8,128)(2,1)S(1)}, u32[]{:S(2)}, u32[]{:S(2)}) %collective-permute-start.97) | collective-permute-done | bytes 589856 | tf_op jit(solution)/shard_map/ppermute | solution.py:333
  626.9 4.0 fusion
  639.2 10.7 %collective-permute-done.99 = bf16[1,384,512]{2,1,0:T(8,128)(2,1)S(1)} collective-permute-done((bf16[1,384,512]{2,1,0:T(8,128)(2,1)S(1)}, bf16[1,384,512]{2,1,0:T(8,128)(2,1)S(1)}, u32[]{:S(2)}, u32[]{:S(2)}) %collective-permute-start.99) | collective-permute-done | bytes 393248 | tf_op jit(solution)/shard_map/ppermute | solution.py:633
  652.8 3.6 collective-permute-start.100
  656.4 12.3 %collective-permute-done.101 = bf16[192,512]{1,0:T(8,128)(2,1)S(1)} collective-permute-done((bf16[192,512]{1,0:T(8,128)(2,1)S(1)}, bf16[192,512]{1,0:T(8,128)(2,1)S(1)}, u32[]{:S(2)}, u32[]{:S(2)}) %collective-permute-start.101) | collective-permute-done | bytes 196640 | tf_op jit(solution)/shard_map/ppermute | solution.py:645
  (386 shorter events, 246.8 us)
Async XLA Ops:
  8.9 25.8 %collective-permute-start.1 = (bf16[144,1152]{1,0:T(8,128)(2,1)S(1)}, bf16[144,1152]{1,0:T(8,128)(2,1)S(1)}, u32[]{:S(2)}, u32[]{:S(2)}) collective-permute-start(bf16[144,1152]{1,0:T(8,128)(2,1)S(1)} %get-tuple-element.547), channel_id=1, source_target_pairs={{0,4},{1,5},{2,6},{3,7},{4,0},{5,1},{6,2},{7,3},{8,12},{9,13},{10,... | collective-permute-start | bytes 995336 | tf_op jit(solution)/shard_map/ppermute | solution.py:333
  11.4 23.3 %collective-permute-start.2 = (bf16[144,1152]{1,0:T(8,128)(2,1)S(1)}, bf16[144,1152]{1,0:T(8,128)(2,1)}, u32[]{:S(2)}, u32[]{:S(2)}) collective-permute-start(bf16[144,1152]{1,0:T(8,128)(2,1)S(1)} %get-tuple-element.548), channel_id=1, source_target_pairs={{0,6},{1,7},{2,4},{3,5},{4,2},{5,3},{6,0},{7,1},{8,14},{9,15},{10,... | collective-permute-start | bytes 995336 | tf_op jit(solution)/shard_map/ppermute | solution.py:333
  11.7 25.5 %collective-permute-start.3 = (bf16[512,512]{1,0:T(8,128)(2,1)S(1)}, bf16[512,512]{1,0:T(8,128)(2,1)S(1)}, u32[]{:S(2)}, u32[]{:S(2)}) collective-permute-start(bf16[512,512]{1,0:T(8,128)(2,1)S(1)} %copy-done.29), channel_id=1, source_target_pairs={{0,1},{1,0},{2,3},{3,2},{4,5},{5,4},{6,7},{7,6},{8,9},{9,8},{10,11... | collective-permute-start | bytes 1572872 | tf_op jit(solution)/shard_map/ppermute | solution.py:333
  37.2 28.8 %collective-permute-start.4 = (bf16[576,1152]{1,0:T(8,128)(2,1)}, bf16[576,1152]{1,0:T(8,128)(2,1)}, u32[]{:S(2)}, u32[]{:S(2)}) collective-permute-start(bf16[576,1152]{1,0:T(8,128)(2,1)} %pad_maximum_fusion.3), channel_id=1, source_target_pairs={{0,1},{1,0},{2,3},{3,2},{4,5},{5,4},{6,7},{7,6},{8,9},{9,8},{10,11... | collective-permute-start | bytes 3981320 | tf_op jit(solution)/shard_map/ppermute | solution.py:333
  70.2 27.8 %collective-permute-start.6 = (bf16[512,512]{1,0:T(8,128)(2,1)}, bf16[512,512]{1,0:T(8,128)(2,1)S(1)}, u32[]{:S(2)}, u32[]{:S(2)}) collective-permute-start(bf16[512,512]{1,0:T(8,128)(2,1)} %side_step.34), channel_id=1, source_target_pairs={{0,1},{1,0},{2,3},{3,2},{4,5},{5,4},{6,7},{7,6},{8,9},{9,8},{10,11... | collective-permute-start | bytes 1572872 | tf_op jit(solution)/shard_map/ppermute | solution.py:333
  77.8 23.5 %collective-permute-start.7 = (bf16[576,512]{1,0:T(8,128)(2,1)}, bf16[576,512]{1,0:T(8,128)(2,1)}, u32[]{:S(2)}, u32[]{:S(2)}) collective-permute-start(bf16[576,512]{1,0:T(8,128)(2,1)} %get-tuple-element.279), channel_id=1, source_target_pairs={{0,2},{1,3},{2,0},{3,1},{4,6},{5,7},{6,4},{7,5},{8,10},{9,11},{10,... | collective-permute-start | bytes 1769480 | tf_op jit(solution)/shard_map/ppermute | solution.py:345
  88.5 25.8 %collective-permute-start.9 = (bf16[512,512]{1,0:T(8,128)(2,1)}, bf16[512,512]{1,0:T(8,128)(2,1)S(1)}, u32[]{:S(2)}, u32[]{:S(2)}) collective-permute-start(bf16[512,512]{1,0:T(8,128)(2,1)} %side_step.35), channel_id=1, source_target_pairs={{0,1},{1,0},{2,3},{3,2},{4,5},{5,4},{6,7},{7,6},{8,9},{9,8},{10,11... | collective-permute-start | bytes 1572872 | tf_op jit(solution)/shard_map/ppermute | solution.py:333
  106.8 21.8 %collective-permute-start.13 = (bf16[576,512]{1,0:T(8,128)(2,1)}, bf16[576,512]{1,0:T(8,128)(2,1)}, u32[]{:S(2)}, u32[]{:S(2)}) collective-permute-start(bf16[576,512]{1,0:T(8,128)(2,1)} %get-tuple-element.293), channel_id=1, source_target_pairs={{0,2},{1,3},{2,0},{3,1},{4,6},{5,7},{6,4},{7,5},{8,10},{9,11},{10,... | collective-permute-start | bytes 1769480 | tf_op jit(solution)/shard_map/ppermute | solution.py:345
  128.6 26.8 %collective-permute-start.18 = (bf16[768,512]{1,0:T(8,128)(2,1)}, bf16[768,512]{1,0:T(8,128)(2,1)S(1)}, u32[]{:S(2)}, u32[]{:S(2)}) collective-permute-start(bf16[768,512]{1,0:T(8,128)(2,1)} %side_step.38), channel_id=1, source_target_pairs={{0,1},{1,0},{2,3},{3,2},{4,5},{5,4},{6,7},{7,6},{8,9},{9,8},{10,11... | collective-permute-start | bytes 2359304 | tf_op jit(solution)/shard_map/ppermute | solution.py:333
  141.1 27.5 %collective-permute-start.21 = (bf16[768,512]{1,0:T(8,128)(2,1)}, bf16[768,512]{1,0:T(8,128)(2,1)}, u32[]{:S(2)}, u32[]{:S(2)}) collective-permute-start(bf16[768,512]{1,0:T(8,128)(2,1)} %side_step.39), channel_id=1, source_target_pairs={{0,1},{1,0},{2,3},{3,2},{4,5},{5,4},{6,7},{7,6},{8,9},{9,8},{10,11... | collective-permute-start | bytes 2359304 | tf_op jit(solution)/shard_map/ppermute | solution.py:333
  150.7 34.6 %collective-permute-start.24 = (bf16[768,512]{1,0:T(8,128)(2,1)}, bf16[768,512]{1,0:T(8,128)(2,1)S(1)}, u32[]{:S(2)}, u32[]{:S(2)}) collective-permute-start(bf16[768,512]{1,0:T(8,128)(2,1)} %side_step.40), channel_id=1, source_target_pairs={{0,1},{1,0},{2,3},{3,2},{4,5},{5,4},{6,7},{7,6},{8,9},{9,8},{10,11... | collective-permute-start | bytes 2359304 | tf_op jit(solution)/shard_map/ppermute | solution.py:333
  163.1 31.4 %collective-permute-start.25 = (bf16[576,768]{1,0:T(8,128)(2,1)}, bf16[576,768]{1,0:T(8,128)(2,1)}, u32[]{:S(2)}, u32[]{:S(2)}) collective-permute-start(bf16[576,768]{1,0:T(8,128)(2,1)} %get-tuple-element.325), channel_id=1, source_target_pairs={{0,2},{1,3},{2,0},{3,1},{4,6},{5,7},{6,4},{7,5},{8,10},{9,11},{10,... | collective-permute-start | bytes 2654216 | tf_op jit(solution)/shard_map/ppermute | solution.py:345
  168.5 28.5 %collective-permute-start.26 = (bf16[576,768]{1,0:T(8,128)(2,1)}, bf16[576,768]{1,0:T(8,128)(2,1)}, u32[]{:S(2)}, u32[]{:S(2)}) collective-permute-start(bf16[576,768]{1,0:T(8,128)(2,1)} %get-tuple-element.326), channel_id=1, source_target_pairs={{0,8},{1,9},{2,4},{3,5},{4,2},{5,3},{6,14},{7,15},{8,0},{9,1},{10,... | collective-permute-start | bytes 2654216 | tf_op jit(solution)/shard_map/ppermute | solution.py:345
  172.5 31.0 %collective-permute-start.27 = (bf16[768,512]{1,0:T(8,128)(2,1)}, bf16[768,512]{1,0:T(8,128)(2,1)}, u32[]{:S(2)}, u32[]{:S(2)}) collective-permute-start(bf16[768,512]{1,0:T(8,128)(2,1)} %side_step.41), channel_id=1, source_target_pairs={{0,1},{1,0},{2,3},{3,2},{4,5},{5,4},{6,7},{7,6},{8,9},{9,8},{10,11... | collective-permute-start | bytes 2359304 | tf_op jit(solution)/shard_map/ppermute | solution.py:333
  181.4 25.9 %collective-permute-start.28 = (bf16[576,768]{1,0:T(8,128)(2,1)}, bf16[576,768]{1,0:T(8,128)(2,1)}, u32[]{:S(2)}, u32[]{:S(2)}) collective-permute-start(bf16[576,768]{1,0:T(8,128)(2,1)} %get-tuple-element.333), channel_id=1, source_target_pairs={{0,2},{1,3},{2,0},{3,1},{4,6},{5,7},{6,4},{7,5},{8,10},{9,11},{10,... | collective-permute-start | bytes 2654216 | tf_op jit(solution)/shard_map/ppermute | solution.py:345
  185.3 23.3 %collective-permute-start.29 = (bf16[576,768]{1,0:T(8,128)(2,1)}, bf16[576,768]{1,0:T(8,128)(2,1)}, u32[]{:S(2)}, u32[]{:S(2)}) collective-permute-start(bf16[576,768]{1,0:T(8,128)(2,1)} %get-tuple-element.334), channel_id=1, source_target_pairs={{0,8},{1,9},{2,4},{3,5},{4,2},{5,3},{6,14},{7,15},{8,0},{9,1},{10,... | collective-permute-start | bytes 2654216 | tf_op jit(solution)/shard_map/ppermute | solution.py:345
  194.5 24.4 %collective-permute-start.30 = (bf16[768,512]{1,0:T(8,128)(2,1)}, bf16[768,512]{1,0:T(8,128)(2,1)S(1)}, u32[]{:S(2)}, u32[]{:S(2)}) collective-permute-start(bf16[768,512]{1,0:T(8,128)(2,1)} %get-tuple-element.343), channel_id=1, source_target_pairs={{0,1},{1,0},{2,3},{3,2},{4,5},{5,4},{6,7},{7,6},{8,9},{9,8},{10,11... | collective-permute-start | bytes 2359304 | tf_op jit(solution)/shard_map/ppermute | solution.py:333
  203.5 22.9 %collective-permute-start.31 = (bf16[576,768]{1,0:T(8,128)(2,1)}, bf16[576,768]{1,0:T(8,128)(2,1)}, u32[]{:S(2)}, u32[]{:S(2)}) collective-permute-start(bf16[576,768]{1,0:T(8,128)(2,1)} %get-tuple-element.344), channel_id=1, source_target_pairs={{0,2},{1,3},{2,0},{3,1},{4,6},{5,7},{6,4},{7,5},{8,10},{9,11},{10,... | collective-permute-start | bytes 2654216 | tf_op jit(solution)/shard_map/ppermute | solution.py:345
  203.6 24.8 %collective-permute-start.32 = (bf16[576,768]{1,0:T(8,128)(2,1)}, bf16[576,768]{1,0:T(8,128)(2,1)}, u32[]{:S(2)}, u32[]{:S(2)}) collective-permute-start(bf16[576,768]{1,0:T(8,128)(2,1)} %get-tuple-element.345), channel_id=1, source_target_pairs={{0,8},{1,9},{2,4},{3,5},{4,2},{5,3},{6,14},{7,15},{8,0},{9,1},{10,... | collective-permute-start | bytes 2654216 | tf_op jit(solution)/shard_map/ppermute | solution.py:345
  207.2 29.3 %collective-permute-start.33 = (bf16[768,512]{1,0:T(8,128)(2,1)}, bf16[768,512]{1,0:T(8,128)(2,1)S(1)}, u32[]{:S(2)}, u32[]{:S(2)}) collective-permute-start(bf16[768,512]{1,0:T(8,128)(2,1)} %side_step.43), channel_id=1, source_target_pairs={{0,1},{1,0},{2,3},{3,2},{4,5},{5,4},{6,7},{7,6},{8,9},{9,8},{10,11... | collective-permute-start | bytes 2359304 | tf_op jit(solution)/shard_map/ppermute | solution.py:333
  215.1 30.2 %collective-permute-start.34 = (bf16[576,768]{1,0:T(8,128)(2,1)}, bf16[576,768]{1,0:T(8,128)(2,1)}, u32[]{:S(2)}, u32[]{:S(2)}) collective-permute-start(bf16[576,768]{1,0:T(8,128)(2,1)} %get-tuple-element.352), channel_id=1, source_target_pairs={{0,2},{1,3},{2,0},{3,1},{4,6},{5,7},{6,4},{7,5},{8,10},{9,11},{10,... | collective-permute-start | bytes 2654216 | tf_op jit(solution)/shard_map/ppermute | solution.py:345
  219.0 27.0 %collective-permute-start.35 = (bf16[576,768]{1,0:T(8,128)(2,1)}, bf16[576,768]{1,0:T(8,128)(2,1)}, u32[]{:S(2)}, u32[]{:S(2)}) collective-permute-start(bf16[576,768]{1,0:T(8,128)(2,1)} %get-tuple-element.353), channel_id=1, source_target_pairs={{0,8},{1,9},{2,4},{3,5},{4,2},{5,3},{6,14},{7,15},{8,0},{9,1},{10,... | collective-permute-start | bytes 2654216 | tf_op jit(solution)/shard_map/ppermute | solution.py:345
  226.4 28.9 %collective-permute-start.36 = (bf16[768,512]{1,0:T(8,128)(2,1)}, bf16[768,512]{1,0:T(8,128)(2,1)S(1)}, u32[]{:S(2)}, u32[]{:S(2)}) collective-permute-start(bf16[768,512]{1,0:T(8,128)(2,1)} %get-tuple-element.362), channel_id=1, source_target_pairs={{0,1},{1,0},{2,3},{3,2},{4,5},{5,4},{6,7},{7,6},{8,9},{9,8},{10,11... | collective-permute-start | bytes 2359304 | tf_op jit(solution)/shard_map/ppermute | solution.py:333
  234.9 29.4 %collective-permute-start.37 = (bf16[576,768]{1,0:T(8,128)(2,1)}, bf16[576,768]{1,0:T(8,128)(2,1)}, u32[]{:S(2)}, u32[]{:S(2)}) collective-permute-start(bf16[576,768]{1,0:T(8,128)(2,1)} %get-tuple-element.363), channel_id=1, source_target_pairs={{0,2},{1,3},{2,0},{3,1},{4,6},{5,7},{6,4},{7,5},{8,10},{9,11},{10,... | collective-permute-start | bytes 2654216 | tf_op jit(solution)/shard_map/ppermute | solution.py:345
  236.6 27.7 %collective-permute-start.38 = (bf16[576,768]{1,0:T(8,128)(2,1)}, bf16[576,768]{1,0:T(8,128)(2,1)}, u32[]{:S(2)}, u32[]{:S(2)}) collective-permute-start(bf16[576,768]{1,0:T(8,128)(2,1)} %get-tuple-element.364), channel_id=1, source_target_pairs={{0,8},{1,9},{2,4},{3,5},{4,2},{5,3},{6,14},{7,15},{8,0},{9,1},{10,... | collective-permute-start | bytes 2654216 | tf_op jit(solution)/shard_map/ppermute | solution.py:345
  245.3 29.0 %collective-permute-start.39 = (bf16[768,512]{1,0:T(8,128)(2,1)}, bf16[768,512]{1,0:T(8,128)(2,1)S(1)}, u32[]{:S(2)}, u32[]{:S(2)}) collective-permute-start(bf16[768,512]{1,0:T(8,128)(2,1)} %side_step.45), channel_id=1, source_target_pairs={{0,1},{1,0},{2,3},{3,2},{4,5},{5,4},{6,7},{7,6},{8,9},{9,8},{10,11... | collective-permute-start | bytes 2359304 | tf_op jit(solution)/shard_map/ppermute | solution.py:333
  252.5 30.8 %collective-permute-start.40 = (bf16[576,768]{1,0:T(8,128)(2,1)}, bf16[576,768]{1,0:T(8,128)(2,1)}, u32[]{:S(2)}, u32[]{:S(2)}) collective-permute-start(bf16[576,768]{1,0:T(8,128)(2,1)} %get-tuple-element.371), channel_id=1, source_target_pairs={{0,2},{1,3},{2,0},{3,1},{4,6},{5,7},{6,4},{7,5},{8,10},{9,11},{10,... | collective-permute-start | bytes 2654216 | tf_op jit(solution)/shard_map/ppermute | solution.py:345
  255.3 28.6 %collective-permute-start.41 = (bf16[576,768]{1,0:T(8,128)(2,1)}, bf16[576,768]{1,0:T(8,128)(2,1)}, u32[]{:S(2)}, u32[]{:S(2)}) collective-permute-start(bf16[576,768]{1,0:T(8,128)(2,1)} %get-tuple-element.372), channel_id=1, source_target_pairs={{0,8},{1,9},{2,4},{3,5},{4,2},{5,3},{6,14},{7,15},{8,0},{9,1},{10,... | collective-permute-start | bytes 2654216 | tf_op jit(solution)/shard_map/ppermute | solution.py:345
  264.3 29.0 %collective-permute-start.42 = (bf16[768,512]{1,0:T(8,128)(2,1)}, bf16[768,512]{1,0:T(8,128)(2,1)S(1)}, u32[]{:S(2)}, u32[]{:S(2)}) collective-permute-start(bf16[768,512]{1,0:T(8,128)(2,1)} %get-tuple-element.381), channel_id=1, source_target_pairs={{0,1},{1,0},{2,3},{3,2},{4,5},{5,4},{6,7},{7,6},{8,9},{9,8},{10,11... | collective-permute-start | bytes 2359304 | tf_op jit(solution)/shard_map/ppermute | solution.py:333
  270.8 31.4 %collective-permute-start.43 = (bf16[576,768]{1,0:T(8,128)(2,1)}, bf16[576,768]{1,0:T(8,128)(2,1)}, u32[]{:S(2)}, u32[]{:S(2)}) collective-permute-start(bf16[576,768]{1,0:T(8,128)(2,1)} %get-tuple-element.382), channel_id=1, source_target_pairs={{0,2},{1,3},{2,0},{3,1},{4,6},{5,7},{6,4},{7,5},{8,10},{9,11},{10,... | collective-permute-start | bytes 2654216 | tf_op jit(solution)/shard_map/ppermute | solution.py:345
  274.3 29.2 %collective-permute-start.44 = (bf16[576,768]{1,0:T(8,128)(2,1)}, bf16[576,768]{1,0:T(8,128)(2,1)}, u32[]{:S(2)}, u32[]{:S(2)}) collective-permute-start(bf16[576,768]{1,0:T(8,128)(2,1)} %get-tuple-element.383), channel_id=1, source_target_pairs={{0,8},{1,9},{2,4},{3,5},{4,2},{5,3},{6,14},{7,15},{8,0},{9,1},{10,... | collective-permute-start | bytes 2654216 | tf_op jit(solution)/shard_map/ppermute | solution.py:345
  283.2 29.0 %collective-permute-start.45 = (bf16[768,512]{1,0:T(8,128)(2,1)}, bf16[768,512]{1,0:T(8,128)(2,1)S(1)}, u32[]{:S(2)}, u32[]{:S(2)}) collective-permute-start(bf16[768,512]{1,0:T(8,128)(2,1)} %side_step.47), channel_id=1, source_target_pairs={{0,1},{1,0},{2,3},{3,2},{4,5},{5,4},{6,7},{7,6},{8,9},{9,8},{10,11... | collective-permute-start | bytes 2359304 | tf_op jit(solution)/shard_map/ppermute | solution.py:333
  290.3 30.8 %collective-permute-start.46 = (bf16[576,768]{1,0:T(8,128)(2,1)}, bf16[576,768]{1,0:T(8,128)(2,1)}, u32[]{:S(2)}, u32[]{:S(2)}) collective-permute-start(bf16[576,768]{1,0:T(8,128)(2,1)} %get-tuple-element.390), channel_id=1, source_target_pairs={{0,2},{1,3},{2,0},{3,1},{4,6},{5,7},{6,4},{7,5},{8,10},{9,11},{10,... | collective-permute-start | bytes 2654216 | tf_op jit(solution)/shard_map/ppermute | solution.py:345
  293.2 27.9 %collective-permute-start.47 = (bf16[576,768]{1,0:T(8,128)(2,1)}, bf16[576,768]{1,0:T(8,128)(2,1)}, u32[]{:S(2)}, u32[]{:S(2)}) collective-permute-start(bf16[576,768]{1,0:T(8,128)(2,1)} %get-tuple-element.391), channel_id=1, source_target_pairs={{0,8},{1,9},{2,4},{3,5},{4,2},{5,3},{6,14},{7,15},{8,0},{9,1},{10,... | collective-permute-start | bytes 2654216 | tf_op jit(solution)/shard_map/ppermute | solution.py:345
  302.2 29.0 %collective-permute-start.48 = (bf16[768,512]{1,0:T(8,128)(2,1)}, bf16[768,512]{1,0:T(8,128)(2,1)S(1)}, u32[]{:S(2)}, u32[]{:S(2)}) collective-permute-start(bf16[768,512]{1,0:T(8,128)(2,1)} %get-tuple-element.400), channel_id=1, source_target_pairs={{0,1},{1,0},{2,3},{3,2},{4,5},{5,4},{6,7},{7,6},{8,9},{9,8},{10,11... | collective-permute-start | bytes 2359304 | tf_op jit(solution)/shard_map/ppermute | solution.py:333
  310.0 30.1 %collective-permute-start.49 = (bf16[576,768]{1,0:T(8,128)(2,1)}, bf16[576,768]{1,0:T(8,128)(2,1)}, u32[]{:S(2)}, u32[]{:S(2)}) collective-permute-start(bf16[576,768]{1,0:T(8,128)(2,1)} %get-tuple-element.401), channel_id=1, source_target_pairs={{0,2},{1,3},{2,0},{3,1},{4,6},{5,7},{6,4},{7,5},{8,10},{9,11},{10,... | collective-permute-start | bytes 2654216 | tf_op jit(solution)/shard_map/ppermute | solution.py:345
  312.2 29.3 %collective-permute-start.50 = (bf16[576,768]{1,0:T(8,128)(2,1)}, bf16[576,768]{1,0:T(8,128)(2,1)}, u32[]{:S(2)}, u32[]{:S(2)}) collective-permute-start(bf16[576,768]{1,0:T(8,128)(2,1)} %get-tuple-element.402), channel_id=1, source_target_pairs={{0,8},{1,9},{2,4},{3,5},{4,2},{5,3},{6,14},{7,15},{8,0},{9,1},{10,... | collective-permute-start | bytes 2654216 | tf_op jit(solution)/shard_map/ppermute | solution.py:345
  321.2 29.0 %collective-permute-start.51 = (bf16[768,512]{1,0:T(8,128)(2,1)}, bf16[768,512]{1,0:T(8,128)(2,1)S(1)}, u32[]{:S(2)}, u32[]{:S(2)}) collective-permute-start(bf16[768,512]{1,0:T(8,128)(2,1)} %side_step.49), channel_id=1, source_target_pairs={{0,1},{1,0},{2,3},{3,2},{4,5},{5,4},{6,7},{7,6},{8,9},{9,8},{10,11... | collective-permute-start | bytes 2359304 | tf_op jit(solution)/shard_map/ppermute | solution.py:333
  327.6 31.4 %collective-permute-start.52 = (bf16[576,768]{1,0:T(8,128)(2,1)}, bf16[576,768]{1,0:T(8,128)(2,1)}, u32[]{:S(2)}, u32[]{:S(2)}) collective-permute-start(bf16[576,768]{1,0:T(8,128)(2,1)} %get-tuple-element.409), channel_id=1, source_target_pairs={{0,2},{1,3},{2,0},{3,1},{4,6},{5,7},{6,4},{7,5},{8,10},{9,11},{10,... | collective-permute-start | bytes 2654216 | tf_op jit(solution)/shard_map/ppermute | solution.py:345
  331.2 27.9 %collective-permute-start.53 = (bf16[576,768]{1,0:T(8,128)(2,1)}, bf16[576,768]{1,0:T(8,128)(2,1)}, u32[]{:S(2)}, u32[]{:S(2)}) collective-permute-start(bf16[576,768]{1,0:T(8,128)(2,1)} %get-tuple-element.410), channel_id=1, source_target_pairs={{0,8},{1,9},{2,4},{3,5},{4,2},{5,3},{6,14},{7,15},{8,0},{9,1},{10,... | collective-permute-start | bytes 2654216 | tf_op jit(solution)/shard_map/ppermute | solution.py:345
  340.1 29.0 %collective-permute-start.54 = (bf16[768,512]{1,0:T(8,128)(2,1)}, bf16[768,512]{1,0:T(8,128)(2,1)S(1)}, u32[]{:S(2)}, u32[]{:S(2)}) collective-permute-start(bf16[768,512]{1,0:T(8,128)(2,1)} %get-tuple-element.419), channel_id=1, source_target_pairs={{0,1},{1,0},{2,3},{3,2},{4,5},{5,4},{6,7},{7,6},{8,9},{9,8},{10,11... | collective-permute-start | bytes 2359304 | tf_op jit(solution)/shard_map/ppermute | solution.py:333
  348.1 29.9 %collective-permute-start.55 = (bf16[576,768]{1,0:T(8,128)(2,1)}, bf16[576,768]{1,0:T(8,128)(2,1)}, u32[]{:S(2)}, u32[]{:S(2)}) collective-permute-start(bf16[576,768]{1,0:T(8,128)(2,1)} %get-tuple-element.420), channel_id=1, source_target_pairs={{0,2},{1,3},{2,0},{3,1},{4,6},{5,7},{6,4},{7,5},{8,10},{9,11},{10,... | collective-permute-start | bytes 2654216 | tf_op jit(solution)/shard_map/ppermute | solution.py:345
  350.2 29.3 %collective-permute-start.56 = (bf16[576,768]{1,0:T(8,128)(2,1)}, bf16[576,768]{1,0:T(8,128)(2,1)}, u32[]{:S(2)}, u32[]{:S(2)}) collective-permute-start(bf16[576,768]{1,0:T(8,128)(2,1)} %get-tuple-element.421), channel_id=1, source_target_pairs={{0,8},{1,9},{2,4},{3,5},{4,2},{5,3},{6,14},{7,15},{8,0},{9,1},{10,... | collective-permute-start | bytes 2654216 | tf_op jit(solution)/shard_map/ppermute | solution.py:345
  359.1 29.0 %collective-permute-start.57 = (bf16[768,512]{1,0:T(8,128)(2,1)}, bf16[768,512]{1,0:T(8,128)(2,1)}, u32[]{:S(2)}, u32[]{:S(2)}) collective-permute-start(bf16[768,512]{1,0:T(8,128)(2,1)} %side_step.51), channel_id=1, source_target_pairs={{0,1},{1,0},{2,3},{3,2},{4,5},{5,4},{6,7},{7,6},{8,9},{9,8},{10,11... | collective-permute-start | bytes 2359304 | tf_op jit(solution)/shard_map/ppermute | solution.py:333
  365.6 31.4 %collective-permute-start.58 = (bf16[576,768]{1,0:T(8,128)(2,1)}, bf16[576,768]{1,0:T(8,128)(2,1)}, u32[]{:S(2)}, u32[]{:S(2)}) collective-permute-start(bf16[576,768]{1,0:T(8,128)(2,1)} %get-tuple-element.428), channel_id=1, source_target_pairs={{0,2},{1,3},{2,0},{3,1},{4,6},{5,7},{6,4},{7,5},{8,10},{9,11},{10,... | collective-permute-start | bytes 2654216 | tf_op jit(solution)/shard_map/ppermute | solution.py:345
  369.1 27.9 %collective-permute-start.59 = (bf16[576,768]{1,0:T(8,128)(2,1)}, bf16[576,768]{1,0:T(8,128)(2,1)}, u32[]{:S(2)}, u32[]{:S(2)}) collective-permute-start(bf16[576,768]{1,0:T(8,128)(2,1)} %get-tuple-element.429), channel_id=1, source_target_pairs={{0,8},{1,9},{2,4},{3,5},{4,2},{5,3},{6,14},{7,15},{8,0},{9,1},{10,... | collective-permute-start | bytes 2654216 | tf_op jit(solution)/shard_map/ppermute | solution.py:345
  378.0 28.9 %collective-permute-start.60 = (bf16[768,512]{1,0:T(8,128)(2,1)}, bf16[768,512]{1,0:T(8,128)(2,1)S(1)}, u32[]{:S(2)}, u32[]{:S(2)}) collective-permute-start(bf16[768,512]{1,0:T(8,128)(2,1)} %get-tuple-element.438), channel_id=1, source_target_pairs={{0,1},{1,0},{2,3},{3,2},{4,5},{5,4},{6,7},{7,6},{8,9},{9,8},{10,11... | collective-permute-start | bytes 2359304 | tf_op jit(solution)/shard_map/ppermute | solution.py:333
  386.0 31.0 %collective-permute-start.61 = (bf16[576,768]{1,0:T(8,128)(2,1)}, bf16[576,768]{1,0:T(8,128)(2,1)}, u32[]{:S(2)}, u32[]{:S(2)}) collective-permute-start(bf16[576,768]{1,0:T(8,128)(2,1)} %get-tuple-element.439), channel_id=1, source_target_pairs={{0,2},{1,3},{2,0},{3,1},{4,6},{5,7},{6,4},{7,5},{8,10},{9,11},{10,... | collective-permute-start | bytes 2654216 | tf_op jit(solution)/shard_map/ppermute | solution.py:345
  388.1 28.9 %collective-permute-start.62 = (bf16[576,768]{1,0:T(8,128)(2,1)}, bf16[576,768]{1,0:T(8,128)(2,1)}, u32[]{:S(2)}, u32[]{:S(2)}) collective-permute-start(bf16[576,768]{1,0:T(8,128)(2,1)} %get-tuple-element.440), channel_id=1, source_target_pairs={{0,8},{1,9},{2,4},{3,5},{4,2},{5,3},{6,14},{7,15},{8,0},{9,1},{10,... | collective-permute-start | bytes 2654216 | tf_op jit(solution)/shard_map/ppermute | solution.py:345
  403.5 31.4 %collective-permute-start.64 = (bf16[576,768]{1,0:T(8,128)(2,1)}, bf16[576,768]{1,0:T(8,128)(2,1)}, u32[]{:S(2)}, u32[]{:S(2)}) collective-permute-start(bf16[576,768]{1,0:T(8,128)(2,1)} %get-tuple-element.447), channel_id=1, source_target_pairs={{0,2},{1,3},{2,0},{3,1},{4,6},{5,7},{6,4},{7,5},{8,10},{9,11},{10,... | collective-permute-start | bytes 2654216 | tf_op jit(solution)/shard_map/ppermute | solution.py:345
  407.0 27.9 %collective-permute-start.65 = (bf16[576,768]{1,0:T(8,128)(2,1)}, bf16[576,768]{1,0:T(8,128)(2,1)}, u32[]{:S(2)}, u32[]{:S(2)}) collective-permute-start(bf16[576,768]{1,0:T(8,128)(2,1)} %get-tuple-element.448), channel_id=1, source_target_pairs={{0,8},{1,9},{2,4},{3,5},{4,2},{5,3},{6,14},{7,15},{8,0},{9,1},{10,... | collective-permute-start | bytes 2654216 | tf_op jit(solution)/shard_map/ppermute | solution.py:345
  407.0 22.7 %collective-permute-start.63 = (bf16[768,512]{1,0:T(8,128)(2,1)}, bf16[768,512]{1,0:T(8,128)(2,1)S(1)}, u32[]{:S(2)}, u32[]{:S(2)}) collective-permute-start(bf16[768,512]{1,0:T(8,128)(2,1)} %side_step.53), channel_id=1, source_target_pairs={{0,1},{1,0},{2,3},{3,2},{4,5},{5,4},{6,7},{7,6},{8,9},{9,8},{10,11... | collective-permute-start | bytes 2359304 | tf_op jit(solution)/shard_map/ppermute | solution.py:333
  423.6 30.3 %collective-permute-start.66 = (bf16[576,768]{1,0:T(8,128)(2,1)}, bf16[576,768]{1,0:T(8,128)(2,1)}, u32[]{:S(2)}, u32[]{:S(2)}) collective-permute-start(bf16[576,768]{1,0:T(8,128)(2,1)} %get-tuple-element.457), channel_id=1, source_target_pairs={{0,2},{1,3},{2,0},{3,1},{4,6},{5,7},{6,4},{7,5},{8,10},{9,11},{10,... | collective-permute-start | bytes 2654216 | tf_op jit(solution)/shard_map/ppermute | solution.py:345
  426.1 27.8 %collective-permute-start.67 = (bf16[576,768]{1,0:T(8,128)(2,1)}, bf16[576,768]{1,0:T(8,128)(2,1)}, u32[]{:S(2)}, u32[]{:S(2)}) collective-permute-start(bf16[576,768]{1,0:T(8,128)(2,1)} %get-tuple-element.458), channel_id=1, source_target_pairs={{0,8},{1,9},{2,4},{3,5},{4,2},{5,3},{6,14},{7,15},{8,0},{9,1},{10,... | collective-permute-start | bytes 2654216 | tf_op jit(solution)/shard_map/ppermute | solution.py:345
  441.4 31.4 %collective-permute-start.68 = (bf16[576,768]{1,0:T(8,128)(2,1)}, bf16[576,768]{1,0:T(8,128)(2,1)S(1)}, u32[]{:S(2)}, u32[]{:S(2)}) collective-permute-start(bf16[576,768]{1,0:T(8,128)(2,1)} %get-tuple-element.464), channel_id=1, source_target_pairs={{0,2},{1,3},{2,0},{3,1},{4,6},{5,7},{6,4},{7,5},{8,10},{9,11},{10,... | collective-permute-start | bytes 2654216 | tf_op jit(solution)/shard_map/ppermute | solution.py:345
  444.9 27.8 %collective-permute-start.69 = (bf16[576,768]{1,0:T(8,128)(2,1)}, bf16[576,768]{1,0:T(8,128)(2,1)}, u32[]{:S(2)}, u32[]{:S(2)}) collective-permute-start(bf16[576,768]{1,0:T(8,128)(2,1)} %get-tuple-element.465), channel_id=1, source_target_pairs={{0,8},{1,9},{2,4},{3,5},{4,2},{5,3},{6,14},{7,15},{8,0},{9,1},{10,... | collective-permute-start | bytes 2654216 | tf_op jit(solution)/shard_map/ppermute | solution.py:345
  460.4 39.6 %collective-permute-start.72 = (bf16[576,768]{1,0:T(8,128)(2,1)}, bf16[576,768]{1,0:T(8,128)(2,1)}, u32[]{:S(2)}, u32[]{:S(2)}) collective-permute-start(bf16[576,768]{1,0:T(8,128)(2,1)} %get-tuple-element.476), channel_id=1, source_target_pairs={{0,2},{1,3},{2,0},{3,1},{4,6},{5,7},{6,4},{7,5},{8,10},{9,11},{10,... | collective-permute-start | bytes 2654216 | tf_op jit(solution)/shard_map/ppermute | solution.py:345
  463.8 36.1 %collective-permute-start.73 = (bf16[576,768]{1,0:T(8,128)(2,1)}, bf16[576,768]{1,0:T(8,128)(2,1)}, u32[]{:S(2)}, u32[]{:S(2)}) collective-permute-start(bf16[576,768]{1,0:T(8,128)(2,1)} %get-tuple-element.477), channel_id=1, source_target_pairs={{0,8},{1,9},{2,4},{3,5},{4,2},{5,3},{6,14},{7,15},{8,0},{9,1},{10,... | collective-permute-start | bytes 2654216 | tf_op jit(solution)/shard_map/ppermute | solution.py:345
  480.2 32.1 %collective-permute-start.74 = (bf16[576,768]{1,0:T(8,128)(2,1)}, bf16[576,768]{1,0:T(8,128)(2,1)}, u32[]{:S(2)}, u32[]{:S(2)}) collective-permute-start(bf16[576,768]{1,0:T(8,128)(2,1)} %get-tuple-element.483), channel_id=1, source_target_pairs={{0,2},{1,3},{2,0},{3,1},{4,6},{5,7},{6,4},{7,5},{8,10},{9,11},{10,... | collective-permute-start | bytes 2654216 | tf_op jit(solution)/shard_map/ppermute | solution.py:345
  482.8 29.4 %collective-permute-start.75 = (bf16[576,768]{1,0:T(8,128)(2,1)}, bf16[576,768]{1,0:T(8,128)(2,1)}, u32[]{:S(2)}, u32[]{:S(2)}) collective-permute-start(bf16[576,768]{1,0:T(8,128)(2,1)} %get-tuple-element.484), channel_id=1, source_target_pairs={{0,8},{1,9},{2,4},{3,5},{4,2},{5,3},{6,14},{7,15},{8,0},{9,1},{10,... | collective-permute-start | bytes 2654216 | tf_op jit(solution)/shard_map/ppermute | solution.py:345
  506.6 31.5 %collective-permute-start.78 = (bf16[576,768]{1,0:T(8,128)(2,1)}, bf16[576,768]{1,0:T(8,128)(2,1)}, u32[]{:S(2)}, u32[]{:S(2)}) collective-permute-start(bf16[576,768]{1,0:T(8,128)(2,1)} %get-tuple-element.493), channel_id=1, source_target_pairs={{0,2},{1,3},{2,0},{3,1},{4,6},{5,7},{6,4},{7,5},{8,10},{9,11},{10,... | collective-permute-start | bytes 2654216 | tf_op jit(solution)/shard_map/ppermute | solution.py:345
  506.7 31.4 %collective-permute-start.79 = (bf16[576,768]{1,0:T(8,128)(2,1)}, bf16[576,768]{1,0:T(8,128)(2,1)}, u32[]{:S(2)}, u32[]{:S(2)}) collective-permute-start(bf16[576,768]{1,0:T(8,128)(2,1)} %get-tuple-element.494), channel_id=1, source_target_pairs={{0,8},{1,9},{2,4},{3,5},{4,2},{5,3},{6,14},{7,15},{8,0},{9,1},{10,... | collective-permute-start | bytes 2654216 | tf_op jit(solution)/shard_map/ppermute | solution.py:345
  518.9 29.6 %collective-permute-start.82 = (bf16[576,768]{1,0:T(8,128)(2,1)}, bf16[576,768]{1,0:T(8,128)(2,1)}, u32[]{:S(2)}, u32[]{:S(2)}) collective-permute-start(bf16[576,768]{1,0:T(8,128)(2,1)} %get-tuple-element.497), channel_id=1, source_target_pairs={{0,2},{1,3},{2,0},{3,1},{4,6},{5,7},{6,4},{7,5},{8,10},{9,11},{10,... | collective-permute-start | bytes 2654216 | tf_op jit(solution)/shard_map/ppermute | solution.py:345
  522.2 26.2 %collective-permute-start.83 = (bf16[576,768]{1,0:T(8,128)(2,1)}, bf16[576,768]{1,0:T(8,128)(2,1)}, u32[]{:S(2)}, u32[]{:S(2)}) collective-permute-start(bf16[576,768]{1,0:T(8,128)(2,1)} %get-tuple-element.498), channel_id=1, source_target_pairs={{0,8},{1,9},{2,4},{3,5},{4,2},{5,3},{6,14},{7,15},{8,0},{9,1},{10,... | collective-permute-start | bytes 2654216 | tf_op jit(solution)/shard_map/ppermute | solution.py:345
  (83 other events, 1018.0 us)

commit v3 on v2

--- a/solution.py
+++ b/solution.py
@@ -9,7 +9,7 @@
 
 WIDTH = 256
 HOP = 2
-AHEAD = 3
+AHEAD = 2
 BATCH = 2
 VMEM = 62 * 1024 * 1024
 
@@ -47,7 +47,8 @@
     take = taker(refs)
     (info,) = take()
     if sums:
-        gate, up, toks = take(3)
+        gate, up = take(2)
+        toks = take(across)
         got = [take(across - 1) for _ in range(deep)]
     came = take(2) if sums_in or back_in else None
     sent = take(2)
@@ -78,14 +79,18 @@
             waits[s].append(pltpu.make_async_copy(came[0], came_v.at[s], came_sem.at[s]))
     if sums:
         part_rows = gate.shape[0] // across
-        tok_copies = [
-            begin(
-                toks.at[:, pl.ds(s * half, half)],
-                toks_v.at[:, pl.ds(s * half, half)],
-                tok_sem.at[s],
-            )
-            for s in (1, 0)
-        ][::-1]
+        group_rows, feat = toks[0].shape[0], gate.shape[1]
+        tok_copies = [[], []]
+        for i in list(range(across // 2, across)) + list(range(across // 2)):
+            for j in range(across):
+                column = pl.multiple_of(jnp.bitwise_xor(info[1], j) * feat, 128)
+                tok_copies[i // (across // 2)].append(
+                    begin(
+                        toks[i].at[:, pl.ds(column, feat)],
+                        toks_v.at[j, pl.ds(i * group_rows, group_rows)],
+                        tok_sem.at[i, j],
+                    )
+                )
         for s in range(2):
             own = info[1] * part_rows + info[2 + s]
             for k, ref in enumerate((gate, up)):
@@ -116,7 +121,8 @@
         if not sums:
             continue
         mine = 1 - s
-        tok_copies[mine].wait()
+        for copy in tok_copies[mine]:
+            copy.wait()
         total = None
         for j in range(across):
             term = lax.dot_general(
@@ -382,7 +388,6 @@
     weights = (gate_weight, up_weight, down_weight)
     early = min(ahead, n_chunks)
     firsts = [lay_out(k, weights) for k in range(early)]
-    firsts[0], tokens = lax.optimization_barrier((firsts[0], tokens))
     hand_over(0, firsts[0])
 
     picked = routes == expert
@@ -397,13 +402,7 @@
     token_ids = jnp.arange(tok_rows, dtype=jnp.int32)
     came_from = jnp.sum(jnp.where(placed, token_ids[:, None] + 1, 0), axis=0)
     weight = jnp.sum(jnp.where(placed, token_weight[:, None], 0.0), axis=0)
-    high = lax.reduce_precision(weight, 8, 7)
-    middle = lax.reduce_precision(weight - high, 8, 7)
-    low = weight - high - middle
-    notes = jnp.stack(
-        [(came_from // 128).astype(f32), (came_from % 128).astype(f32), high, middle, low], axis=1
-    ).astype(bf)
-    notes = jnp.pad(notes, ((0, 0), (0, 128 - notes.shape[1])))
+    notes = jnp.stack([came_from.astype(f32), weight])
 
     def pick(array, index):
         return lax.dynamic_index_in_dim(array, index, 0, keepdims=False)
@@ -413,23 +412,18 @@
 
     pieces = []
     for k in range(deep):
-        piece = jnp.concatenate([columns(packed, z ^ k, across * feat), notes], axis=1)
+        piece = columns(packed, z ^ k, across * feat)
         pieces.append(swap(piece, k, 0) if k else piece)
     pieces = jnp.stack(pieces)
     mine = jnp.concatenate([pick(pieces, z ^ a) for a in range(deep)])
-    mine, got[0] = lax.optimization_barrier((mine, got[0]))
+    mine, notes, ready = lax.optimization_barrier((mine, notes, {k: got[k] for k in got}))
+    got.update(ready)
+    notes = jnp.stack([swap(notes, k, 0) if k else notes for k in range(deep)])
+    notes = jnp.stack([pick(notes, z ^ a) for a in range(deep)])
     by_group = [swap(mine, 0, i) if i else mine for i in range(across)]
-    by_group, firsts = lax.optimization_barrier((by_group, firsts))
+    by_group, notes, firsts = lax.optimization_barrier((by_group, notes, firsts))
     for k in range(1, early):
         hand_over(k, firsts[k])
-    toks = jnp.stack(
-        [jnp.concatenate([columns(g, x ^ j, feat) for g in by_group]) for j in range(across)]
-    )
-    notes = jnp.concatenate([g[:, across * feat :] for g in by_group])[:, :5].astype(f32)
-    notes = notes.T.reshape(5, across * deep, capacity)
-    came_from = (notes[0] * 128.0 + notes[1]).astype(jnp.int32) - 1
-    weight = notes[2] + notes[3] + notes[4]
-
     n_steps = n_chunks + 2 * reach
     acc = jnp.zeros((total_rows, across * feat), f32)
     msgs, waiting, order = {}, [], None
@@ -450,7 +444,9 @@
         msgs[t] = (pairing(res[0], 0), pairing(res[1], 1))
         if t == n_chunks + reach - 1:
             for u in range(t + 1, n_steps - hop):
-                msgs[u] = (pairing(msgs[u - hop][1], 0), pairing(msgs[u - hop][0], 1))
+                msgs[u] = [pairing(msgs[u - hop][1], 0)] * 2
+                if u < n_steps - 2 * hop:
+                    msgs[u] = (msgs[u][0], pairing(msgs[u - hop][0], 1))
 
     def chunks(base):
         return [min(max(base - hop * i, 0), n_chunks - 1) for i in range(deep)]
@@ -480,11 +476,11 @@
                 order = None
             args, outs, scratch = [info], [], []
             if sums:
-                args += [gate_weight, up_weight, toks] + [a for c in chunks(t) for a in got[c]]
+                args += [gate_weight, up_weight] + by_group + [a for c in chunks(t) for a in got[c]]
                 scratch += [
                     pltpu.VMEM((across, total_rows, feat), bf),
                     pltpu.VMEM((2, across, 2 * width, feat), bf),
-                    dma((2,)),
+                    dma((across, across)),
                     dma((2, across, 2)),
                 ]
             if sums_in or back_in:
@@ -512,7 +508,8 @@
         next_k = t + early
         kinds = kinds_of(next_k)
         n_send = across - 1 if kinds else 0
-        flush = (len(waiting) == batch and t < early_at) or t in (early_at, n_steps - 1)
+        flush = len(waiting) == batch and t < early_at
+        flush = flush or t in (early_at, n_steps - 1)
         steps = len(waiting) if flush else 0
         if not steps and not n_send:
             if sums:
@@ -528,13 +525,20 @@
         if n_send:
             entries += send_starts(next_k)
         side_info = jnp.stack([jnp.int32(e) for e in entries]).astype(jnp.int32)
-        if t == n_steps - 1:
-            side_info, early_parts = lax.optimization_barrier((side_info, early_parts))
         if sums:
             side_info, res = lax.optimization_barrier((side_info, res))
+            if t == n_chunks + 2:
+                notes, res = lax.optimization_barrier((notes, res))
+                notes = [swap(notes, 0, i) if i else notes for i in range(across)]
             send_on(t, res)
-        if t >= n_chunks + reach - 1 and t + 1 in msgs:
-            side_info, msgs[t + 1] = lax.optimization_barrier((side_info, msgs[t + 1]))
+        if t == n_chunks + reach - 1:
+            side_info, msgs[t + hop], got[t] = lax.optimization_barrier(
+                (side_info, msgs[t + hop], got[t])
+            )
+        elif t == early_at:
+            late = {u: m for u, m in msgs.items() if u >= n_chunks + reach}
+            side_info, notes, late = lax.optimization_barrier((side_info, notes, late))
+            msgs.update(late)
         args = [side_info]
         args += [gate_weight, up_weight, down_weight] + [h for _, hid in done for h in hid]
         offsets = []
@@ -593,6 +597,7 @@
         if t == early_at:
             early_parts = own_parts(early_half)
 
+    acc, early_parts = lax.optimization_barrier((acc, early_parts))
     late_parts = own_parts(1 - early_half)
     group_rows = total_rows // across
     whole = acc[:, :feat]
@@ -609,16 +614,26 @@
         )
         whole = whole + part.astype(f32)
     whole = whole.reshape(across * deep, capacity, feat)
-    spread = jnp.where(
-        came_from[:, None, :] == token_ids[None, :, None], weight[:, None, :], 0.0
+    notes = jnp.concatenate(notes)
+    came_from, weight = notes[:, 0].astype(jnp.int32) - 1, notes[:, 1]
+    spread = (came_from[:, None, :] == token_ids[None, :, None]).astype(bf)
+    high = lax.reduce_precision(whole, 8, 7)
+    weighted = sum(
+        lax.dot_general(
+            spread,
+            part.astype(bf),
+            (((2,), (1,)), ((0,), (0,))),
+            preferred_element_type=f32,
+        )
+        for part in (high, whole - high)
     )
-    weighted = lax.dot_general(
-        spread,
-        whole,
-        (((2,), (1,)), ((0,), (0,))),
-        precision=lax.Precision.HIGHEST,
-        preferred_element_type=f32,
-    ).reshape(across, deep, tok_rows, feat)
+    row_weight = jnp.sum(
+        jnp.where(
+            came_from[:, None, :] == token_ids[None, :, None], weight[:, None, :], 0.0
+        ),
+        axis=2,
+    )
+    weighted = (weighted * row_weight[:, :, None]).reshape(across, deep, tok_rows, feat)
     weighted = jnp.stack([pick(weighted, x ^ b) for b in range(across)], axis=1)
     share = groups // members
     left = weighted.reshape(members, share * tok_rows, feat)

time: 683 us -> 678 us (level)
  waiting for transfers between devices: 151 us -> 193 us
  starting transfers between devices: 141 us -> 111 us
  Pallas kernels: 310 us -> 302 us
    ppermute x64 -> x62, starting transfers between devices: 92.8 us -> 60.7 us  [pairing(): return lax.ppermute(array, ('member', 'fsdp'), perm)]
    ppermute x64 -> x62, waiting for transfers between devices: 47.5 us -> 68 us  [pairing(): return lax.ppermute(array, ('member', 'fsdp'), perm)]
    ppermute x34 -> x38, waiting for transfers between devices: 74.5 us -> 94.9 us  [swap(): return lax.ppermute(array, 'fsdp', perm)]
    pallas_call x60 -> x59, Pallas kernels: 310 us -> 302 us  [call(): pl.pallas_call(kernel, out_shape=outs, in_specs=[pl.BlockSpec(memory_spac...]
    ppermute x34 -> x38, starting transfers between devices: 41.5 us -> 42.5 us  [swap(): return lax.ppermute(array, 'fsdp', perm)]
  transfers between devices with their start and end apart: 102 -> 104, of which waited for: 33 -> 40; matrix products, arithmetic and copies ran while one was open for 6% -> 5% of each run, Pallas kernels for 44% -> 44%
where the time goes in v3:
time: 678 us; the launch traced here: 668 us
  Pallas kernels  302 us (45%)
  waiting for transfers between devices  193 us (28%)
  starting transfers between devices  111 us (16%)
  local copies, waits for them, and re-layouts  44.5 us (7%)
  other arithmetic  12.8 us (2%)
    pallas_call x59, Pallas kernels, call(): pl.pallas_call(kernel, out_shape=outs, in_specs=[pl.BlockSpec(memory_spac...  302 us
    ppermute x38, waiting for transfers between devices, swap(): return lax.ppermute(array, 'fsdp', perm)  94.9 us
    ppermute x62, waiting for transfers between devices, pairing(): return lax.ppermute(array, ('member', 'fsdp'), perm)  68 us
    ppermute x62, starting transfers between devices, pairing(): return lax.ppermute(array, ('member', 'fsdp'), perm)  60.7 us
    ppermute x38, starting transfers between devices, swap(): return lax.ppermute(array, 'fsdp', perm)  42.5 us
    another operation x28, local copies, waits for them, and re-layouts, body(): jnp.stack([z, x, start_of(up_c), start_of(dn_c), jnp.int32(skip)])  18.7 us
    ppermute x2, waiting for transfers between devices, body(): parts.append(lax.ppermute(pick(mixed, slot ^ j), ('member', 'fsdp'), perm))  15.3 us
    ppermute x2, waiting for transfers between devices, body(): came = lax.ppermute(give, 'member', [(m, m ^ bit) for m in range(members)])  14.4 us
  transfers between devices with their start and end apart: 104, of which 40 were waited for; matrix products, arithmetic and copies ran while one was open for 5% of the time, Pallas kernels for 44%

profile of v3, /device:TPU:4, one launch (start us, length us, event | category | flops | bytes accessed | tf_op | source)
XLA Modules:
  0.0 667.6 jit_solution(12357088176965778150)
XLA Ops:
  6.7 3.7 collective-permute-start.2
  11.5 7.1 %collective-permute-done.2 = bf16[144,1024]{1,0:T(8,128)(2,1)S(1)} collective-permute-done((bf16[144,1024]{1,0:T(8,128)(2,1)S(1)}, bf16[144,1024]{1,0:T(8,128)(2,1)S(1)}, u32[]{:S(2)}, u32[]{:S(2)}) %collective-permute-start.2) | collective-permute-done | bytes 294944 | tf_op jit(solution)/shard_map/ppermute | solution.py:339
  18.6 16.6 %collective-permute-done.1 = bf16[144,1024]{1,0:T(8,128)(2,1)S(1)} collective-permute-done((bf16[144,1024]{1,0:T(8,128)(2,1)S(1)}, bf16[144,1024]{1,0:T(8,128)(2,1)S(1)}, u32[]{:S(2)}, u32[]{:S(2)}) %collective-permute-start.1) | collective-permute-done | bytes 294944 | tf_op jit(solution)/shard_map/ppermute | solution.py:339
  44.5 18.2 %collective-permute-done.4.refs_4_ = bf16[576,1024]{1,0:T(8,128)(2,1)} collective-permute-done((bf16[576,1024]{1,0:T(8,128)(2,1)S(1)}, bf16[576,1024]{1,0:T(8,128)(2,1)}, u32[]{:S(2)}, u32[]{:S(2)}) %collective-permute-start.4) | collective-permute-done | bytes 1179680 | tf_op jit(solution)/shard_map/ppermute | solution.py:339
  64.6 5.2 chain_step.28
  77.7 5.2 chain_step.29
  88.3 5.4 chain_step.30
  102.1 5.4 chain_step.31
  115.5 5.4 chain_step.32
  127.1 5.4 chain_step.33
  139.1 5.2 collective-permute-done.21.refs_5_.refs_6_.refs_7_.refs_8_.refs_9_.refs_11_.refs_12_.refs_13_
  145.2 6.3 chain_step.34
  162.1 6.2 chain_step.35
  171.0 5.7 side_step.40
  179.3 6.2 chain_step.36
  192.1 4.5 collective-permute-done.30.refs_5_.refs_10_.refs_6_.refs_11_.refs_7_.refs_12_.refs_8_.refs_13_
  199.8 6.3 chain_step.37
  206.0 5.7 side_step.42
  217.1 6.2 chain_step.38
  232.4 4.5 collective-permute-done.37.refs_9_
  236.9 6.3 chain_step.39
  243.2 5.7 side_step.44
  255.9 6.2 chain_step.40
  268.9 5.9 collective-permute-done.43.refs_9_
  274.8 6.3 chain_step.41
  281.1 7.4 %side_step.46 = (bf16[768,512]{1,0:T(8,128)(2,1)}, f32[1152,1024]{1,0:T(8,128)}) custom-call(s32[12]{0:T(128)} %stack.1170.refs_0_, bf16[11008,512]{1,0:T(8,128)(2,1)} %bitcast.217, bf16[11008,512]{1,0:T(8,128)(2,1)} %bitcast.276, bf16[11008,512]{1,0:T(8,128)(2,1)} %bitcast.321, ...), custom_call_target="tpu_custom_call", output_to_operand_aliasing={{1}: (14, {})} | custom-call | flops 1207959552 | bytes 12582912 | tf_op jit(solution)/shard_map/side_step/pallas_call | solution.py:297
  293.7 6.2 chain_step.42
  307.1 5.5 collective-permute-done.49.refs_9_
  312.6 6.3 chain_step.43
  318.9 7.3 %side_step.48 = (bf16[768,512]{1,0:T(8,128)(2,1)}, f32[1152,1024]{1,0:T(8,128)}) custom-call(s32[12]{0:T(128)} %stack.1152.refs_0_, bf16[11008,512]{1,0:T(8,128)(2,1)} %bitcast.221, bf16[11008,512]{1,0:T(8,128)(2,1)} %bitcast.280, bf16[11008,512]{1,0:T(8,128)(2,1)} %bitcast.323, ...), custom_call_target="tpu_custom_call", output_to_operand_aliasing={{1}: (14, {})} | custom-call | flops 1207959552 | bytes 12582912 | tf_op jit(solution)/shard_map/side_step/pallas_call | solution.py:297
  331.6 6.2 chain_step.44
  345.0 5.5 collective-permute-done.55.refs_9_
  350.5 6.3 chain_step.45
  356.8 7.3 %side_step.50 = (bf16[768,512]{1,0:T(8,128)(2,1)}, f32[1152,1024]{1,0:T(8,128)}) custom-call(s32[12]{0:T(128)} %stack.1134.refs_0_, bf16[11008,512]{1,0:T(8,128)(2,1)} %bitcast.225, bf16[11008,512]{1,0:T(8,128)(2,1)} %bitcast.284, bf16[11008,512]{1,0:T(8,128)(2,1)} %bitcast.325, ...), custom_call_target="tpu_custom_call", output_to_operand_aliasing={{1}: (14, {})} | custom-call | flops 1207959552 | bytes 12582912 | tf_op jit(solution)/shard_map/side_step/pallas_call | solution.py:297
  369.5 6.2 chain_step.46
  382.8 5.7 collective-permute-done.61.refs_9_
  388.5 6.2 chain_step.47
  396.6 7.4 %side_step.52 = (bf16[768,512]{1,0:T(8,128)(2,1)}, f32[1152,1024]{1,0:T(8,128)}) custom-call(s32[12]{0:T(128)} %stack.1112.refs_0_, bf16[11008,512]{1,0:T(8,128)(2,1)} %bitcast.229, bf16[11008,512]{1,0:T(8,128)(2,1)} %bitcast.288, bf16[11008,512]{1,0:T(8,128)(2,1)} %bitcast.327, ...), custom_call_target="tpu_custom_call", output_to_operand_aliasing={{1}: (14, {})} | custom-call | flops 1207959552 | bytes 12582912 | tf_op jit(solution)/shard_map/side_step/pallas_call | solution.py:297
  407.4 6.2 chain_step.48
  419.2 5.0 collective-permute-done.66.refs_5_.refs_10_.refs_6_.refs_11_.refs_7_.refs_12_.refs_8_.refs_13_
  426.4 6.2 chain_step.49
  435.1 7.2 %side_step.54 = (bf16[256,512]{1,0:T(8,128)(2,1)}, f32[1152,1024]{1,0:T(8,128)}) custom-call(s32[12]{0:T(128)} %stack.1090.refs_0_, bf16[11008,512]{1,0:T(8,128)(2,1)} %bitcast.233, bf16[11008,512]{1,0:T(8,128)(2,1)} %bitcast.292, bf16[11008,512]{1,0:T(8,128)(2,1)} %bitcast.329, ...), custom_call_target="tpu_custom_call", output_to_operand_aliasing={{1}: (14, {})} | custom-call | flops 1207959552 | bytes 12582912 | tf_op jit(solution)/shard_map/side_step/pallas_call | solution.py:297
  445.3 6.2 chain_step.50
  458.4 5.8 collective-permute-done.71.refs_9_
  465.1 6.3 chain_step.51
  474.6 7.4 %collective-permute-done.74.refs_10_.refs_11_.refs_12_.refs_15_ = bf16[256,512]{1,0:T(8,128)(2,1)S(1)} collective-permute-done((bf16[256,512]{1,0:T(8,128)(2,1)S(1)}, bf16[256,512]{1,0:T(8,128)(2,1)S(1)}, u32[]{:S(2)}, u32[]{:S(2)}) %collective-permute-start.74) | collective-permute-done | bytes 262176 | tf_op jit(solution)/shard_map/ppermute | solution.py:339
  482.7 7.3 %side_step.56 = (bf16[256,512]{1,0:T(8,128)(2,1)}, f32[1152,1024]{1,0:T(8,128)}) custom-call(s32[12]{0:T(128)} %stack.1072.refs_0_, bf16[11008,512]{1,0:T(8,128)(2,1)} %bitcast.237, bf16[11008,512]{1,0:T(8,128)(2,1)} %bitcast.296, bf16[11008,512]{1,0:T(8,128)(2,1)} %bitcast.331, ...), custom_call_target="tpu_custom_call", output_to_operand_aliasing={{1}: (14, {})} | custom-call | flops 1207959552 | bytes 12582912 | tf_op jit(solution)/shard_map/side_step/pallas_call | solution.py:297
  490.0 6.3 chain_step.52
  500.9 6.3 chain_step.53
  512.4 6.9 %collective-permute-done.81.refs_10_.refs_11_.refs_14_.refs_19_ = bf16[256,512]{1,0:T(8,128)(2,1)S(1)} collective-permute-done((bf16[256,512]{1,0:T(8,128)(2,1)S(1)}, bf16[256,512]{1,0:T(8,128)(2,1)S(1)}, u32[]{:S(2)}, u32[]{:S(2)}) %collective-permute-start.81) | collective-permute-done | bytes 262176 | tf_op jit(solution)/shard_map/ppermute | solution.py:339
  520.1 7.2 %side_step.58 = (bf16[256,512]{1,0:T(8,128)(2,1)}, f32[1152,1024]{1,0:T(8,128)}) custom-call(s32[12]{0:T(128)} %stack.1252.refs_0_, bf16[11008,512]{1,0:T(8,128)(2,1)} %bitcast.241, bf16[11008,512]{1,0:T(8,128)(2,1)} %bitcast.300, bf16[11008,512]{1,0:T(8,128)(2,1)} %bitcast.333, ...), custom_call_target="tpu_custom_call", output_to_operand_aliasing={{1}: (14, {})} | custom-call | flops 1207959552 | bytes 12582912 | tf_op jit(solution)/shard_map/side_step/pallas_call | solution.py:297
  527.3 5.8 chain_step.54
  538.2 5.8 chain_step.55
  546.7 5.7 collective-permute-done.92.refs_6_
  569.2 6.4 side_step.59.refs_16_
  578.5 4.0 collective-permute-done.96.refs_10_.refs_11_
  582.5 5.1 side_step.60.refs_28_
  591.8 7.3 %side_step.61 = f32[1152,1024]{1,0:T(8,128)} custom-call(s32[18]{0:T(128)} %stack.1284.refs_0_, bf16[11008,512]{1,0:T(8,128)(2,1)} %bitcast.246, bf16[11008,512]{1,0:T(8,128)(2,1)} %bitcast.305, bf16[11008,512]{1,0:T(8,128)(2,1)} %bitcast.336, bf16[576,256]{1,0:T(8,128)(2,1)} %collective-permute-done.88.refs_4_, ...), custom_call_target="tpu_custom_call", output_to_operand_aliasing={{}: (28, {})} | custom-call | flops 2415919104 | bytes 12582912 | tf_op jit(solution)/shard_map/side_step/pallas_call | solution.py:297
  599.1 4.0 collective-permute-done.98
  606.9 10.4 %collective-permute-done.99 = bf16[576,512]{1,0:T(8,128)(2,1)S(1)} collective-permute-done((bf16[576,512]{1,0:T(8,128)(2,1)S(1)}, bf16[576,512]{1,0:T(8,128)(2,1)S(1)}, u32[]{:S(2)}, u32[]{:S(2)}) %collective-permute-start.99) | collective-permute-done | bytes 589856 | tf_op jit(solution)/shard_map/ppermute | solution.py:339
  633.1 10.9 %collective-permute-done.101 = bf16[1,384,512]{2,1,0:T(8,128)(2,1)S(1)} collective-permute-done((bf16[1,384,512]{2,1,0:T(8,128)(2,1)}, bf16[1,384,512]{2,1,0:T(8,128)(2,1)S(1)}, u32[]{:S(2)}, u32[]{:S(2)}) %collective-permute-start.101) | collective-permute-done | bytes 393248 | tf_op jit(solution)/shard_map/ppermute | solution.py:648
  645.3 5.8 collective-permute-start.102
  651.1 11.0 %collective-permute-done.103 = bf16[192,512]{1,0:T(8,128)(2,1)S(1)} collective-permute-done((bf16[192,512]{1,0:T(8,128)(2,1)S(1)}, bf16[192,512]{1,0:T(8,128)(2,1)S(1)}, u32[]{:S(2)}, u32[]{:S(2)}) %collective-permute-start.103) | collective-permute-done | bytes 196640 | tf_op jit(solution)/shard_map/ppermute | solution.py:660
  662.1 4.3 collective-permute-done.102
  (384 shorter events, 246.8 us)
Async XLA Ops:
  3.9 31.7 %collective-permute-start.3 = (bf16[512,512]{1,0:T(8,128)(2,1)}, bf16[512,512]{1,0:T(8,128)(2,1)}, u32[]{:S(2)}, u32[]{:S(2)}) collective-permute-start(bf16[512,512]{1,0:T(8,128)(2,1)} %side_step.31), channel_id=1, source_target_pairs={{0,1},{1,0},{2,3},{3,2},{4,5},{5,4},{6,7},{7,6},{8,9},{9,8},{10,11... | collective-permute-start | bytes 1572872 | tf_op jit(solution)/shard_map/ppermute | solution.py:339
  10.4 24.8 %collective-permute-start.1 = (bf16[144,1024]{1,0:T(8,128)(2,1)S(1)}, bf16[144,1024]{1,0:T(8,128)(2,1)S(1)}, u32[]{:S(2)}, u32[]{:S(2)}) collective-permute-start(bf16[144,1024]{1,0:T(8,128)(2,1)S(1)} %get-tuple-element.561), channel_id=1, source_target_pairs={{0,4},{1,5},{2,6},{3,7},{4,0},{5,1},{6,2},{7,3},{8,12},{9,13},{10,... | collective-permute-start | bytes 884744 | tf_op jit(solution)/shard_map/ppermute | solution.py:339
  10.4 24.8 %collective-permute-start = (bf16[144,1024]{1,0:T(8,128)(2,1)S(1)}, bf16[144,1024]{1,0:T(8,128)(2,1)S(1)}, u32[]{:S(2)}, u32[]{:S(2)}) collective-permute-start(bf16[144,1024]{1,0:T(8,128)(2,1)S(1)} %get-tuple-element.562), channel_id=1, source_target_pairs={{0,2},{1,3},{2,0},{3,1},{4,6},{5,7},{6,4},{7,5},{8,10},{9,11},{10,... | collective-permute-start | bytes 884744 | tf_op jit(solution)/shard_map/ppermute | solution.py:339
  35.6 27.2 %collective-permute-start.4 = (bf16[576,1024]{1,0:T(8,128)(2,1)S(1)}, bf16[576,1024]{1,0:T(8,128)(2,1)}, u32[]{:S(2)}, u32[]{:S(2)}) collective-permute-start(bf16[576,1024]{1,0:T(8,128)(2,1)S(1)} %pad_maximum_fusion.2.refs_3_), channel_id=1, source_target_pairs={{0,1},{1,0},{2,3},{3,2},{4,5},{5,4},{6,7},{7,6},{8,9},{9,8},{10,11... | collective-permute-start | bytes 3538952 | tf_op jit(solution)/shard_map/ppermute | solution.py:339
  93.7 21.0 %collective-permute-start.16 = (bf16[576,512]{1,0:T(8,128)(2,1)}, bf16[576,512]{1,0:T(8,128)(2,1)}, u32[]{:S(2)}, u32[]{:S(2)}) collective-permute-start(bf16[576,512]{1,0:T(8,128)(2,1)} %get-tuple-element.307), channel_id=1, source_target_pairs={{0,2},{1,3},{2,0},{3,1},{4,6},{5,7},{6,4},{7,5},{8,10},{9,11},{10,... | collective-permute-start | bytes 1769480 | tf_op jit(solution)/shard_map/ppermute | solution.py:351
  94.1 20.5 %collective-permute-start.17 = (bf16[576,512]{1,0:T(8,128)(2,1)}, bf16[576,512]{1,0:T(8,128)(2,1)}, u32[]{:S(2)}, u32[]{:S(2)}) collective-permute-start(bf16[576,512]{1,0:T(8,128)(2,1)} %get-tuple-element.308), channel_id=1, source_target_pairs={{0,8},{1,9},{2,4},{3,5},{4,2},{5,3},{6,14},{7,15},{8,0},{9,1},{10,... | collective-permute-start | bytes 1769480 | tf_op jit(solution)/shard_map/ppermute | solution.py:351
  123.6 20.7 %collective-permute-start.21 = (bf16[768,512]{1,0:T(8,128)(2,1)}, bf16[768,512]{1,0:T(8,128)(2,1)S(1)}, u32[]{:S(2)}, u32[]{:S(2)}) collective-permute-start(bf16[768,512]{1,0:T(8,128)(2,1)} %side_step.37), channel_id=1, source_target_pairs={{0,1},{1,0},{2,3},{3,2},{4,5},{5,4},{6,7},{7,6},{8,9},{9,8},{10,11... | collective-permute-start | bytes 2359304 | tf_op jit(solution)/shard_map/ppermute | solution.py:339
  135.3 25.9 %collective-permute-start.24 = (bf16[768,512]{1,0:T(8,128)(2,1)}, bf16[768,512]{1,0:T(8,128)(2,1)S(1)}, u32[]{:S(2)}, u32[]{:S(2)}) collective-permute-start(bf16[768,512]{1,0:T(8,128)(2,1)} %side_step.38), channel_id=1, source_target_pairs={{0,1},{1,0},{2,3},{3,2},{4,5},{5,4},{6,7},{7,6},{8,9},{9,8},{10,11... | collective-permute-start | bytes 2359304 | tf_op jit(solution)/shard_map/ppermute | solution.py:339
  135.4 21.6 %collective-permute-start.25 = (bf16[576,512]{1,0:T(8,128)(2,1)}, bf16[576,512]{1,0:T(8,128)(2,1)}, u32[]{:S(2)}, u32[]{:S(2)}) collective-permute-start(bf16[576,512]{1,0:T(8,128)(2,1)} %get-tuple-element.329), channel_id=1, source_target_pairs={{0,2},{1,3},{2,0},{3,1},{4,6},{5,7},{6,4},{7,5},{8,10},{9,11},{10,... | collective-permute-start | bytes 1769480 | tf_op jit(solution)/shard_map/ppermute | solution.py:351
  139.1 19.2 %collective-permute-start.26 = (bf16[576,512]{1,0:T(8,128)(2,1)}, bf16[576,512]{1,0:T(8,128)(2,1)}, u32[]{:S(2)}, u32[]{:S(2)}) collective-permute-start(bf16[576,512]{1,0:T(8,128)(2,1)} %get-tuple-element.330), channel_id=1, source_target_pairs={{0,8},{1,9},{2,4},{3,5},{4,2},{5,3},{6,14},{7,15},{8,0},{9,1},{10,... | collective-permute-start | bytes 1769480 | tf_op jit(solution)/shard_map/ppermute | solution.py:351
  154.2 23.6 %collective-permute-start.27 = (bf16[768,512]{1,0:T(8,128)(2,1)}, bf16[768,512]{1,0:T(8,128)(2,1)S(1)}, u32[]{:S(2)}, u32[]{:S(2)}) collective-permute-start(bf16[768,512]{1,0:T(8,128)(2,1)} %side_step.39), channel_id=1, source_target_pairs={{0,1},{1,0},{2,3},{3,2},{4,5},{5,4},{6,7},{7,6},{8,9},{9,8},{10,11... | collective-permute-start | bytes 2359304 | tf_op jit(solution)/shard_map/ppermute | solution.py:339
  154.4 24.9 %collective-permute-start.28 = (bf16[576,768]{1,0:T(8,128)(2,1)}, bf16[576,768]{1,0:T(8,128)(2,1)}, u32[]{:S(2)}, u32[]{:S(2)}) collective-permute-start(bf16[576,768]{1,0:T(8,128)(2,1)} %get-tuple-element.339), channel_id=1, source_target_pairs={{0,2},{1,3},{2,0},{3,1},{4,6},{5,7},{6,4},{7,5},{8,10},{9,11},{10,... | collective-permute-start | bytes 2654216 | tf_op jit(solution)/shard_map/ppermute | solution.py:351
  157.0 22.3 %collective-permute-start.29 = (bf16[576,768]{1,0:T(8,128)(2,1)}, bf16[576,768]{1,0:T(8,128)(2,1)}, u32[]{:S(2)}, u32[]{:S(2)}) collective-permute-start(bf16[576,768]{1,0:T(8,128)(2,1)} %get-tuple-element.340), channel_id=1, source_target_pairs={{0,8},{1,9},{2,4},{3,5},{4,2},{5,3},{6,14},{7,15},{8,0},{9,1},{10,... | collective-permute-start | bytes 2654216 | tf_op jit(solution)/shard_map/ppermute | solution.py:351
  176.7 19.9 %collective-permute-start.30 = (bf16[768,512]{1,0:T(8,128)(2,1)}, bf16[768,512]{1,0:T(8,128)(2,1)}, u32[]{:S(2)}, u32[]{:S(2)}) collective-permute-start(bf16[768,512]{1,0:T(8,128)(2,1)} %get-tuple-element.346), channel_id=1, source_target_pairs={{0,1},{1,0},{2,3},{3,2},{4,5},{5,4},{6,7},{7,6},{8,9},{9,8},{10,11... | collective-permute-start | bytes 2359304 | tf_op jit(solution)/shard_map/ppermute | solution.py:339
  176.8 23.0 %collective-permute-start.31 = (bf16[576,768]{1,0:T(8,128)(2,1)}, bf16[576,768]{1,0:T(8,128)(2,1)}, u32[]{:S(2)}, u32[]{:S(2)}) collective-permute-start(bf16[576,768]{1,0:T(8,128)(2,1)} %get-tuple-element.347), channel_id=1, source_target_pairs={{0,2},{1,3},{2,0},{3,1},{4,6},{5,7},{6,4},{7,5},{8,10},{9,11},{10,... | collective-permute-start | bytes 2654216 | tf_op jit(solution)/shard_map/ppermute | solution.py:351
  177.9 21.9 %collective-permute-start.32 = (bf16[576,768]{1,0:T(8,128)(2,1)}, bf16[576,768]{1,0:T(8,128)(2,1)}, u32[]{:S(2)}, u32[]{:S(2)}) collective-permute-start(bf16[576,768]{1,0:T(8,128)(2,1)} %get-tuple-element.348), channel_id=1, source_target_pairs={{0,8},{1,9},{2,4},{3,5},{4,2},{5,3},{6,14},{7,15},{8,0},{9,1},{10,... | collective-permute-start | bytes 2654216 | tf_op jit(solution)/shard_map/ppermute | solution.py:351
  188.2 27.8 %collective-permute-start.33 = (bf16[768,512]{1,0:T(8,128)(2,1)}, bf16[768,512]{1,0:T(8,128)(2,1)S(1)}, u32[]{:S(2)}, u32[]{:S(2)}) collective-permute-start(bf16[768,512]{1,0:T(8,128)(2,1)} %side_step.41), channel_id=1, source_target_pairs={{0,1},{1,0},{2,3},{3,2},{4,5},{5,4},{6,7},{7,6},{8,9},{9,8},{10,11... | collective-permute-start | bytes 2359304 | tf_op jit(solution)/shard_map/ppermute | solution.py:339
  189.3 27.8 %collective-permute-start.34 = (bf16[576,768]{1,0:T(8,128)(2,1)}, bf16[576,768]{1,0:T(8,128)(2,1)}, u32[]{:S(2)}, u32[]{:S(2)}) collective-permute-start(bf16[576,768]{1,0:T(8,128)(2,1)} %get-tuple-element.358), channel_id=1, source_target_pairs={{0,2},{1,3},{2,0},{3,1},{4,6},{5,7},{6,4},{7,5},{8,10},{9,11},{10,... | collective-permute-start | bytes 2654216 | tf_op jit(solution)/shard_map/ppermute | solution.py:351
  196.6 20.5 %collective-permute-start.35 = (bf16[576,768]{1,0:T(8,128)(2,1)}, bf16[576,768]{1,0:T(8,128)(2,1)}, u32[]{:S(2)}, u32[]{:S(2)}) collective-permute-start(bf16[576,768]{1,0:T(8,128)(2,1)} %get-tuple-element.359), channel_id=1, source_target_pairs={{0,8},{1,9},{2,4},{3,5},{4,2},{5,3},{6,14},{7,15},{8,0},{9,1},{10,... | collective-permute-start | bytes 2654216 | tf_op jit(solution)/shard_map/ppermute | solution.py:351
  211.7 19.4 %collective-permute-start.36 = (bf16[768,512]{1,0:T(8,128)(2,1)}, bf16[768,512]{1,0:T(8,128)(2,1)}, u32[]{:S(2)}, u32[]{:S(2)}) collective-permute-start(bf16[768,512]{1,0:T(8,128)(2,1)} %get-tuple-element.365), channel_id=1, source_target_pairs={{0,1},{1,0},{2,3},{3,2},{4,5},{5,4},{6,7},{7,6},{8,9},{9,8},{10,11... | collective-permute-start | bytes 2359304 | tf_op jit(solution)/shard_map/ppermute | solution.py:339
  213.8 23.1 %collective-permute-start.37 = (bf16[576,768]{1,0:T(8,128)(2,1)}, bf16[576,768]{1,0:T(8,128)(2,1)}, u32[]{:S(2)}, u32[]{:S(2)}) collective-permute-start(bf16[576,768]{1,0:T(8,128)(2,1)} %get-tuple-element.366), channel_id=1, source_target_pairs={{0,2},{1,3},{2,0},{3,1},{4,6},{5,7},{6,4},{7,5},{8,10},{9,11},{10,... | collective-permute-start | bytes 2654216 | tf_op jit(solution)/shard_map/ppermute | solution.py:351
  216.0 20.9 %collective-permute-start.38 = (bf16[576,768]{1,0:T(8,128)(2,1)}, bf16[576,768]{1,0:T(8,128)(2,1)}, u32[]{:S(2)}, u32[]{:S(2)}) collective-permute-start(bf16[576,768]{1,0:T(8,128)(2,1)} %get-tuple-element.367), channel_id=1, source_target_pairs={{0,8},{1,9},{2,4},{3,5},{4,2},{5,3},{6,14},{7,15},{8,0},{9,1},{10,... | collective-permute-start | bytes 2654216 | tf_op jit(solution)/shard_map/ppermute | solution.py:351
  226.0 27.2 %collective-permute-start.39 = (bf16[768,512]{1,0:T(8,128)(2,1)}, bf16[768,512]{1,0:T(8,128)(2,1)S(1)}, u32[]{:S(2)}, u32[]{:S(2)}) collective-permute-start(bf16[768,512]{1,0:T(8,128)(2,1)} %side_step.43), channel_id=1, source_target_pairs={{0,1},{1,0},{2,3},{3,2},{4,5},{5,4},{6,7},{7,6},{8,9},{9,8},{10,11... | collective-permute-start | bytes 2359304 | tf_op jit(solution)/shard_map/ppermute | solution.py:339
  227.8 28.1 %collective-permute-start.40 = (bf16[576,768]{1,0:T(8,128)(2,1)}, bf16[576,768]{1,0:T(8,128)(2,1)}, u32[]{:S(2)}, u32[]{:S(2)}) collective-permute-start(bf16[576,768]{1,0:T(8,128)(2,1)} %get-tuple-element.377), channel_id=1, source_target_pairs={{0,2},{1,3},{2,0},{3,1},{4,6},{5,7},{6,4},{7,5},{8,10},{9,11},{10,... | collective-permute-start | bytes 2654216 | tf_op jit(solution)/shard_map/ppermute | solution.py:351
  231.1 24.7 %collective-permute-start.41 = (bf16[576,768]{1,0:T(8,128)(2,1)}, bf16[576,768]{1,0:T(8,128)(2,1)}, u32[]{:S(2)}, u32[]{:S(2)}) collective-permute-start(bf16[576,768]{1,0:T(8,128)(2,1)} %get-tuple-element.378), channel_id=1, source_target_pairs={{0,8},{1,9},{2,4},{3,5},{4,2},{5,3},{6,14},{7,15},{8,0},{9,1},{10,... | collective-permute-start | bytes 2654216 | tf_op jit(solution)/shard_map/ppermute | solution.py:351
  248.9 18.5 %collective-permute-start.42 = (bf16[768,512]{1,0:T(8,128)(2,1)}, bf16[768,512]{1,0:T(8,128)(2,1)S(1)}, u32[]{:S(2)}, u32[]{:S(2)}) collective-permute-start(bf16[768,512]{1,0:T(8,128)(2,1)} %get-tuple-element.384), channel_id=1, source_target_pairs={{0,1},{1,0},{2,3},{3,2},{4,5},{5,4},{6,7},{7,6},{8,9},{9,8},{10,11... | collective-permute-start | bytes 2359304 | tf_op jit(solution)/shard_map/ppermute | solution.py:339
  249.8 25.0 %collective-permute-start.43 = (bf16[576,768]{1,0:T(8,128)(2,1)}, bf16[576,768]{1,0:T(8,128)(2,1)}, u32[]{:S(2)}, u32[]{:S(2)}) collective-permute-start(bf16[576,768]{1,0:T(8,128)(2,1)} %get-tuple-element.385), channel_id=1, source_target_pairs={{0,2},{1,3},{2,0},{3,1},{4,6},{5,7},{6,4},{7,5},{8,10},{9,11},{10,... | collective-permute-start | bytes 2654216 | tf_op jit(solution)/shard_map/ppermute | solution.py:351
  253.2 21.6 %collective-permute-start.44 = (bf16[576,768]{1,0:T(8,128)(2,1)}, bf16[576,768]{1,0:T(8,128)(2,1)}, u32[]{:S(2)}, u32[]{:S(2)}) collective-permute-start(bf16[576,768]{1,0:T(8,128)(2,1)} %get-tuple-element.386), channel_id=1, source_target_pairs={{0,8},{1,9},{2,4},{3,5},{4,2},{5,3},{6,14},{7,15},{8,0},{9,1},{10,... | collective-permute-start | bytes 2654216 | tf_op jit(solution)/shard_map/ppermute | solution.py:351
  264.8 26.6 %collective-permute-start.45 = (bf16[768,512]{1,0:T(8,128)(2,1)}, bf16[768,512]{1,0:T(8,128)(2,1)S(1)}, u32[]{:S(2)}, u32[]{:S(2)}) collective-permute-start(bf16[768,512]{1,0:T(8,128)(2,1)} %side_step.45), channel_id=1, source_target_pairs={{0,1},{1,0},{2,3},{3,2},{4,5},{5,4},{6,7},{7,6},{8,9},{9,8},{10,11... | collective-permute-start | bytes 2359304 | tf_op jit(solution)/shard_map/ppermute | solution.py:339
  265.7 27.9 %collective-permute-start.46 = (bf16[576,768]{1,0:T(8,128)(2,1)}, bf16[576,768]{1,0:T(8,128)(2,1)}, u32[]{:S(2)}, u32[]{:S(2)}) collective-permute-start(bf16[576,768]{1,0:T(8,128)(2,1)} %get-tuple-element.396), channel_id=1, source_target_pairs={{0,2},{1,3},{2,0},{3,1},{4,6},{5,7},{6,4},{7,5},{8,10},{9,11},{10,... | collective-permute-start | bytes 2654216 | tf_op jit(solution)/shard_map/ppermute | solution.py:351
  267.5 26.2 %collective-permute-start.47 = (bf16[576,768]{1,0:T(8,128)(2,1)}, bf16[576,768]{1,0:T(8,128)(2,1)}, u32[]{:S(2)}, u32[]{:S(2)}) collective-permute-start(bf16[576,768]{1,0:T(8,128)(2,1)} %get-tuple-element.397), channel_id=1, source_target_pairs={{0,8},{1,9},{2,4},{3,5},{4,2},{5,3},{6,14},{7,15},{8,0},{9,1},{10,... | collective-permute-start | bytes 2654216 | tf_op jit(solution)/shard_map/ppermute | solution.py:351
  289.4 23.2 %collective-permute-start.49 = (bf16[576,768]{1,0:T(8,128)(2,1)}, bf16[576,768]{1,0:T(8,128)(2,1)}, u32[]{:S(2)}, u32[]{:S(2)}) collective-permute-start(bf16[576,768]{1,0:T(8,128)(2,1)} %get-tuple-element.404), channel_id=1, source_target_pairs={{0,2},{1,3},{2,0},{3,1},{4,6},{5,7},{6,4},{7,5},{8,10},{9,11},{10,... | collective-permute-start | bytes 2654216 | tf_op jit(solution)/shard_map/ppermute | solution.py:351
  291.4 21.2 %collective-permute-start.50 = (bf16[576,768]{1,0:T(8,128)(2,1)}, bf16[576,768]{1,0:T(8,128)(2,1)}, u32[]{:S(2)}, u32[]{:S(2)}) collective-permute-start(bf16[576,768]{1,0:T(8,128)(2,1)} %get-tuple-element.405), channel_id=1, source_target_pairs={{0,8},{1,9},{2,4},{3,5},{4,2},{5,3},{6,14},{7,15},{8,0},{9,1},{10,... | collective-permute-start | bytes 2654216 | tf_op jit(solution)/shard_map/ppermute | solution.py:351
  302.6 26.8 %collective-permute-start.51 = (bf16[768,512]{1,0:T(8,128)(2,1)}, bf16[768,512]{1,0:T(8,128)(2,1)S(1)}, u32[]{:S(2)}, u32[]{:S(2)}) collective-permute-start(bf16[768,512]{1,0:T(8,128)(2,1)} %side_step.47), channel_id=1, source_target_pairs={{0,1},{1,0},{2,3},{3,2},{4,5},{5,4},{6,7},{7,6},{8,9},{9,8},{10,11... | collective-permute-start | bytes 2359304 | tf_op jit(solution)/shard_map/ppermute | solution.py:339
  303.6 28.0 %collective-permute-start.52 = (bf16[576,768]{1,0:T(8,128)(2,1)}, bf16[576,768]{1,0:T(8,128)(2,1)}, u32[]{:S(2)}, u32[]{:S(2)}) collective-permute-start(bf16[576,768]{1,0:T(8,128)(2,1)} %get-tuple-element.415), channel_id=1, source_target_pairs={{0,2},{1,3},{2,0},{3,1},{4,6},{5,7},{6,4},{7,5},{8,10},{9,11},{10,... | collective-permute-start | bytes 2654216 | tf_op jit(solution)/shard_map/ppermute | solution.py:351
  305.6 25.9 %collective-permute-start.53 = (bf16[576,768]{1,0:T(8,128)(2,1)}, bf16[576,768]{1,0:T(8,128)(2,1)}, u32[]{:S(2)}, u32[]{:S(2)}) collective-permute-start(bf16[576,768]{1,0:T(8,128)(2,1)} %get-tuple-element.416), channel_id=1, source_target_pairs={{0,8},{1,9},{2,4},{3,5},{4,2},{5,3},{6,14},{7,15},{8,0},{9,1},{10,... | collective-permute-start | bytes 2654216 | tf_op jit(solution)/shard_map/ppermute | solution.py:351
  327.4 23.1 %collective-permute-start.55 = (bf16[576,768]{1,0:T(8,128)(2,1)}, bf16[576,768]{1,0:T(8,128)(2,1)}, u32[]{:S(2)}, u32[]{:S(2)}) collective-permute-start(bf16[576,768]{1,0:T(8,128)(2,1)} %get-tuple-element.423), channel_id=1, source_target_pairs={{0,2},{1,3},{2,0},{3,1},{4,6},{5,7},{6,4},{7,5},{8,10},{9,11},{10,... | collective-permute-start | bytes 2654216 | tf_op jit(solution)/shard_map/ppermute | solution.py:351
  329.3 21.2 %collective-permute-start.56 = (bf16[576,768]{1,0:T(8,128)(2,1)}, bf16[576,768]{1,0:T(8,128)(2,1)}, u32[]{:S(2)}, u32[]{:S(2)}) collective-permute-start(bf16[576,768]{1,0:T(8,128)(2,1)} %get-tuple-element.424), channel_id=1, source_target_pairs={{0,8},{1,9},{2,4},{3,5},{4,2},{5,3},{6,14},{7,15},{8,0},{9,1},{10,... | collective-permute-start | bytes 2654216 | tf_op jit(solution)/shard_map/ppermute | solution.py:351
  340.5 26.9 %collective-permute-start.57 = (bf16[768,512]{1,0:T(8,128)(2,1)}, bf16[768,512]{1,0:T(8,128)(2,1)S(1)}, u32[]{:S(2)}, u32[]{:S(2)}) collective-permute-start(bf16[768,512]{1,0:T(8,128)(2,1)} %side_step.49), channel_id=1, source_target_pairs={{0,1},{1,0},{2,3},{3,2},{4,5},{5,4},{6,7},{7,6},{8,9},{9,8},{10,11... | collective-permute-start | bytes 2359304 | tf_op jit(solution)/shard_map/ppermute | solution.py:339
  341.5 28.0 %collective-permute-start.58 = (bf16[576,768]{1,0:T(8,128)(2,1)}, bf16[576,768]{1,0:T(8,128)(2,1)}, u32[]{:S(2)}, u32[]{:S(2)}) collective-permute-start(bf16[576,768]{1,0:T(8,128)(2,1)} %get-tuple-element.434), channel_id=1, source_target_pairs={{0,2},{1,3},{2,0},{3,1},{4,6},{5,7},{6,4},{7,5},{8,10},{9,11},{10,... | collective-permute-start | bytes 2654216 | tf_op jit(solution)/shard_map/ppermute | solution.py:351
  343.6 25.9 %collective-permute-start.59 = (bf16[576,768]{1,0:T(8,128)(2,1)}, bf16[576,768]{1,0:T(8,128)(2,1)}, u32[]{:S(2)}, u32[]{:S(2)}) collective-permute-start(bf16[576,768]{1,0:T(8,128)(2,1)} %get-tuple-element.435), channel_id=1, source_target_pairs={{0,8},{1,9},{2,4},{3,5},{4,2},{5,3},{6,14},{7,15},{8,0},{9,1},{10,... | collective-permute-start | bytes 2654216 | tf_op jit(solution)/shard_map/ppermute | solution.py:351
  365.2 23.2 %collective-permute-start.61 = (bf16[576,768]{1,0:T(8,128)(2,1)}, bf16[576,768]{1,0:T(8,128)(2,1)}, u32[]{:S(2)}, u32[]{:S(2)}) collective-permute-start(bf16[576,768]{1,0:T(8,128)(2,1)} %get-tuple-element.442), channel_id=1, source_target_pairs={{0,2},{1,3},{2,0},{3,1},{4,6},{5,7},{6,4},{7,5},{8,10},{9,11},{10,... | collective-permute-start | bytes 2654216 | tf_op jit(solution)/shard_map/ppermute | solution.py:351
  367.4 21.1 %collective-permute-start.62 = (bf16[576,768]{1,0:T(8,128)(2,1)}, bf16[576,768]{1,0:T(8,128)(2,1)}, u32[]{:S(2)}, u32[]{:S(2)}) collective-permute-start(bf16[576,768]{1,0:T(8,128)(2,1)} %get-tuple-element.443), channel_id=1, source_target_pairs={{0,8},{1,9},{2,4},{3,5},{4,2},{5,3},{6,14},{7,15},{8,0},{9,1},{10,... | collective-permute-start | bytes 2654216 | tf_op jit(solution)/shard_map/ppermute | solution.py:351
  378.4 25.6 %collective-permute-start.63 = (bf16[768,512]{1,0:T(8,128)(2,1)}, bf16[768,512]{1,0:T(8,128)(2,1)S(1)}, u32[]{:S(2)}, u32[]{:S(2)}) collective-permute-start(bf16[768,512]{1,0:T(8,128)(2,1)} %side_step.51), channel_id=1, source_target_pairs={{0,1},{1,0},{2,3},{3,2},{4,5},{5,4},{6,7},{7,6},{8,9},{9,8},{10,11... | collective-permute-start | bytes 2359304 | tf_op jit(solution)/shard_map/ppermute | solution.py:339
  379.4 28.0 %collective-permute-start.64 = (bf16[576,768]{1,0:T(8,128)(2,1)}, bf16[576,768]{1,0:T(8,128)(2,1)}, u32[]{:S(2)}, u32[]{:S(2)}) collective-permute-start(bf16[576,768]{1,0:T(8,128)(2,1)} %get-tuple-element.453), channel_id=1, source_target_pairs={{0,2},{1,3},{2,0},{3,1},{4,6},{5,7},{6,4},{7,5},{8,10},{9,11},{10,... | collective-permute-start | bytes 2654216 | tf_op jit(solution)/shard_map/ppermute | solution.py:351
  381.5 25.9 %collective-permute-start.65 = (bf16[576,768]{1,0:T(8,128)(2,1)}, bf16[576,768]{1,0:T(8,128)(2,1)}, u32[]{:S(2)}, u32[]{:S(2)}) collective-permute-start(bf16[576,768]{1,0:T(8,128)(2,1)} %get-tuple-element.454), channel_id=1, source_target_pairs={{0,8},{1,9},{2,4},{3,5},{4,2},{5,3},{6,14},{7,15},{8,0},{9,1},{10,... | collective-permute-start | bytes 2654216 | tf_op jit(solution)/shard_map/ppermute | solution.py:351
  394.7 31.7 %collective-permute-start.67 = (bf16[576,768]{1,0:T(8,128)(2,1)}, bf16[576,768]{1,0:T(8,128)(2,1)}, u32[]{:S(2)}, u32[]{:S(2)}) collective-permute-start(bf16[576,768]{1,0:T(8,128)(2,1)} %get-tuple-element.461), channel_id=1, source_target_pairs={{0,2},{1,3},{2,0},{3,1},{4,6},{5,7},{6,4},{7,5},{8,10},{9,11},{10,... | collective-permute-start | bytes 2654216 | tf_op jit(solution)/shard_map/ppermute | solution.py:351
  396.6 29.8 %collective-permute-start.68 = (bf16[576,768]{1,0:T(8,128)(2,1)}, bf16[576,768]{1,0:T(8,128)(2,1)}, u32[]{:S(2)}, u32[]{:S(2)}) collective-permute-start(bf16[576,768]{1,0:T(8,128)(2,1)} %get-tuple-element.462), channel_id=1, source_target_pairs={{0,8},{1,9},{2,4},{3,5},{4,2},{5,3},{6,14},{7,15},{8,0},{9,1},{10,... | collective-permute-start | bytes 2654216 | tf_op jit(solution)/shard_map/ppermute | solution.py:351
  404.0 20.2 %collective-permute-start.66 = (bf16[768,512]{1,0:T(8,128)(2,1)}, bf16[768,512]{1,0:T(8,128)(2,1)S(1)}, u32[]{:S(2)}, u32[]{:S(2)}) collective-permute-start(bf16[768,512]{1,0:T(8,128)(2,1)} %get-tuple-element.460), channel_id=1, source_target_pairs={{0,1},{1,0},{2,3},{3,2},{4,5},{5,4},{6,7},{7,6},{8,9},{9,8},{10,11... | collective-permute-start | bytes 2359304 | tf_op jit(solution)/shard_map/ppermute | solution.py:339
  413.6 31.7 %collective-permute-start.69 = (bf16[576,768]{1,0:T(8,128)(2,1)}, bf16[576,768]{1,0:T(8,128)(2,1)}, u32[]{:S(2)}, u32[]{:S(2)}) collective-permute-start(bf16[576,768]{1,0:T(8,128)(2,1)} %get-tuple-element.471), channel_id=1, source_target_pairs={{0,2},{1,3},{2,0},{3,1},{4,6},{5,7},{6,4},{7,5},{8,10},{9,11},{10,... | collective-permute-start | bytes 2654216 | tf_op jit(solution)/shard_map/ppermute | solution.py:351
  415.6 29.8 %collective-permute-start.70 = (bf16[576,768]{1,0:T(8,128)(2,1)}, bf16[576,768]{1,0:T(8,128)(2,1)}, u32[]{:S(2)}, u32[]{:S(2)}) collective-permute-start(bf16[576,768]{1,0:T(8,128)(2,1)} %get-tuple-element.472), channel_id=1, source_target_pairs={{0,8},{1,9},{2,4},{3,5},{4,2},{5,3},{6,14},{7,15},{8,0},{9,1},{10,... | collective-permute-start | bytes 2654216 | tf_op jit(solution)/shard_map/ppermute | solution.py:351
  432.6 31.6 %collective-permute-start.71 = (bf16[576,768]{1,0:T(8,128)(2,1)}, bf16[576,768]{1,0:T(8,128)(2,1)S(1)}, u32[]{:S(2)}, u32[]{:S(2)}) collective-permute-start(bf16[576,768]{1,0:T(8,128)(2,1)} %get-tuple-element.478), channel_id=1, source_target_pairs={{0,2},{1,3},{2,0},{3,1},{4,6},{5,7},{6,4},{7,5},{8,10},{9,11},{10,... | collective-permute-start | bytes 2654216 | tf_op jit(solution)/shard_map/ppermute | solution.py:351
  434.5 29.7 %collective-permute-start.72 = (bf16[576,768]{1,0:T(8,128)(2,1)}, bf16[576,768]{1,0:T(8,128)(2,1)}, u32[]{:S(2)}, u32[]{:S(2)}) collective-permute-start(bf16[576,768]{1,0:T(8,128)(2,1)} %get-tuple-element.479), channel_id=1, source_target_pairs={{0,8},{1,9},{2,4},{3,5},{4,2},{5,3},{6,14},{7,15},{8,0},{9,1},{10,... | collective-permute-start | bytes 2654216 | tf_op jit(solution)/shard_map/ppermute | solution.py:351
  451.6 38.4 %collective-permute-start.75 = (bf16[576,768]{1,0:T(8,128)(2,1)}, bf16[576,768]{1,0:T(8,128)(2,1)}, u32[]{:S(2)}, u32[]{:S(2)}) collective-permute-start(bf16[576,768]{1,0:T(8,128)(2,1)} %get-tuple-element.490), channel_id=1, source_target_pairs={{0,2},{1,3},{2,0},{3,1},{4,6},{5,7},{6,4},{7,5},{8,10},{9,11},{10,... | collective-permute-start | bytes 2654216 | tf_op jit(solution)/shard_map/ppermute | solution.py:351
  453.5 36.5 %collective-permute-start.76 = (bf16[576,768]{1,0:T(8,128)(2,1)}, bf16[576,768]{1,0:T(8,128)(2,1)}, u32[]{:S(2)}, u32[]{:S(2)}) collective-permute-start(bf16[576,768]{1,0:T(8,128)(2,1)} %get-tuple-element.491), channel_id=1, source_target_pairs={{0,8},{1,9},{2,4},{3,5},{4,2},{5,3},{6,14},{7,15},{8,0},{9,1},{10,... | collective-permute-start | bytes 2654216 | tf_op jit(solution)/shard_map/ppermute | solution.py:351
  454.9 18.3 %collective-permute-start.73 = (bf16[256,512]{1,0:T(8,128)(2,1)S(1)}, bf16[256,512]{1,0:T(8,128)(2,1)S(1)}, u32[]{:S(2)}, u32[]{:S(2)}) collective-permute-start(bf16[256,512]{1,0:T(8,128)(2,1)S(1)} %copy-done.38), channel_id=1, source_target_pairs={{0,1},{1,0},{2,3},{3,2},{4,5},{5,4},{6,7},{7,6},{8,9},{9,8},{10,11... | collective-permute-start | bytes 786440 | tf_op jit(solution)/shard_map/ppermute | solution.py:339
  471.4 29.5 %collective-permute-start.78 = (bf16[576,768]{1,0:T(8,128)(2,1)}, bf16[576,768]{1,0:T(8,128)(2,1)}, u32[]{:S(2)}, u32[]{:S(2)}) collective-permute-start(bf16[576,768]{1,0:T(8,128)(2,1)} %get-tuple-element.500), channel_id=1, source_target_pairs={{0,2},{1,3},{2,0},{3,1},{4,6},{5,7},{6,4},{7,5},{8,10},{9,11},{10,... | collective-permute-start | bytes 2654216 | tf_op jit(solution)/shard_map/ppermute | solution.py:351
  473.2 27.7 %collective-permute-start.79 = (bf16[576,768]{1,0:T(8,128)(2,1)}, bf16[576,768]{1,0:T(8,128)(2,1)}, u32[]{:S(2)}, u32[]{:S(2)}) collective-permute-start(bf16[576,768]{1,0:T(8,128)(2,1)} %get-tuple-element.501), channel_id=1, source_target_pairs={{0,8},{1,9},{2,4},{3,5},{4,2},{5,3},{6,14},{7,15},{8,0},{9,1},{10,... | collective-permute-start | bytes 2654216 | tf_op jit(solution)/shard_map/ppermute | solution.py:351
  496.4 30.9 %collective-permute-start.82 = (bf16[576,768]{1,0:T(8,128)(2,1)}, bf16[576,768]{1,0:T(8,128)(2,1)}, u32[]{:S(2)}, u32[]{:S(2)}) collective-permute-start(bf16[576,768]{1,0:T(8,128)(2,1)} %get-tuple-element.512), channel_id=1, source_target_pairs={{0,2},{1,3},{2,0},{3,1},{4,6},{5,7},{6,4},{7,5},{8,10},{9,11},{10,... | collective-permute-start | bytes 2654216 | tf_op jit(solution)/shard_map/ppermute | solution.py:351
  496.4 30.8 %collective-permute-start.83 = (bf16[576,768]{1,0:T(8,128)(2,1)}, bf16[576,768]{1,0:T(8,128)(2,1)}, u32[]{:S(2)}, u32[]{:S(2)}) collective-permute-start(bf16[576,768]{1,0:T(8,128)(2,1)} %get-tuple-element.513), channel_id=1, source_target_pairs={{0,8},{1,9},{2,4},{3,5},{4,2},{5,3},{6,14},{7,15},{8,0},{9,1},{10,... | collective-permute-start | bytes 2654216 | tf_op jit(solution)/shard_map/ppermute | solution.py:351
  507.2 31.0 %collective-permute-start.86 = (bf16[576,768]{1,0:T(8,128)(2,1)}, bf16[576,768]{1,0:T(8,128)(2,1)}, u32[]{:S(2)}, u32[]{:S(2)}) collective-permute-start(bf16[576,768]{1,0:T(8,128)(2,1)} %get-tuple-element.516), channel_id=1, source_target_pairs={{0,2},{1,3},{2,0},{3,1},{4,6},{5,7},{6,4},{7,5},{8,10},{9,11},{10,... | collective-permute-start | bytes 2654216 | tf_op jit(solution)/shard_map/ppermute | solution.py:351
  510.6 27.7 %collective-permute-start.87 = (bf16[576,768]{1,0:T(8,128)(2,1)}, bf16[576,768]{1,0:T(8,128)(2,1)}, u32[]{:S(2)}, u32[]{:S(2)}) collective-permute-start(bf16[576,768]{1,0:T(8,128)(2,1)} %get-tuple-element.517), channel_id=1, source_target_pairs={{0,8},{1,9},{2,4},{3,5},{4,2},{5,3},{6,14},{7,15},{8,0},{9,1},{10,... | collective-permute-start | bytes 2654216 | tf_op jit(solution)/shard_map/ppermute | solution.py:351
  564.2 18.4 %collective-permute-start.96 = (bf16[576,256]{1,0:T(8,128)(2,1)}, bf16[576,256]{1,0:T(8,128)(2,1)S(1)}, u32[]{:S(2)}, u32[]{:S(2)}) collective-permute-start(bf16[576,256]{1,0:T(8,128)(2,1)} %collective-permute-done.93.refs_7_), channel_id=1, source_target_pairs={{0,2},{1,3},{2,0},{3,1},{4,6},{5,7},{6,4},{7,5},{8,10},{9,11},{10,... | collective-permute-start | bytes 884744 | tf_op jit(solution)/shard_map/ppermute | solution.py:351
  645.3 21.1 %collective-permute-start.102 = (bf16[192,512]{1,0:T(8,128)(2,1)S(1)}, bf16[192,512]{1,0:T(8,128)(2,1)S(1)}, u32[]{:S(2)}, u32[]{:S(2)}) collective-permute-start(bf16[192,512]{1,0:T(8,128)(2,1)S(1)} %get-tuple-element.566), channel_id=1, source_target_pairs={{0,0},{1,1},{2,8},{3,9},{4,16},{5,17},{6,24},{7,25},{8,2},{9,3},{1... | collective-permute-start | bytes 589832 | tf_op jit(solution)/shard_map/ppermute | solution.py:660
  (85 other events, 821.3 us)

commit v4 on v3

--- a/solution.py
+++ b/solution.py
@@ -387,8 +387,6 @@
 
     weights = (gate_weight, up_weight, down_weight)
     early = min(ahead, n_chunks)
-    firsts = [lay_out(k, weights) for k in range(early)]
-    hand_over(0, firsts[0])
 
     picked = routes == expert
     chosen = jnp.any(picked, axis=1)
@@ -410,6 +408,9 @@
     def columns(array, index, size):
         return lax.dynamic_slice_in_dim(array, index * size, size, 1)
 
+    packed, weights = lax.optimization_barrier((packed, weights))
+    firsts = [lay_out(k, weights) for k in range(early)]
+    hand_over(0, firsts[0])
     pieces = []
     for k in range(deep):
         piece = columns(packed, z ^ k, across * feat)

time: 678 us -> 676 us (level)
  starting transfers between devices: 111 us -> 104 us
  transfers between devices with their start and end apart: 104 -> 104, of which waited for: 40 -> 43; matrix products, arithmetic and copies ran while one was open for 5% -> 5% of each run, Pallas kernels for 44% -> 45%
where the time goes in v4:
time: 676 us; the launch traced here: 666 us
  Pallas kernels  302 us (45%)
  waiting for transfers between devices  194 us (29%)
  starting transfers between devices  104 us (15%)
  local copies, waits for them, and re-layouts  45.9 us (7%)
  other arithmetic  14.6 us (2%)
    pallas_call x59, Pallas kernels, call(): pl.pallas_call(kernel, out_shape=outs, in_specs=[pl.BlockSpec(memory_spac...  302 us
    ppermute x38, waiting for transfers between devices, swap(): return lax.ppermute(array, 'fsdp', perm)  94.2 us
    ppermute x62, waiting for transfers between devices, pairing(): return lax.ppermute(array, ('member', 'fsdp'), perm)  70.1 us
    ppermute x62, starting transfers between devices, pairing(): return lax.ppermute(array, ('member', 'fsdp'), perm)  55.6 us
    ppermute x38, starting transfers between devices, swap(): return lax.ppermute(array, 'fsdp', perm)  42.8 us
    another operation x28, local copies, waits for them, and re-layouts, body(): jnp.stack([z, x, start_of(up_c), start_of(dn_c), jnp.int32(skip)])  18.8 us
    ppermute x2, waiting for transfers between devices, body(): parts.append(lax.ppermute(pick(mixed, slot ^ j), ('member', 'fsdp'), perm))  15.6 us
    ppermute x2, waiting for transfers between devices, body(): came = lax.ppermute(give, 'member', [(m, m ^ bit) for m in range(members)])  14.3 us
  transfers between devices with their start and end apart: 104, of which 43 were waited for; matrix products, arithmetic and copies ran while one was open for 5% of the time, Pallas kernels for 45%

profile of v4, /device:TPU:4, one launch (start us, length us, event | category | flops | bytes accessed | tf_op | source)
XLA Modules:
  0.0 666.1 jit_solution(15986629181694936027)
XLA Ops:
  14.8 16.9 %collective-permute-done.1 = bf16[144,1024]{1,0:T(8,128)(2,1)S(1)} collective-permute-done((bf16[144,1024]{1,0:T(8,128)(2,1)S(1)}, bf16[144,1024]{1,0:T(8,128)(2,1)S(1)}, u32[]{:S(2)}, u32[]{:S(2)}) %collective-permute-start.1) | collective-permute-done | bytes 294944 | tf_op jit(solution)/shard_map/ppermute | solution.py:339
  43.9 17.3 %collective-permute-done.4.refs_4_ = bf16[576,1024]{1,0:T(8,128)(2,1)} collective-permute-done((bf16[576,1024]{1,0:T(8,128)(2,1)S(1)}, bf16[576,1024]{1,0:T(8,128)(2,1)}, u32[]{:S(2)}, u32[]{:S(2)}) %collective-permute-start.4) | collective-permute-done | bytes 1179680 | tf_op jit(solution)/shard_map/ppermute | solution.py:339
  64.0 5.1 chain_step.28
  75.1 5.2 chain_step.29
  87.9 5.3 chain_step.30
  101.9 5.4 chain_step.31
  113.7 5.3 chain_step.32
  125.4 5.4 chain_step.33
  138.5 4.0 collective-permute-done.21.refs_5_.refs_6_.refs_7_.refs_8_.refs_9_.refs_11_.refs_12_.refs_13_
  143.4 6.3 chain_step.34
  160.2 6.2 chain_step.35
  169.2 5.7 side_step.40
  178.2 6.2 chain_step.36
  190.6 3.8 collective-permute-done.30.refs_5_.refs_10_.refs_6_.refs_11_.refs_7_.refs_12_.refs_8_.refs_13_
  195.7 3.9 collective-permute-done.31.refs_9_
  199.6 6.3 chain_step.37
  205.9 5.7 side_step.42
  216.3 6.2 chain_step.38
  235.3 6.3 chain_step.39
  241.6 5.7 side_step.44
  254.3 6.2 chain_step.40
  267.6 5.6 collective-permute-done.43.refs_9_
  273.2 6.3 chain_step.41
  279.5 7.4 %side_step.46 = (bf16[768,512]{1,0:T(8,128)(2,1)}, f32[1152,1024]{1,0:T(8,128)}) custom-call(s32[12]{0:T(128)} %stack.1170.refs_0_, bf16[11008,512]{1,0:T(8,128)(2,1)} %bitcast.217, bf16[11008,512]{1,0:T(8,128)(2,1)} %bitcast.276, bf16[11008,512]{1,0:T(8,128)(2,1)} %bitcast.321, ...), custom_call_target="tpu_custom_call", output_to_operand_aliasing={{1}: (14, {})} | custom-call | flops 1207959552 | bytes 12582912 | tf_op jit(solution)/shard_map/side_step/pallas_call | solution.py:297
  292.2 6.2 chain_step.42
  306.7 4.5 collective-permute-done.49.refs_9_
  311.1 6.3 chain_step.43
  317.4 7.3 %side_step.48 = (bf16[768,512]{1,0:T(8,128)(2,1)}, f32[1152,1024]{1,0:T(8,128)}) custom-call(s32[12]{0:T(128)} %stack.1152.refs_0_, bf16[11008,512]{1,0:T(8,128)(2,1)} %bitcast.221, bf16[11008,512]{1,0:T(8,128)(2,1)} %bitcast.280, bf16[11008,512]{1,0:T(8,128)(2,1)} %bitcast.323, ...), custom_call_target="tpu_custom_call", output_to_operand_aliasing={{1}: (14, {})} | custom-call | flops 1207959552 | bytes 12582912 | tf_op jit(solution)/shard_map/side_step/pallas_call | solution.py:297
  330.1 6.2 chain_step.44
  344.1 4.9 collective-permute-done.55.refs_9_
  349.0 6.3 chain_step.45
  355.4 7.3 %side_step.50 = (bf16[768,512]{1,0:T(8,128)(2,1)}, f32[1152,1024]{1,0:T(8,128)}) custom-call(s32[12]{0:T(128)} %stack.1134.refs_0_, bf16[11008,512]{1,0:T(8,128)(2,1)} %bitcast.225, bf16[11008,512]{1,0:T(8,128)(2,1)} %bitcast.284, bf16[11008,512]{1,0:T(8,128)(2,1)} %bitcast.325, ...), custom_call_target="tpu_custom_call", output_to_operand_aliasing={{1}: (14, {})} | custom-call | flops 1207959552 | bytes 12582912 | tf_op jit(solution)/shard_map/side_step/pallas_call | solution.py:297
  368.0 6.2 chain_step.46
  382.0 4.9 collective-permute-done.61.refs_9_
  387.0 6.2 chain_step.47
  395.4 7.4 %side_step.52 = (bf16[768,512]{1,0:T(8,128)(2,1)}, f32[1152,1024]{1,0:T(8,128)}) custom-call(s32[12]{0:T(128)} %stack.1112.refs_0_, bf16[11008,512]{1,0:T(8,128)(2,1)} %bitcast.229, bf16[11008,512]{1,0:T(8,128)(2,1)} %bitcast.288, bf16[11008,512]{1,0:T(8,128)(2,1)} %bitcast.327, ...), custom_call_target="tpu_custom_call", output_to_operand_aliasing={{1}: (14, {})} | custom-call | flops 1207959552 | bytes 12582912 | tf_op jit(solution)/shard_map/side_step/pallas_call | solution.py:297
  405.9 6.2 chain_step.48
  418.0 5.1 collective-permute-done.66.refs_5_.refs_10_.refs_6_.refs_11_.refs_7_.refs_12_.refs_8_.refs_13_
  424.9 6.2 chain_step.49
  434.0 7.2 %side_step.54 = (bf16[256,512]{1,0:T(8,128)(2,1)}, f32[1152,1024]{1,0:T(8,128)}) custom-call(s32[12]{0:T(128)} %stack.1090.refs_0_, bf16[11008,512]{1,0:T(8,128)(2,1)} %bitcast.233, bf16[11008,512]{1,0:T(8,128)(2,1)} %bitcast.292, bf16[11008,512]{1,0:T(8,128)(2,1)} %bitcast.329, ...), custom_call_target="tpu_custom_call", output_to_operand_aliasing={{1}: (14, {})} | custom-call | flops 1207959552 | bytes 12582912 | tf_op jit(solution)/shard_map/side_step/pallas_call | solution.py:297
  443.8 6.2 chain_step.50
  456.6 6.1 collective-permute-done.71.refs_9_
  463.6 6.2 chain_step.51
  473.4 6.9 %collective-permute-done.74.refs_10_.refs_11_.refs_12_.refs_15_ = bf16[256,512]{1,0:T(8,128)(2,1)S(1)} collective-permute-done((bf16[256,512]{1,0:T(8,128)(2,1)S(1)}, bf16[256,512]{1,0:T(8,128)(2,1)S(1)}, u32[]{:S(2)}, u32[]{:S(2)}) %collective-permute-start.74) | collective-permute-done | bytes 262176 | tf_op jit(solution)/shard_map/ppermute | solution.py:339
  481.1 7.3 %side_step.56 = (bf16[256,512]{1,0:T(8,128)(2,1)}, f32[1152,1024]{1,0:T(8,128)}) custom-call(s32[12]{0:T(128)} %stack.1072.refs_0_, bf16[11008,512]{1,0:T(8,128)(2,1)} %bitcast.237, bf16[11008,512]{1,0:T(8,128)(2,1)} %bitcast.296, bf16[11008,512]{1,0:T(8,128)(2,1)} %bitcast.331, ...), custom_call_target="tpu_custom_call", output_to_operand_aliasing={{1}: (14, {})} | custom-call | flops 1207959552 | bytes 12582912 | tf_op jit(solution)/shard_map/side_step/pallas_call | solution.py:297
  488.4 6.3 chain_step.52
  500.7 6.2 chain_step.53
  511.3 7.2 %collective-permute-done.81.refs_10_.refs_11_.refs_14_.refs_19_ = bf16[256,512]{1,0:T(8,128)(2,1)S(1)} collective-permute-done((bf16[256,512]{1,0:T(8,128)(2,1)S(1)}, bf16[256,512]{1,0:T(8,128)(2,1)S(1)}, u32[]{:S(2)}, u32[]{:S(2)}) %collective-permute-start.81) | collective-permute-done | bytes 262176 | tf_op jit(solution)/shard_map/ppermute | solution.py:339
  519.2 7.3 %side_step.58 = (bf16[256,512]{1,0:T(8,128)(2,1)}, f32[1152,1024]{1,0:T(8,128)}) custom-call(s32[12]{0:T(128)} %stack.1252.refs_0_, bf16[11008,512]{1,0:T(8,128)(2,1)} %bitcast.241, bf16[11008,512]{1,0:T(8,128)(2,1)} %bitcast.300, bf16[11008,512]{1,0:T(8,128)(2,1)} %bitcast.333, ...), custom_call_target="tpu_custom_call", output_to_operand_aliasing={{1}: (14, {})} | custom-call | flops 1207959552 | bytes 12582912 | tf_op jit(solution)/shard_map/side_step/pallas_call | solution.py:297
  526.5 5.7 chain_step.54
  533.7 4.9 collective-permute-done.86.refs_9_
  538.6 5.8 chain_step.55
  547.2 4.4 collective-permute-done.92.refs_6_
  552.2 4.7 collective-permute-start.91
  556.9 3.9 collective-permute-done.94.refs_10_.refs_8_.refs_12_.refs_13_.refs_16_.refs_17_.refs_18_.refs_20_.refs_21_.refs_22_.refs_24_.refs_25_.refs_26_.refs_27_
  568.1 6.4 side_step.59.refs_16_
  577.3 4.5 collective-permute-done.96.refs_10_.refs_11_
  581.7 5.1 side_step.60.refs_28_
  590.2 7.3 %side_step.61 = f32[1152,1024]{1,0:T(8,128)} custom-call(s32[18]{0:T(128)} %stack.1284.refs_0_, bf16[11008,512]{1,0:T(8,128)(2,1)} %bitcast.246, bf16[11008,512]{1,0:T(8,128)(2,1)} %bitcast.305, bf16[11008,512]{1,0:T(8,128)(2,1)} %bitcast.336, bf16[576,256]{1,0:T(8,128)(2,1)} %collective-permute-done.88.refs_4_, ...), custom_call_target="tpu_custom_call", output_to_operand_aliasing={{}: (28, {})} | custom-call | flops 2415919104 | bytes 12582912 | tf_op jit(solution)/shard_map/side_step/pallas_call | solution.py:297
  597.6 5.2 collective-permute-done.98
  605.1 11.9 %collective-permute-done.99 = bf16[576,512]{1,0:T(8,128)(2,1)S(1)} collective-permute-done((bf16[576,512]{1,0:T(8,128)(2,1)S(1)}, bf16[576,512]{1,0:T(8,128)(2,1)S(1)}, u32[]{:S(2)}, u32[]{:S(2)}) %collective-permute-start.99) | collective-permute-done | bytes 589856 | tf_op jit(solution)/shard_map/ppermute | solution.py:339
  632.7 10.9 %collective-permute-done.101 = bf16[1,384,512]{2,1,0:T(8,128)(2,1)S(1)} collective-permute-done((bf16[1,384,512]{2,1,0:T(8,128)(2,1)}, bf16[1,384,512]{2,1,0:T(8,128)(2,1)S(1)}, u32[]{:S(2)}, u32[]{:S(2)}) %collective-permute-start.101) | collective-permute-done | bytes 393248 | tf_op jit(solution)/shard_map/ppermute | solution.py:649
  644.9 4.4 collective-permute-start.102
  649.3 12.6 %collective-permute-done.103 = bf16[192,512]{1,0:T(8,128)(2,1)S(1)} collective-permute-done((bf16[192,512]{1,0:T(8,128)(2,1)S(1)}, bf16[192,512]{1,0:T(8,128)(2,1)S(1)}, u32[]{:S(2)}, u32[]{:S(2)}) %collective-permute-start.103) | collective-permute-done | bytes 196640 | tf_op jit(solution)/shard_map/ppermute | solution.py:661
  (388 shorter events, 250.6 us)
Async XLA Ops:
  6.4 25.3 %collective-permute-start.1 = (bf16[144,1024]{1,0:T(8,128)(2,1)S(1)}, bf16[144,1024]{1,0:T(8,128)(2,1)S(1)}, u32[]{:S(2)}, u32[]{:S(2)}) collective-permute-start(bf16[144,1024]{1,0:T(8,128)(2,1)S(1)} %get-tuple-element.569), channel_id=1, source_target_pairs={{0,4},{1,5},{2,6},{3,7},{4,0},{5,1},{6,2},{7,3},{8,12},{9,13},{10,... | collective-permute-start | bytes 884744 | tf_op jit(solution)/shard_map/ppermute | solution.py:339
  6.4 25.3 %collective-permute-start = (bf16[144,1024]{1,0:T(8,128)(2,1)S(1)}, bf16[144,1024]{1,0:T(8,128)(2,1)S(1)}, u32[]{:S(2)}, u32[]{:S(2)}) collective-permute-start(bf16[144,1024]{1,0:T(8,128)(2,1)S(1)} %get-tuple-element.570), channel_id=1, source_target_pairs={{0,2},{1,3},{2,0},{3,1},{4,6},{5,7},{6,4},{7,5},{8,10},{9,11},{10,... | collective-permute-start | bytes 884744 | tf_op jit(solution)/shard_map/ppermute | solution.py:339
  11.1 22.8 %collective-permute-start.3 = (bf16[512,512]{1,0:T(8,128)(2,1)}, bf16[512,512]{1,0:T(8,128)(2,1)}, u32[]{:S(2)}, u32[]{:S(2)}) collective-permute-start(bf16[512,512]{1,0:T(8,128)(2,1)} %side_step.31), channel_id=1, source_target_pairs={{0,1},{1,0},{2,3},{3,2},{4,5},{5,4},{6,7},{7,6},{8,9},{9,8},{10,11... | collective-permute-start | bytes 1572872 | tf_op jit(solution)/shard_map/ppermute | solution.py:339
  33.9 27.2 %collective-permute-start.4 = (bf16[576,1024]{1,0:T(8,128)(2,1)S(1)}, bf16[576,1024]{1,0:T(8,128)(2,1)}, u32[]{:S(2)}, u32[]{:S(2)}) collective-permute-start(bf16[576,1024]{1,0:T(8,128)(2,1)S(1)} %pad_maximum_fusion.2.refs_3_), channel_id=1, source_target_pairs={{0,1},{1,0},{2,3},{3,2},{4,5},{5,4},{6,7},{7,6},{8,9},{9,8},{10,11... | collective-permute-start | bytes 3538952 | tf_op jit(solution)/shard_map/ppermute | solution.py:339
  93.3 19.6 %collective-permute-start.16 = (bf16[576,512]{1,0:T(8,128)(2,1)}, bf16[576,512]{1,0:T(8,128)(2,1)}, u32[]{:S(2)}, u32[]{:S(2)}) collective-permute-start(bf16[576,512]{1,0:T(8,128)(2,1)} %get-tuple-element.315), channel_id=1, source_target_pairs={{0,2},{1,3},{2,0},{3,1},{4,6},{5,7},{6,4},{7,5},{8,10},{9,11},{10,... | collective-permute-start | bytes 1769480 | tf_op jit(solution)/shard_map/ppermute | solution.py:351
  94.0 18.9 %collective-permute-start.17 = (bf16[576,512]{1,0:T(8,128)(2,1)}, bf16[576,512]{1,0:T(8,128)(2,1)}, u32[]{:S(2)}, u32[]{:S(2)}) collective-permute-start(bf16[576,512]{1,0:T(8,128)(2,1)} %get-tuple-element.316), channel_id=1, source_target_pairs={{0,8},{1,9},{2,4},{3,5},{4,2},{5,3},{6,14},{7,15},{8,0},{9,1},{10,... | collective-permute-start | bytes 1769480 | tf_op jit(solution)/shard_map/ppermute | solution.py:351
  121.8 20.7 %collective-permute-start.21 = (bf16[768,512]{1,0:T(8,128)(2,1)}, bf16[768,512]{1,0:T(8,128)(2,1)S(1)}, u32[]{:S(2)}, u32[]{:S(2)}) collective-permute-start(bf16[768,512]{1,0:T(8,128)(2,1)} %side_step.37), channel_id=1, source_target_pairs={{0,1},{1,0},{2,3},{3,2},{4,5},{5,4},{6,7},{7,6},{8,9},{9,8},{10,11... | collective-permute-start | bytes 2359304 | tf_op jit(solution)/shard_map/ppermute | solution.py:339
  133.5 25.8 %collective-permute-start.24 = (bf16[768,512]{1,0:T(8,128)(2,1)}, bf16[768,512]{1,0:T(8,128)(2,1)S(1)}, u32[]{:S(2)}, u32[]{:S(2)}) collective-permute-start(bf16[768,512]{1,0:T(8,128)(2,1)} %side_step.38), channel_id=1, source_target_pairs={{0,1},{1,0},{2,3},{3,2},{4,5},{5,4},{6,7},{7,6},{8,9},{9,8},{10,11... | collective-permute-start | bytes 2359304 | tf_op jit(solution)/shard_map/ppermute | solution.py:339
  135.5 19.7 %collective-permute-start.25 = (bf16[576,512]{1,0:T(8,128)(2,1)}, bf16[576,512]{1,0:T(8,128)(2,1)}, u32[]{:S(2)}, u32[]{:S(2)}) collective-permute-start(bf16[576,512]{1,0:T(8,128)(2,1)} %get-tuple-element.337), channel_id=1, source_target_pairs={{0,2},{1,3},{2,0},{3,1},{4,6},{5,7},{6,4},{7,5},{8,10},{9,11},{10,... | collective-permute-start | bytes 1769480 | tf_op jit(solution)/shard_map/ppermute | solution.py:351
  152.4 24.3 %collective-permute-start.27 = (bf16[768,512]{1,0:T(8,128)(2,1)}, bf16[768,512]{1,0:T(8,128)(2,1)S(1)}, u32[]{:S(2)}, u32[]{:S(2)}) collective-permute-start(bf16[768,512]{1,0:T(8,128)(2,1)} %side_step.39), channel_id=1, source_target_pairs={{0,1},{1,0},{2,3},{3,2},{4,5},{5,4},{6,7},{7,6},{8,9},{9,8},{10,11... | collective-permute-start | bytes 2359304 | tf_op jit(solution)/shard_map/ppermute | solution.py:339
  154.1 24.1 %collective-permute-start.28 = (bf16[576,768]{1,0:T(8,128)(2,1)}, bf16[576,768]{1,0:T(8,128)(2,1)}, u32[]{:S(2)}, u32[]{:S(2)}) collective-permute-start(bf16[576,768]{1,0:T(8,128)(2,1)} %get-tuple-element.347), channel_id=1, source_target_pairs={{0,2},{1,3},{2,0},{3,1},{4,6},{5,7},{6,4},{7,5},{8,10},{9,11},{10,... | collective-permute-start | bytes 2654216 | tf_op jit(solution)/shard_map/ppermute | solution.py:351
  155.2 23.0 %collective-permute-start.29 = (bf16[576,768]{1,0:T(8,128)(2,1)}, bf16[576,768]{1,0:T(8,128)(2,1)}, u32[]{:S(2)}, u32[]{:S(2)}) collective-permute-start(bf16[576,768]{1,0:T(8,128)(2,1)} %get-tuple-element.348), channel_id=1, source_target_pairs={{0,8},{1,9},{2,4},{3,5},{4,2},{5,3},{6,14},{7,15},{8,0},{9,1},{10,... | collective-permute-start | bytes 2654216 | tf_op jit(solution)/shard_map/ppermute | solution.py:351
  174.8 19.6 %collective-permute-start.30 = (bf16[768,512]{1,0:T(8,128)(2,1)}, bf16[768,512]{1,0:T(8,128)(2,1)}, u32[]{:S(2)}, u32[]{:S(2)}) collective-permute-start(bf16[768,512]{1,0:T(8,128)(2,1)} %get-tuple-element.354), channel_id=1, source_target_pairs={{0,1},{1,0},{2,3},{3,2},{4,5},{5,4},{6,7},{7,6},{8,9},{9,8},{10,11... | collective-permute-start | bytes 2359304 | tf_op jit(solution)/shard_map/ppermute | solution.py:339
  176.7 22.9 %collective-permute-start.31 = (bf16[576,768]{1,0:T(8,128)(2,1)}, bf16[576,768]{1,0:T(8,128)(2,1)}, u32[]{:S(2)}, u32[]{:S(2)}) collective-permute-start(bf16[576,768]{1,0:T(8,128)(2,1)} %get-tuple-element.355), channel_id=1, source_target_pairs={{0,2},{1,3},{2,0},{3,1},{4,6},{5,7},{6,4},{7,5},{8,10},{9,11},{10,... | collective-permute-start | bytes 2654216 | tf_op jit(solution)/shard_map/ppermute | solution.py:351
  176.7 22.9 %collective-permute-start.32 = (bf16[576,768]{1,0:T(8,128)(2,1)}, bf16[576,768]{1,0:T(8,128)(2,1)}, u32[]{:S(2)}, u32[]{:S(2)}) collective-permute-start(bf16[576,768]{1,0:T(8,128)(2,1)} %get-tuple-element.356), channel_id=1, source_target_pairs={{0,8},{1,9},{2,4},{3,5},{4,2},{5,3},{6,14},{7,15},{8,0},{9,1},{10,... | collective-permute-start | bytes 2654216 | tf_op jit(solution)/shard_map/ppermute | solution.py:351
  187.2 26.8 %collective-permute-start.33 = (bf16[768,512]{1,0:T(8,128)(2,1)}, bf16[768,512]{1,0:T(8,128)(2,1)S(1)}, u32[]{:S(2)}, u32[]{:S(2)}) collective-permute-start(bf16[768,512]{1,0:T(8,128)(2,1)} %side_step.41), channel_id=1, source_target_pairs={{0,1},{1,0},{2,3},{3,2},{4,5},{5,4},{6,7},{7,6},{8,9},{9,8},{10,11... | collective-permute-start | bytes 2359304 | tf_op jit(solution)/shard_map/ppermute | solution.py:339
  188.1 28.2 %collective-permute-start.34 = (bf16[576,768]{1,0:T(8,128)(2,1)}, bf16[576,768]{1,0:T(8,128)(2,1)}, u32[]{:S(2)}, u32[]{:S(2)}) collective-permute-start(bf16[576,768]{1,0:T(8,128)(2,1)} %get-tuple-element.366), channel_id=1, source_target_pairs={{0,2},{1,3},{2,0},{3,1},{4,6},{5,7},{6,4},{7,5},{8,10},{9,11},{10,... | collective-permute-start | bytes 2654216 | tf_op jit(solution)/shard_map/ppermute | solution.py:351
  194.4 21.9 %collective-permute-start.35 = (bf16[576,768]{1,0:T(8,128)(2,1)}, bf16[576,768]{1,0:T(8,128)(2,1)}, u32[]{:S(2)}, u32[]{:S(2)}) collective-permute-start(bf16[576,768]{1,0:T(8,128)(2,1)} %get-tuple-element.367), channel_id=1, source_target_pairs={{0,8},{1,9},{2,4},{3,5},{4,2},{5,3},{6,14},{7,15},{8,0},{9,1},{10,... | collective-permute-start | bytes 2654216 | tf_op jit(solution)/shard_map/ppermute | solution.py:351
  211.6 19.1 %collective-permute-start.36 = (bf16[768,512]{1,0:T(8,128)(2,1)}, bf16[768,512]{1,0:T(8,128)(2,1)}, u32[]{:S(2)}, u32[]{:S(2)}) collective-permute-start(bf16[768,512]{1,0:T(8,128)(2,1)} %get-tuple-element.373), channel_id=1, source_target_pairs={{0,1},{1,0},{2,3},{3,2},{4,5},{5,4},{6,7},{7,6},{8,9},{9,8},{10,11... | collective-permute-start | bytes 2359304 | tf_op jit(solution)/shard_map/ppermute | solution.py:339
  212.0 23.3 %collective-permute-start.37 = (bf16[576,768]{1,0:T(8,128)(2,1)}, bf16[576,768]{1,0:T(8,128)(2,1)}, u32[]{:S(2)}, u32[]{:S(2)}) collective-permute-start(bf16[576,768]{1,0:T(8,128)(2,1)} %get-tuple-element.374), channel_id=1, source_target_pairs={{0,2},{1,3},{2,0},{3,1},{4,6},{5,7},{6,4},{7,5},{8,10},{9,11},{10,... | collective-permute-start | bytes 2654216 | tf_op jit(solution)/shard_map/ppermute | solution.py:351
  213.9 21.4 %collective-permute-start.38 = (bf16[576,768]{1,0:T(8,128)(2,1)}, bf16[576,768]{1,0:T(8,128)(2,1)}, u32[]{:S(2)}, u32[]{:S(2)}) collective-permute-start(bf16[576,768]{1,0:T(8,128)(2,1)} %get-tuple-element.375), channel_id=1, source_target_pairs={{0,8},{1,9},{2,4},{3,5},{4,2},{5,3},{6,14},{7,15},{8,0},{9,1},{10,... | collective-permute-start | bytes 2654216 | tf_op jit(solution)/shard_map/ppermute | solution.py:351
  225.2 27.2 %collective-permute-start.39 = (bf16[768,512]{1,0:T(8,128)(2,1)}, bf16[768,512]{1,0:T(8,128)(2,1)S(1)}, u32[]{:S(2)}, u32[]{:S(2)}) collective-permute-start(bf16[768,512]{1,0:T(8,128)(2,1)} %side_step.43), channel_id=1, source_target_pairs={{0,1},{1,0},{2,3},{3,2},{4,5},{5,4},{6,7},{7,6},{8,9},{9,8},{10,11... | collective-permute-start | bytes 2359304 | tf_op jit(solution)/shard_map/ppermute | solution.py:339
  225.6 28.6 %collective-permute-start.40 = (bf16[576,768]{1,0:T(8,128)(2,1)}, bf16[576,768]{1,0:T(8,128)(2,1)}, u32[]{:S(2)}, u32[]{:S(2)}) collective-permute-start(bf16[576,768]{1,0:T(8,128)(2,1)} %get-tuple-element.385), channel_id=1, source_target_pairs={{0,2},{1,3},{2,0},{3,1},{4,6},{5,7},{6,4},{7,5},{8,10},{9,11},{10,... | collective-permute-start | bytes 2654216 | tf_op jit(solution)/shard_map/ppermute | solution.py:351
  230.7 23.6 %collective-permute-start.41 = (bf16[576,768]{1,0:T(8,128)(2,1)}, bf16[576,768]{1,0:T(8,128)(2,1)}, u32[]{:S(2)}, u32[]{:S(2)}) collective-permute-start(bf16[576,768]{1,0:T(8,128)(2,1)} %get-tuple-element.386), channel_id=1, source_target_pairs={{0,8},{1,9},{2,4},{3,5},{4,2},{5,3},{6,14},{7,15},{8,0},{9,1},{10,... | collective-permute-start | bytes 2654216 | tf_op jit(solution)/shard_map/ppermute | solution.py:351
  247.3 18.8 %collective-permute-start.42 = (bf16[768,512]{1,0:T(8,128)(2,1)}, bf16[768,512]{1,0:T(8,128)(2,1)S(1)}, u32[]{:S(2)}, u32[]{:S(2)}) collective-permute-start(bf16[768,512]{1,0:T(8,128)(2,1)} %get-tuple-element.392), channel_id=1, source_target_pairs={{0,1},{1,0},{2,3},{3,2},{4,5},{5,4},{6,7},{7,6},{8,9},{9,8},{10,11... | collective-permute-start | bytes 2359304 | tf_op jit(solution)/shard_map/ppermute | solution.py:339
  248.6 24.6 %collective-permute-start.43 = (bf16[576,768]{1,0:T(8,128)(2,1)}, bf16[576,768]{1,0:T(8,128)(2,1)}, u32[]{:S(2)}, u32[]{:S(2)}) collective-permute-start(bf16[576,768]{1,0:T(8,128)(2,1)} %get-tuple-element.393), channel_id=1, source_target_pairs={{0,2},{1,3},{2,0},{3,1},{4,6},{5,7},{6,4},{7,5},{8,10},{9,11},{10,... | collective-permute-start | bytes 2654216 | tf_op jit(solution)/shard_map/ppermute | solution.py:351
  252.4 20.8 %collective-permute-start.44 = (bf16[576,768]{1,0:T(8,128)(2,1)}, bf16[576,768]{1,0:T(8,128)(2,1)}, u32[]{:S(2)}, u32[]{:S(2)}) collective-permute-start(bf16[576,768]{1,0:T(8,128)(2,1)} %get-tuple-element.394), channel_id=1, source_target_pairs={{0,8},{1,9},{2,4},{3,5},{4,2},{5,3},{6,14},{7,15},{8,0},{9,1},{10,... | collective-permute-start | bytes 2654216 | tf_op jit(solution)/shard_map/ppermute | solution.py:351
  263.2 26.4 %collective-permute-start.45 = (bf16[768,512]{1,0:T(8,128)(2,1)}, bf16[768,512]{1,0:T(8,128)(2,1)S(1)}, u32[]{:S(2)}, u32[]{:S(2)}) collective-permute-start(bf16[768,512]{1,0:T(8,128)(2,1)} %side_step.45), channel_id=1, source_target_pairs={{0,1},{1,0},{2,3},{3,2},{4,5},{5,4},{6,7},{7,6},{8,9},{9,8},{10,11... | collective-permute-start | bytes 2359304 | tf_op jit(solution)/shard_map/ppermute | solution.py:339
  264.4 27.8 %collective-permute-start.46 = (bf16[576,768]{1,0:T(8,128)(2,1)}, bf16[576,768]{1,0:T(8,128)(2,1)}, u32[]{:S(2)}, u32[]{:S(2)}) collective-permute-start(bf16[576,768]{1,0:T(8,128)(2,1)} %get-tuple-element.404), channel_id=1, source_target_pairs={{0,2},{1,3},{2,0},{3,1},{4,6},{5,7},{6,4},{7,5},{8,10},{9,11},{10,... | collective-permute-start | bytes 2654216 | tf_op jit(solution)/shard_map/ppermute | solution.py:351
  266.0 26.1 %collective-permute-start.47 = (bf16[576,768]{1,0:T(8,128)(2,1)}, bf16[576,768]{1,0:T(8,128)(2,1)}, u32[]{:S(2)}, u32[]{:S(2)}) collective-permute-start(bf16[576,768]{1,0:T(8,128)(2,1)} %get-tuple-element.405), channel_id=1, source_target_pairs={{0,8},{1,9},{2,4},{3,5},{4,2},{5,3},{6,14},{7,15},{8,0},{9,1},{10,... | collective-permute-start | bytes 2654216 | tf_op jit(solution)/shard_map/ppermute | solution.py:351
  286.9 18.3 %collective-permute-start.48 = (bf16[768,512]{1,0:T(8,128)(2,1)}, bf16[768,512]{1,0:T(8,128)(2,1)S(1)}, u32[]{:S(2)}, u32[]{:S(2)}) collective-permute-start(bf16[768,512]{1,0:T(8,128)(2,1)} %get-tuple-element.411), channel_id=1, source_target_pairs={{0,1},{1,0},{2,3},{3,2},{4,5},{5,4},{6,7},{7,6},{8,9},{9,8},{10,11... | collective-permute-start | bytes 2359304 | tf_op jit(solution)/shard_map/ppermute | solution.py:339
  288.0 23.1 %collective-permute-start.49 = (bf16[576,768]{1,0:T(8,128)(2,1)}, bf16[576,768]{1,0:T(8,128)(2,1)}, u32[]{:S(2)}, u32[]{:S(2)}) collective-permute-start(bf16[576,768]{1,0:T(8,128)(2,1)} %get-tuple-element.412), channel_id=1, source_target_pairs={{0,2},{1,3},{2,0},{3,1},{4,6},{5,7},{6,4},{7,5},{8,10},{9,11},{10,... | collective-permute-start | bytes 2654216 | tf_op jit(solution)/shard_map/ppermute | solution.py:351
  289.6 21.5 %collective-permute-start.50 = (bf16[576,768]{1,0:T(8,128)(2,1)}, bf16[576,768]{1,0:T(8,128)(2,1)}, u32[]{:S(2)}, u32[]{:S(2)}) collective-permute-start(bf16[576,768]{1,0:T(8,128)(2,1)} %get-tuple-element.413), channel_id=1, source_target_pairs={{0,8},{1,9},{2,4},{3,5},{4,2},{5,3},{6,14},{7,15},{8,0},{9,1},{10,... | collective-permute-start | bytes 2654216 | tf_op jit(solution)/shard_map/ppermute | solution.py:351
  301.1 26.7 %collective-permute-start.51 = (bf16[768,512]{1,0:T(8,128)(2,1)}, bf16[768,512]{1,0:T(8,128)(2,1)S(1)}, u32[]{:S(2)}, u32[]{:S(2)}) collective-permute-start(bf16[768,512]{1,0:T(8,128)(2,1)} %side_step.47), channel_id=1, source_target_pairs={{0,1},{1,0},{2,3},{3,2},{4,5},{5,4},{6,7},{7,6},{8,9},{9,8},{10,11... | collective-permute-start | bytes 2359304 | tf_op jit(solution)/shard_map/ppermute | solution.py:339
  302.2 27.9 %collective-permute-start.52 = (bf16[576,768]{1,0:T(8,128)(2,1)}, bf16[576,768]{1,0:T(8,128)(2,1)}, u32[]{:S(2)}, u32[]{:S(2)}) collective-permute-start(bf16[576,768]{1,0:T(8,128)(2,1)} %get-tuple-element.423), channel_id=1, source_target_pairs={{0,2},{1,3},{2,0},{3,1},{4,6},{5,7},{6,4},{7,5},{8,10},{9,11},{10,... | collective-permute-start | bytes 2654216 | tf_op jit(solution)/shard_map/ppermute | solution.py:351
  305.3 24.8 %collective-permute-start.53 = (bf16[576,768]{1,0:T(8,128)(2,1)}, bf16[576,768]{1,0:T(8,128)(2,1)}, u32[]{:S(2)}, u32[]{:S(2)}) collective-permute-start(bf16[576,768]{1,0:T(8,128)(2,1)} %get-tuple-element.424), channel_id=1, source_target_pairs={{0,8},{1,9},{2,4},{3,5},{4,2},{5,3},{6,14},{7,15},{8,0},{9,1},{10,... | collective-permute-start | bytes 2654216 | tf_op jit(solution)/shard_map/ppermute | solution.py:351
  326.1 23.0 %collective-permute-start.55 = (bf16[576,768]{1,0:T(8,128)(2,1)}, bf16[576,768]{1,0:T(8,128)(2,1)}, u32[]{:S(2)}, u32[]{:S(2)}) collective-permute-start(bf16[576,768]{1,0:T(8,128)(2,1)} %get-tuple-element.431), channel_id=1, source_target_pairs={{0,2},{1,3},{2,0},{3,1},{4,6},{5,7},{6,4},{7,5},{8,10},{9,11},{10,... | collective-permute-start | bytes 2654216 | tf_op jit(solution)/shard_map/ppermute | solution.py:351
  327.8 21.3 %collective-permute-start.56 = (bf16[576,768]{1,0:T(8,128)(2,1)}, bf16[576,768]{1,0:T(8,128)(2,1)}, u32[]{:S(2)}, u32[]{:S(2)}) collective-permute-start(bf16[576,768]{1,0:T(8,128)(2,1)} %get-tuple-element.432), channel_id=1, source_target_pairs={{0,8},{1,9},{2,4},{3,5},{4,2},{5,3},{6,14},{7,15},{8,0},{9,1},{10,... | collective-permute-start | bytes 2654216 | tf_op jit(solution)/shard_map/ppermute | solution.py:351
  339.0 26.7 %collective-permute-start.57 = (bf16[768,512]{1,0:T(8,128)(2,1)}, bf16[768,512]{1,0:T(8,128)(2,1)S(1)}, u32[]{:S(2)}, u32[]{:S(2)}) collective-permute-start(bf16[768,512]{1,0:T(8,128)(2,1)} %side_step.49), channel_id=1, source_target_pairs={{0,1},{1,0},{2,3},{3,2},{4,5},{5,4},{6,7},{7,6},{8,9},{9,8},{10,11... | collective-permute-start | bytes 2359304 | tf_op jit(solution)/shard_map/ppermute | solution.py:339
  340.2 27.8 %collective-permute-start.58 = (bf16[576,768]{1,0:T(8,128)(2,1)}, bf16[576,768]{1,0:T(8,128)(2,1)}, u32[]{:S(2)}, u32[]{:S(2)}) collective-permute-start(bf16[576,768]{1,0:T(8,128)(2,1)} %get-tuple-element.442), channel_id=1, source_target_pairs={{0,2},{1,3},{2,0},{3,1},{4,6},{5,7},{6,4},{7,5},{8,10},{9,11},{10,... | collective-permute-start | bytes 2654216 | tf_op jit(solution)/shard_map/ppermute | solution.py:351
  342.7 25.3 %collective-permute-start.59 = (bf16[576,768]{1,0:T(8,128)(2,1)}, bf16[576,768]{1,0:T(8,128)(2,1)}, u32[]{:S(2)}, u32[]{:S(2)}) collective-permute-start(bf16[576,768]{1,0:T(8,128)(2,1)} %get-tuple-element.443), channel_id=1, source_target_pairs={{0,8},{1,9},{2,4},{3,5},{4,2},{5,3},{6,14},{7,15},{8,0},{9,1},{10,... | collective-permute-start | bytes 2654216 | tf_op jit(solution)/shard_map/ppermute | solution.py:351
  363.8 23.1 %collective-permute-start.61 = (bf16[576,768]{1,0:T(8,128)(2,1)}, bf16[576,768]{1,0:T(8,128)(2,1)}, u32[]{:S(2)}, u32[]{:S(2)}) collective-permute-start(bf16[576,768]{1,0:T(8,128)(2,1)} %get-tuple-element.450), channel_id=1, source_target_pairs={{0,2},{1,3},{2,0},{3,1},{4,6},{5,7},{6,4},{7,5},{8,10},{9,11},{10,... | collective-permute-start | bytes 2654216 | tf_op jit(solution)/shard_map/ppermute | solution.py:351
  365.7 21.3 %collective-permute-start.62 = (bf16[576,768]{1,0:T(8,128)(2,1)}, bf16[576,768]{1,0:T(8,128)(2,1)}, u32[]{:S(2)}, u32[]{:S(2)}) collective-permute-start(bf16[576,768]{1,0:T(8,128)(2,1)} %get-tuple-element.451), channel_id=1, source_target_pairs={{0,8},{1,9},{2,4},{3,5},{4,2},{5,3},{6,14},{7,15},{8,0},{9,1},{10,... | collective-permute-start | bytes 2654216 | tf_op jit(solution)/shard_map/ppermute | solution.py:351
  377.0 25.9 %collective-permute-start.63 = (bf16[768,512]{1,0:T(8,128)(2,1)}, bf16[768,512]{1,0:T(8,128)(2,1)S(1)}, u32[]{:S(2)}, u32[]{:S(2)}) collective-permute-start(bf16[768,512]{1,0:T(8,128)(2,1)} %side_step.51), channel_id=1, source_target_pairs={{0,1},{1,0},{2,3},{3,2},{4,5},{5,4},{6,7},{7,6},{8,9},{9,8},{10,11... | collective-permute-start | bytes 2359304 | tf_op jit(solution)/shard_map/ppermute | solution.py:339
  378.1 27.8 %collective-permute-start.64 = (bf16[576,768]{1,0:T(8,128)(2,1)}, bf16[576,768]{1,0:T(8,128)(2,1)}, u32[]{:S(2)}, u32[]{:S(2)}) collective-permute-start(bf16[576,768]{1,0:T(8,128)(2,1)} %get-tuple-element.461), channel_id=1, source_target_pairs={{0,2},{1,3},{2,0},{3,1},{4,6},{5,7},{6,4},{7,5},{8,10},{9,11},{10,... | collective-permute-start | bytes 2654216 | tf_op jit(solution)/shard_map/ppermute | solution.py:351
  380.8 25.1 %collective-permute-start.65 = (bf16[576,768]{1,0:T(8,128)(2,1)}, bf16[576,768]{1,0:T(8,128)(2,1)}, u32[]{:S(2)}, u32[]{:S(2)}) collective-permute-start(bf16[576,768]{1,0:T(8,128)(2,1)} %get-tuple-element.462), channel_id=1, source_target_pairs={{0,8},{1,9},{2,4},{3,5},{4,2},{5,3},{6,14},{7,15},{8,0},{9,1},{10,... | collective-permute-start | bytes 2654216 | tf_op jit(solution)/shard_map/ppermute | solution.py:351
  393.2 31.7 %collective-permute-start.67 = (bf16[576,768]{1,0:T(8,128)(2,1)}, bf16[576,768]{1,0:T(8,128)(2,1)}, u32[]{:S(2)}, u32[]{:S(2)}) collective-permute-start(bf16[576,768]{1,0:T(8,128)(2,1)} %get-tuple-element.469), channel_id=1, source_target_pairs={{0,2},{1,3},{2,0},{3,1},{4,6},{5,7},{6,4},{7,5},{8,10},{9,11},{10,... | collective-permute-start | bytes 2654216 | tf_op jit(solution)/shard_map/ppermute | solution.py:351
  395.4 29.5 %collective-permute-start.68 = (bf16[576,768]{1,0:T(8,128)(2,1)}, bf16[576,768]{1,0:T(8,128)(2,1)}, u32[]{:S(2)}, u32[]{:S(2)}) collective-permute-start(bf16[576,768]{1,0:T(8,128)(2,1)} %get-tuple-element.470), channel_id=1, source_target_pairs={{0,8},{1,9},{2,4},{3,5},{4,2},{5,3},{6,14},{7,15},{8,0},{9,1},{10,... | collective-permute-start | bytes 2654216 | tf_op jit(solution)/shard_map/ppermute | solution.py:351
  402.9 20.2 %collective-permute-start.66 = (bf16[768,512]{1,0:T(8,128)(2,1)}, bf16[768,512]{1,0:T(8,128)(2,1)S(1)}, u32[]{:S(2)}, u32[]{:S(2)}) collective-permute-start(bf16[768,512]{1,0:T(8,128)(2,1)} %get-tuple-element.468), channel_id=1, source_target_pairs={{0,1},{1,0},{2,3},{3,2},{4,5},{5,4},{6,7},{7,6},{8,9},{9,8},{10,11... | collective-permute-start | bytes 2359304 | tf_op jit(solution)/shard_map/ppermute | solution.py:339
  412.1 31.7 %collective-permute-start.69 = (bf16[576,768]{1,0:T(8,128)(2,1)}, bf16[576,768]{1,0:T(8,128)(2,1)}, u32[]{:S(2)}, u32[]{:S(2)}) collective-permute-start(bf16[576,768]{1,0:T(8,128)(2,1)} %get-tuple-element.479), channel_id=1, source_target_pairs={{0,2},{1,3},{2,0},{3,1},{4,6},{5,7},{6,4},{7,5},{8,10},{9,11},{10,... | collective-permute-start | bytes 2654216 | tf_op jit(solution)/shard_map/ppermute | solution.py:351
  414.4 29.5 %collective-permute-start.70 = (bf16[576,768]{1,0:T(8,128)(2,1)}, bf16[576,768]{1,0:T(8,128)(2,1)}, u32[]{:S(2)}, u32[]{:S(2)}) collective-permute-start(bf16[576,768]{1,0:T(8,128)(2,1)} %get-tuple-element.480), channel_id=1, source_target_pairs={{0,8},{1,9},{2,4},{3,5},{4,2},{5,3},{6,14},{7,15},{8,0},{9,1},{10,... | collective-permute-start | bytes 2654216 | tf_op jit(solution)/shard_map/ppermute | solution.py:351
  431.1 31.6 %collective-permute-start.71 = (bf16[576,768]{1,0:T(8,128)(2,1)}, bf16[576,768]{1,0:T(8,128)(2,1)S(1)}, u32[]{:S(2)}, u32[]{:S(2)}) collective-permute-start(bf16[576,768]{1,0:T(8,128)(2,1)} %get-tuple-element.486), channel_id=1, source_target_pairs={{0,2},{1,3},{2,0},{3,1},{4,6},{5,7},{6,4},{7,5},{8,10},{9,11},{10,... | collective-permute-start | bytes 2654216 | tf_op jit(solution)/shard_map/ppermute | solution.py:351
  433.3 29.4 %collective-permute-start.72 = (bf16[576,768]{1,0:T(8,128)(2,1)}, bf16[576,768]{1,0:T(8,128)(2,1)}, u32[]{:S(2)}, u32[]{:S(2)}) collective-permute-start(bf16[576,768]{1,0:T(8,128)(2,1)} %get-tuple-element.487), channel_id=1, source_target_pairs={{0,8},{1,9},{2,4},{3,5},{4,2},{5,3},{6,14},{7,15},{8,0},{9,1},{10,... | collective-permute-start | bytes 2654216 | tf_op jit(solution)/shard_map/ppermute | solution.py:351
  450.1 38.3 %collective-permute-start.75 = (bf16[576,768]{1,0:T(8,128)(2,1)}, bf16[576,768]{1,0:T(8,128)(2,1)}, u32[]{:S(2)}, u32[]{:S(2)}) collective-permute-start(bf16[576,768]{1,0:T(8,128)(2,1)} %get-tuple-element.498), channel_id=1, source_target_pairs={{0,2},{1,3},{2,0},{3,1},{4,6},{5,7},{6,4},{7,5},{8,10},{9,11},{10,... | collective-permute-start | bytes 2654216 | tf_op jit(solution)/shard_map/ppermute | solution.py:351
  452.3 36.1 %collective-permute-start.76 = (bf16[576,768]{1,0:T(8,128)(2,1)}, bf16[576,768]{1,0:T(8,128)(2,1)}, u32[]{:S(2)}, u32[]{:S(2)}) collective-permute-start(bf16[576,768]{1,0:T(8,128)(2,1)} %get-tuple-element.499), channel_id=1, source_target_pairs={{0,8},{1,9},{2,4},{3,5},{4,2},{5,3},{6,14},{7,15},{8,0},{9,1},{10,... | collective-permute-start | bytes 2654216 | tf_op jit(solution)/shard_map/ppermute | solution.py:351
  469.9 30.8 %collective-permute-start.78 = (bf16[576,768]{1,0:T(8,128)(2,1)}, bf16[576,768]{1,0:T(8,128)(2,1)}, u32[]{:S(2)}, u32[]{:S(2)}) collective-permute-start(bf16[576,768]{1,0:T(8,128)(2,1)} %get-tuple-element.508), channel_id=1, source_target_pairs={{0,2},{1,3},{2,0},{3,1},{4,6},{5,7},{6,4},{7,5},{8,10},{9,11},{10,... | collective-permute-start | bytes 2654216 | tf_op jit(solution)/shard_map/ppermute | solution.py:351
  471.6 29.2 %collective-permute-start.79 = (bf16[576,768]{1,0:T(8,128)(2,1)}, bf16[576,768]{1,0:T(8,128)(2,1)}, u32[]{:S(2)}, u32[]{:S(2)}) collective-permute-start(bf16[576,768]{1,0:T(8,128)(2,1)} %get-tuple-element.509), channel_id=1, source_target_pairs={{0,8},{1,9},{2,4},{3,5},{4,2},{5,3},{6,14},{7,15},{8,0},{9,1},{10,... | collective-permute-start | bytes 2654216 | tf_op jit(solution)/shard_map/ppermute | solution.py:351
  494.7 31.8 %collective-permute-start.82 = (bf16[576,768]{1,0:T(8,128)(2,1)}, bf16[576,768]{1,0:T(8,128)(2,1)}, u32[]{:S(2)}, u32[]{:S(2)}) collective-permute-start(bf16[576,768]{1,0:T(8,128)(2,1)} %get-tuple-element.520), channel_id=1, source_target_pairs={{0,2},{1,3},{2,0},{3,1},{4,6},{5,7},{6,4},{7,5},{8,10},{9,11},{10,... | collective-permute-start | bytes 2654216 | tf_op jit(solution)/shard_map/ppermute | solution.py:351
  494.8 31.7 %collective-permute-start.83 = (bf16[576,768]{1,0:T(8,128)(2,1)}, bf16[576,768]{1,0:T(8,128)(2,1)}, u32[]{:S(2)}, u32[]{:S(2)}) collective-permute-start(bf16[576,768]{1,0:T(8,128)(2,1)} %get-tuple-element.521), channel_id=1, source_target_pairs={{0,8},{1,9},{2,4},{3,5},{4,2},{5,3},{6,14},{7,15},{8,0},{9,1},{10,... | collective-permute-start | bytes 2654216 | tf_op jit(solution)/shard_map/ppermute | solution.py:351
  507.0 31.7 %collective-permute-start.86 = (bf16[576,768]{1,0:T(8,128)(2,1)}, bf16[576,768]{1,0:T(8,128)(2,1)}, u32[]{:S(2)}, u32[]{:S(2)}) collective-permute-start(bf16[576,768]{1,0:T(8,128)(2,1)} %get-tuple-element.524), channel_id=1, source_target_pairs={{0,2},{1,3},{2,0},{3,1},{4,6},{5,7},{6,4},{7,5},{8,10},{9,11},{10,... | collective-permute-start | bytes 2654216 | tf_op jit(solution)/shard_map/ppermute | solution.py:351
  509.7 28.9 %collective-permute-start.87 = (bf16[576,768]{1,0:T(8,128)(2,1)}, bf16[576,768]{1,0:T(8,128)(2,1)}, u32[]{:S(2)}, u32[]{:S(2)}) collective-permute-start(bf16[576,768]{1,0:T(8,128)(2,1)} %get-tuple-element.525), channel_id=1, source_target_pairs={{0,8},{1,9},{2,4},{3,5},{4,2},{5,3},{6,14},{7,15},{8,0},{9,1},{10,... | collective-permute-start | bytes 2654216 | tf_op jit(solution)/shard_map/ppermute | solution.py:351
  562.8 18.9 %collective-permute-start.96 = (bf16[576,256]{1,0:T(8,128)(2,1)}, bf16[576,256]{1,0:T(8,128)(2,1)S(1)}, u32[]{:S(2)}, u32[]{:S(2)}) collective-permute-start(bf16[576,256]{1,0:T(8,128)(2,1)} %collective-permute-done.93.refs_7_), channel_id=1, source_target_pairs={{0,2},{1,3},{2,0},{3,1},{4,6},{5,7},{6,4},{7,5},{8,10},{9,11},{10,... | collective-permute-start | bytes 884744 | tf_op jit(solution)/shard_map/ppermute | solution.py:351
  643.8 18.1 %collective-permute-start.103 = (bf16[192,512]{1,0:T(8,128)(2,1)S(1)}, bf16[192,512]{1,0:T(8,128)(2,1)S(1)}, u32[]{:S(2)}, u32[]{:S(2)}) collective-permute-start(bf16[192,512]{1,0:T(8,128)(2,1)S(1)} %get-tuple-element.573), channel_id=1, source_target_pairs={{0,1},{1,0},{2,9},{3,8},{4,17},{5,16},{6,25},{7,24},{8,3},{9,2},{1... | collective-permute-start | bytes 589832 | tf_op jit(solution)/shard_map/ppermute | solution.py:661
  644.9 20.0 %collective-permute-start.102 = (bf16[192,512]{1,0:T(8,128)(2,1)S(1)}, bf16[192,512]{1,0:T(8,128)(2,1)S(1)}, u32[]{:S(2)}, u32[]{:S(2)}) collective-permute-start(bf16[192,512]{1,0:T(8,128)(2,1)S(1)} %get-tuple-element.574), channel_id=1, source_target_pairs={{0,0},{1,1},{2,8},{3,9},{4,16},{5,17},{6,24},{7,25},{8,2},{9,3},{1... | collective-permute-start | bytes 589832 | tf_op jit(solution)/shard_map/ppermute | solution.py:661
  (87 other events, 814.0 us)
